TPU v7x, 128 devices: a whole 4x4x4 slice. The times are simulated.
128 devices in a mesh: depth: 16 (over z, x_hi, core), res: 8 (over x_lo, y).
Axes of the slice: x: 4 (x_hi: 2, x_lo: 2; x = x_hi * 2 + x_lo), y: 4, z: 4, core: 2. Of those that a mesh axis runs over, the one named last changes fastest.
Arguments:
- alignment_state: bfloat16 [256, 256, 64], P('depth', 'res'), may hold values from -8 to 8
- pairwise_state: bfloat16 [256, 256, 128], P('res', 'depth'), may hold values from -6 to 6
- alignment_mask: int32 [256, 256], P('depth', 'res'), may hold values 0 or 1
- residue_entry_mask: int32 [256], P('res'), may hold values 0 or 1
- sequence_live_count: int32 [16], P('depth'), may hold values from 5 to 16, as said below
- horizontal_intake_coefs: bfloat16 [64, 256], replicated, may hold values from -0.75 to 0.75
- pairwise_bias_weights: bfloat16 [128, 8], replicated, may hold values from -0.5 to 0.5
- horizontal_readout_coefs: bfloat16 [64, 64], replicated, may hold values from -0.75 to 0.75
- column_input_weights: bfloat16 [64, 144], replicated, may hold values from -0.75 to 0.75
- vertical_readout_coefs: bfloat16 [64, 64], replicated, may hold values from -0.75 to 0.75
- tensor_factor_coefs: bfloat16 [64, 64], replicated, may hold values from -0.75 to 0.75
- outer_output_weights: bfloat16 [1024, 128], replicated, may hold values from -0.1875 to 0.1875
- adjoint_of_result_track: bfloat16 [256, 256, 64], P('depth', 'res'), may hold values from -6 to 6
- pairwise_cotangent: bfloat16 [256, 256, 128], P('res', 'depth'), may hold values from -3 to 3
Outputs:
- alignment_gradient: float32 [256, 256, 64], P('depth', 'res')
- pair_grad: float32 [256, 256, 128], P('res', 'depth')
Inputs may be any that keep to these rules, and one draw needn't show every extreme that they name: `sequence_live_count`: the last block holds 16 live sequences.
All inputs are finite; a program needn't handle non-finite values. No bound on the sum of `alignment_mask` or of `residue_entry_mask` on one device may be relied on, other than what follows from the above.
Results may differ from a plain program's by a relative error of at most 0.0015.
Values may be sent and summed in bfloat16 or wider, within the bound.
No kernel may reach another device: no remote copies, remote signals or barrier semaphores. Data moves between devices by JAX's collectives and lax.ppermute only.
A program may use at most 448 MiB of HBM per device.

v0:
```python
import jax
import jax.numpy as jnp
from jax import lax
from jax.sharding import PartitionSpec as P

highest_precision = lax.Precision.HIGHEST


def layer_normalize(payload_lanes):
    center = payload_lanes - jnp.mean(payload_lanes, -1, keepdims=True)
    spread = jnp.mean(center * center, -1, keepdims=True)
    return center * lax.rsqrt(spread + 1e-05)


def pair_bias(pairwise_single, bias_weight):
    return jnp.einsum(
        "ijc,ch->ijh", layer_normalize(pairwise_single), bias_weight, precision=highest_precision
    )


def attend(queries, gating, key_value, bias_complete, key_entry_mask):
    sequence_row_group, row_len = (queries.shape[0], queries.shape[1])
    col_len = key_value.shape[1]
    head_number = bias_complete.shape[2]
    inner_channel_width = queries.shape[2]
    head_dim = inner_channel_width // head_number
    query_heads = queries.reshape(sequence_row_group, row_len, head_number, head_dim)
    key_rows = key_value[..., :inner_channel_width].reshape(
        sequence_row_group, col_len, head_number, head_dim
    )
    value_rows = key_value[..., inner_channel_width:].reshape(
        sequence_row_group, col_len, head_number, head_dim
    )
    logits = jnp.einsum(
        "sihd,sjhd->shij", query_heads, key_rows, precision=highest_precision
    ) * head_dim ** (-0.5)
    logits = logits + jnp.transpose(bias_complete, (2, 0, 1))[None]
    logits = jnp.where(key_entry_mask[:, None, None, :] > 0, logits, -1000000000.0)
    weights = jax.nn.softmax(logits, axis=-1)
    attended_output = jnp.einsum(
        "shij,sjhd->sihd", weights, value_rows, precision=highest_precision
    )
    return jax.nn.sigmoid(gating) * attended_output.reshape(
        sequence_row_group, row_len, inner_channel_width
    )


def project_kv(normalized_input, input_weight, inner_channel_width):
    return jnp.einsum(
        "nze,eb->nzb",
        normalized_input,
        input_weight[:, inner_channel_width : 3 * inner_channel_width],
        precision=highest_precision,
    )


def row_device_local(
    solo_aligned_track,
    key_value_entire,
    bias_entire,
    key_entry_mask,
    input_weight,
    output_weight,
    inner_channel_width,
):
    normalized_input = layer_normalize(solo_aligned_track)
    queries = jnp.einsum(
        "nze,eb->nzb",
        normalized_input,
        input_weight[:, :inner_channel_width],
        precision=highest_precision,
    )
    gating = jnp.einsum(
        "nze,eb->nzb",
        normalized_input,
        input_weight[:, 3 * inner_channel_width :],
        precision=highest_precision,
    )
    attended_output = attend(queries, gating, key_value_entire, bias_entire, key_entry_mask)
    return solo_aligned_track + jnp.einsum(
        "iwu,ux->iwx", attended_output, output_weight, precision=highest_precision
    )


def query_summation(alignment_after_rows, active_mask):
    return jnp.einsum(
        "yo,yob->ob",
        active_mask,
        layer_normalize(alignment_after_rows),
        precision=highest_precision,
    )


def column_scores(
    alignment_after_rows,
    query_grand_total,
    sequence_grand_total,
    active_mask,
    column_weight_matrix,
    inner_channel_width,
    head_number,
):
    head_dim = inner_channel_width // head_number
    normalized_input = layer_normalize(alignment_after_rows)
    query_mean = query_grand_total / jnp.maximum(sequence_grand_total, 1.0)[:, None]
    col_query = (
        jnp.dot(
            query_mean, column_weight_matrix[:, :inner_channel_width], precision=highest_precision
        )
        * head_dim ** (-0.5)
    ).reshape(-1, head_number, head_dim)
    col_proj = jnp.einsum(
        "sic,cf->sif",
        normalized_input,
        column_weight_matrix[:, inner_channel_width : inner_channel_width + 2 * head_dim],
        precision=highest_precision,
    )
    logits = jnp.einsum(
        "ihd,sid->sih", col_query, col_proj[..., :head_dim], precision=highest_precision
    )
    logits = jnp.where(active_mask[..., None] > 0, logits, -1000000000.0)
    return (logits, col_proj[..., head_dim:])


def col_sums(
    alignment_after_rows,
    query_grand_total,
    sequence_grand_total,
    peak_value,
    active_mask,
    column_weight_matrix,
    inner_channel_width,
    head_number,
):
    logits, col_value = column_scores(
        alignment_after_rows,
        query_grand_total,
        sequence_grand_total,
        active_mask,
        column_weight_matrix,
        inner_channel_width,
        head_number,
    )
    exp_logits = jnp.exp(logits - peak_value[None])
    return (
        jnp.sum(exp_logits, 0),
        jnp.einsum("sih,sid->ihd", exp_logits, col_value, precision=highest_precision),
    )


def column_attend_apply(
    alignment_after_rows,
    denominator_sum,
    numerator_sum,
    column_weight_matrix,
    column_output,
    inner_channel_width,
    head_number,
):
    head_dim = inner_channel_width // head_number
    sequence_row_group, residue_row_group = (
        alignment_after_rows.shape[0],
        alignment_after_rows.shape[1],
    )
    normalized_input = layer_normalize(alignment_after_rows)
    gating = jnp.einsum(
        "sic,cf->sif",
        normalized_input,
        column_weight_matrix[:, inner_channel_width + 2 * head_dim :],
        precision=highest_precision,
    )
    attended_output = numerator_sum / denominator_sum[..., None]
    mixed_heads = (
        jax.nn.sigmoid(gating).reshape(sequence_row_group, residue_row_group, head_number, head_dim)
        * attended_output[None]
    ).reshape(sequence_row_group, residue_row_group, inner_channel_width)
    return alignment_after_rows + jnp.einsum(
        "dvn,na->dva", mixed_heads, column_output, precision=highest_precision
    )


def outer_product_inputs(
    alignment_after_columns, active_mask, outer_weight_matrix, outer_product_width
):
    projected_input = jnp.einsum(
        "nze,eb->nzb",
        layer_normalize(alignment_after_columns),
        outer_weight_matrix,
        precision=highest_precision,
    )
    return (
        active_mask[..., None] * projected_input[..., :outer_product_width],
        active_mask[..., None] * projected_input[..., outer_product_width:],
    )


def body(
    alignment_state,
    pairwise_state,
    alignment_mask,
    residue_entry_mask,
    sequence_live_count,
    horizontal_intake_coefs,
    pairwise_bias_weights,
    horizontal_readout_coefs,
    column_input_weights,
    vertical_readout_coefs,
    tensor_factor_coefs,
    outer_output_weights,
    adjoint_of_result_track,
    pairwise_cotangent,
):
    sequence_row_group, residue_row_group = (alignment_state.shape[0], alignment_state.shape[1])
    head_number = pairwise_bias_weights.shape[1]
    inner_channel_width = horizontal_readout_coefs.shape[0]
    outer_product_width = tensor_factor_coefs.shape[1] // 2
    input_weight = horizontal_intake_coefs.astype(jnp.float32)
    output_weight = horizontal_readout_coefs.astype(jnp.float32)
    column_weight_matrix = column_input_weights.astype(jnp.float32)
    column_output = vertical_readout_coefs.astype(jnp.float32)
    seq_index = jnp.arange(sequence_row_group, dtype=jnp.int32)
    sequence_active = (seq_index < sequence_live_count[0]).astype(jnp.float32)
    active_mask = (
        alignment_mask.astype(jnp.float32)
        * residue_entry_mask.astype(jnp.float32)[None, :]
        * sequence_active[:, None]
    )
    solo_aligned_track = alignment_state.astype(jnp.float32)
    bias_local, pull_bias = jax.vjp(
        lambda payload_lanes: pair_bias(payload_lanes, pairwise_bias_weights.astype(jnp.float32)),
        pairwise_state.astype(jnp.float32),
    )
    flat_bias = bias_local.reshape(residue_row_group, -1)
    unused_value, backprop_normalize = jax.vjp(layer_normalize, solo_aligned_track)
    rows_whole, mask_rows = (
        lax.all_gather(alignment_state, "res", axis=1, tiled=True),
        lax.all_gather(active_mask.astype(jnp.bfloat16), "res", axis=1, tiled=True),
    )
    mask_whole = mask_rows.astype(jnp.float32)
    normed_whole = layer_normalize(rows_whole.astype(jnp.float32))
    key_value_entire, pull_kv = jax.vjp(
        lambda normalized_input: project_kv(normalized_input, input_weight, inner_channel_width),
        normed_whole,
    )
    bias_entire = lax.all_gather(flat_bias, "depth", axis=1, tiled=True).reshape(
        residue_row_group, -1, head_number
    )
    alignment_after_rows, backprop_row_attend = jax.vjp(
        lambda payload_lanes, key_value, bias_complete: row_device_local(
            payload_lanes,
            key_value,
            bias_complete,
            mask_whole,
            input_weight,
            output_weight,
            inner_channel_width,
        ),
        solo_aligned_track,
        key_value_entire,
        bias_entire,
    )
    pairwise_portion = jnp.einsum("si,sj->ij", active_mask, mask_whole, precision=highest_precision)
    seq_part = jnp.sum(active_mask, 0)
    pair_norm, sequence_grand_total = (
        lax.psum(pairwise_portion.astype(jnp.bfloat16), "depth").astype(jnp.float32),
        lax.psum(seq_part.astype(jnp.bfloat16), "depth").astype(jnp.float32),
    )
    query_portion, backprop_query = jax.vjp(
        lambda payload_lanes: query_summation(payload_lanes, active_mask), alignment_after_rows
    )
    query_grand_total = lax.psum(query_portion, "depth")
    logits, unused_value = column_scores(
        alignment_after_rows,
        query_grand_total,
        sequence_grand_total,
        active_mask,
        column_weight_matrix,
        inner_channel_width,
        head_number,
    )
    peak_value = lax.pmax(jnp.max(logits, 0), "depth")
    own_sums, pull_sums = jax.vjp(
        lambda payload_lanes, total: col_sums(
            payload_lanes,
            total,
            sequence_grand_total,
            peak_value,
            active_mask,
            column_weight_matrix,
            inner_channel_width,
            head_number,
        ),
        alignment_after_rows,
        query_grand_total,
    )
    denominator_sum, numerator_sum = lax.psum((own_sums[0], own_sums[1]), "depth")
    alignment_after_columns, backprop_apply = jax.vjp(
        lambda payload_lanes, denom, numer: column_attend_apply(
            payload_lanes,
            denom,
            numer,
            column_weight_matrix,
            column_output,
            inner_channel_width,
            head_number,
        ),
        alignment_after_rows,
        denominator_sum,
        numerator_sum,
    )
    outer_factors, pull_factors = jax.vjp(
        lambda payload_lanes: outer_product_inputs(
            payload_lanes, active_mask, tensor_factor_coefs.astype(jnp.float32), outer_product_width
        ),
        alignment_after_columns,
    )
    left_proj, right_proj = outer_factors
    right_whole = (
        lax.all_gather(
            right_proj.reshape(sequence_row_group, -1).astype(jnp.bfloat16),
            "res",
            axis=1,
            tiled=True,
        )
        .astype(jnp.float32)
        .reshape(sequence_row_group, -1, outer_product_width)
    )
    inverse = 1.0 / jnp.maximum(pair_norm, 1.0)
    block_piece = lax.all_gather(pairwise_cotangent, "depth", axis=1, tiled=True)
    left_total = jnp.zeros_like(left_proj)
    right_total = jnp.zeros_like(right_whole)
    span_len = block_piece.shape[1]
    pair_back = jnp.einsum(
        "ijk,fk->ijf", block_piece, outer_output_weights, preferred_element_type=jnp.float32
    )
    pair_back = (pair_back * inverse[..., None]).reshape(
        residue_row_group, span_len, outer_product_width, outer_product_width
    )
    left_total = left_total + jnp.einsum(
        "ijab,sjb->sia", pair_back, right_whole, precision=highest_precision
    )
    right_new = jnp.einsum("sia,ijab->sjb", left_proj, pair_back, precision=highest_precision)
    right_total = lax.dynamic_update_slice_in_dim(right_total, right_new, jnp.int32(0), 1)
    right_grad = (
        lax.psum_scatter(
            right_total.reshape(sequence_row_group, -1).astype(jnp.bfloat16),
            "res",
            scatter_dimension=1,
            tiled=True,
        )
        .astype(jnp.float32)
        .reshape(sequence_row_group, residue_row_group, outer_product_width)
    )
    (second_gradient,) = pull_factors((left_total, right_grad))
    second_gradient = second_gradient + adjoint_of_result_track.astype(jnp.float32)
    first_gradient, denom_grad, numer_grad = backprop_apply(second_gradient)
    denom_total, numer_total = lax.psum((denom_grad, numer_grad), "depth")
    sums_grad, query_grad = pull_sums((denom_total, numer_total))
    query_grad_total = lax.psum(query_grad, "depth")
    (mean_grad,) = backprop_query(query_grad_total)
    first_gradient = first_gradient + sums_grad + mean_grad
    alignment_gradient, key_value_gradient_entire, bias_gradient_complete = backprop_row_attend(
        first_gradient
    )
    (normed_grad_whole,) = pull_kv(key_value_gradient_entire)
    normalized_gradient = lax.psum_scatter(
        normed_grad_whole, "res", scatter_dimension=1, tiled=True
    )
    (key_value_sequence_gradient,) = backprop_normalize(normalized_gradient)
    alignment_gradient = alignment_gradient + key_value_sequence_gradient
    bias_grad = lax.psum_scatter(
        bias_gradient_complete.reshape(residue_row_group, -1),
        "depth",
        scatter_dimension=1,
        tiled=True,
    ).reshape(bias_local.shape)
    (pairwise_portion_gradient,) = pull_bias(bias_grad)
    return (alignment_gradient, pairwise_portion_gradient + pairwise_cotangent.astype(jnp.float32))


def solution(mesh):
    in_specs = (
        P("depth", "res", None),
        P("res", "depth", None),
        P("depth", "res"),
        P("res"),
        P("depth"),
        P(),
        P(),
        P(),
        P(),
        P(),
        P(),
        P(),
        P("depth", "res", None),
        P("res", "depth", None),
    )
    out_specs = (P("depth", "res", None), P("res", "depth", None))
    return jax.shard_map(body, mesh=mesh, in_specs=in_specs, out_specs=out_specs, check_vma=False)
```

profile of v0, /device:TPU:1, one launch (start us, length us, event | category | flops | bytes accessed | tf_op | source)
XLA Modules:
  0.0 1005.7 jit_solution(1093752049533944771)
XLA Ops:
  7.2 0.7 all-gather.3.cloned.1.call-update
  8.6 0.7 convert_element_type.64
  9.3 0.8 broadcast_compare_fusion
  10.1 23.1 %all-gather = bf16[8,32,16]{1,2,0:T(8,128)(2,1)S(1)} all-gather(bf16[1,32,16]{1,2,0:T(8,128)(2,1)S(1)} %get-tuple-element.38), channel_id=1, replica_groups=mesh['depth'=16,'res'=8] {'res'}, dimensions={0}, use_global_device_ids=true | all-gather | bytes 9216 | tf_op jit(solution)/shard_map/all_gather | solution.py:237
  33.6 1.0 convert_reduce_fusion.1
  34.6 1.2 fusion.62
  36.4 1.3 fusion.34
  37.8 1.9 convolution_bitcast_fusion.1
  39.6 26.8 %all_gather.15 = bf16[16,256,64]{2,1,0:T(8,128)(2,1)S(1)} all-gather(bf16[16,32,64]{2,1,0:T(8,128)(2,1)} %param.14), channel_id=1, replica_groups=mesh['depth'=16,'res'=8] {'res'}, dimensions={1}, use_global_device_ids=true | all-gather | bytes 589824 | tf_op jit(solution)/shard_map/all_gather | solution.py:236
  66.5 1.0 convert_reduce_fusion.2
  67.6 1.1 fusion.58
  69.9 1.1 fusion.59
  71.1 42.0 %all_gather.17 = f32[32,2048]{0,1:T(8,128)S(1)} all-gather(f32[32,128]{0,1:T(8,128)S(1)} %bitcast.208), channel_id=1, replica_groups=mesh['depth'=16,'res'=8] {'depth'}, dimensions={1}, use_global_device_ids=true | all-gather | bytes 278528 | tf_op jit(solution)/shard_map/all_gather | solution.py:245
  113.9 1.5 fusion.10
  115.4 3.8 fusion.11
  119.3 4.4 fusion.7
  123.6 1.6 fusion.167
  125.6 4.5 fusion.25
  131.2 59.9 %all-reduce.8 = (bf16[32,256]{1,0:T(8,128)(2,1)S(1)}, bf16[32]{0:T(256)(128)(2,1)S(1)}) all-reduce(bf16[32,256]{1,0:T(8,128)(2,1)S(1)} %convolution_convert_fusion, bf16[32]{0:T(256)(128)(2,1)S(1)} %get-tuple-element.37), channel_id=1, replica_groups=mesh['depth'=16,'res'=8] {'depth'}, use_global_device_ids=true, to_apply=%region_20.21 | all-reduce | flops 8224 | bytes 32896 | tf_op jit(solution)/shard_map/psum | solution.py:265
  191.8 0.7 copy.85
  192.5 64.9 %psum.56 = f32[32,64]{1,0:T(8,128)S(1)} all-reduce(f32[32,64]{1,0:T(8,128)S(1)} %bitcast.213), channel_id=1, replica_groups=mesh['depth'=16,'res'=8] {'depth'}, use_global_device_ids=true, to_apply=%region_10.11 | all-reduce | flops 2048 | bytes 16384 | tf_op jit(solution)/shard_map/psum | solution.py:271
  257.8 0.7 fusion.120
  259.3 64.9 %pmax.7 = f32[32,8]{1,0:T(8,128)S(1)} all-reduce(f32[32,8]{1,0:T(8,128)S(1)} %get-tuple-element.43), channel_id=1, replica_groups=mesh['depth'=16,'res'=8] {'depth'}, use_global_device_ids=true, to_apply=%region_14.15 | all-reduce | flops 256 | bytes 2048 | tf_op jit(solution)/shard_map/pmax | solution.py:281
  325.3 66.6 %all-reduce.7 = (f32[32,8,8]{2,1,0:T(8,128)S(1)}, f32[32,8]{1,0:T(8,128)S(1)}) all-reduce(f32[32,8,8]{2,1,0:T(8,128)S(1)} %fusion.110, f32[32,8]{1,0:T(8,128)S(1)} %fusion.109), channel_id=1, replica_groups=mesh['depth'=16,'res'=8] {'depth'}, use_global_device_ids=true, to_apply=%region_15.16 | all-reduce | flops 2304 | bytes 18432 | tf_op jit(solution)/shard_map/psum | solution.py:296
  395.5 22.0 %all_gather.19 = bf16[16,8192]{1,0:T(8,128)(2,1)S(1)} all-gather(bf16[16,1024]{1,0:T(8,128)(2,1)S(1)} %convert_element_type.77), channel_id=1, replica_groups=mesh['depth'=16,'res'=8] {'res'}, dimensions={1}, use_global_device_ids=true | all-gather | bytes 294912 | tf_op jit(solution)/shard_map/all_gather | solution.py:319
  417.5 0.8 reshape.261
  419.5 0.6 multiply_divide_fusion
  420.1 14.3 %broadcast_multiply_fusion = f32[32,256,1024]{2,1,0:T(8,128)} fusion(f32[32,256]{1,0:T(8,128)S(1)} %maximum_divide_fusion, bf16[32,256,128]{2,1,0:T(8,128)(2,1)} %all-gather.3.cloned.1.call-done, bf16[1024,128]{1,0:T(8,128)(2,1)S(1)} %copy-done), kind=kOutput, calls=%fused_computation.2 | convolution fusion | flops 2155872256 | bytes 35946496 | tf_op jit(solution)/shard_map/ijk,fk->ijf/dot_general | solution.py:333
  434.4 33.4 %copy.76 = f32[32,256,1024]{1,2,0:T(8,128)} copy(f32[32,256,1024]{2,1,0:T(8,128)} %broadcast_multiply_fusion) | data formatting | bytes 67108864 | tf_op jit(solution)/shard_map/mul | solution.py:336
  467.8 73.7 %copy.77 = f32[256,32,32,32]{1,0,3,2:T(8,128)} copy(f32[256,32,32,32]{0,1,2,3:T(8,128)} %bitcast.199) | data formatting | bytes 67108864 | tf_op jit(solution)/shard_map/sia,ijab->sjb/dot_general | solution.py:342
  541.4 93.2 %dot_general.143 = f32[8192,32,32]{0,2,1:T(8,128)} reshape(f32[256,32,32,32]{1,0,3,2:T(8,128)} %copy.77) | data formatting | bytes 67108864 | tf_op jit(solution)/shard_map/sia,ijab->sjb/dot_general | solution.py:342
  634.6 29.2 %fusion.2 = bf16[16,8192]{1,0:T(8,128)(2,1)} fusion(f32[16,32,32]{1,0,2:T(8,128)S(1)} %copy.78, f32[8192,32,32]{0,2,1:T(8,128)} %dot_general.143), kind=kOutput, calls=%fused_computation.4 | convolution fusion | flops 1610743808 | bytes 33882112 | tf_op jit(solution)/shard_map/sia,ijab->sjb/dot_general | solution.py:342
  664.0 54.1 %fusion.35 = f32[16,32,32]{2,0,1:T(8,128)S(1)} fusion(f32[32,256,32,32]{1,3,2,0:T(8,128)} %bitcast.200, bf16[16,256,32]{1,0,2:T(8,128)(2,1)S(1)} %copy.79), kind=kOutput, calls=%fused_computation.45 | convolution fusion | flops 1610612736 | bytes 33882112 | tf_op jit(solution)/shard_map/ijab,sjb->sia/dot_general | solution.py:339
  718.3 1.1 reshape.269
  721.3 73.1 %all-reduce.6 = (f32[32,8,8]{2,1,0:T(8,128)S(1)}, f32[32,8]{1,0:T(8,128)S(1)}) all-reduce(f32[32,8,8]{2,1,0:T(8,128)S(1)} %get-tuple-element.27, f32[32,8]{1,0:T(8,128)S(1)} %neg.43), channel_id=1, replica_groups=mesh['depth'=16,'res'=8] {'depth'}, use_global_device_ids=true, to_apply=%region_27.28 | all-reduce | flops 2304 | bytes 18432 | tf_op jit(solution)/shard_map/psum | solution.py:357
  796.1 0.9 convolution_divide_fusion
  797.1 65.4 %psum.63 = f32[32,64]{1,0:T(8,128)S(1)} all-reduce(f32[32,64]{1,0:T(8,128)S(1)} %convolution_divide_fusion), channel_id=1, replica_groups=mesh['depth'=16,'res'=8] {'depth'}, use_global_device_ids=true, to_apply=%region_32.33 | all-reduce | flops 2048 | bytes 16384 | tf_op jit(solution)/shard_map/psum | solution.py:359
  862.7 1.2 fusion.118
  863.9 1.2 multiply_reduce_fusion.3
  865.1 0.7 fusion.90
  865.9 0.9 add_add_fusion.8
  866.8 1.0 fusion.174
  867.8 1.0 copy.93
  868.8 6.7 fusion.21
  875.6 5.7 multiply_reduce_fusion
  881.3 3.9 fusion.168
  885.2 1.3 copy.97
  886.6 5.6 fusion.22
  892.2 3.2 copy.95
  895.4 3.2 copy.96
  898.6 5.0 fusion.13
  903.6 1.1 fusion.69
  904.7 5.6 fusion.26
  910.3 41.7 %reduce-scatter.8.cloned.1.call-done = f32[32,128]{0,1:T(8,128)} async-done(((f32[32,2048]{0,1:T(8,128)}), f32[32,128]{0,1:T(8,128)}) %reduce-scatter.8.cloned.1.call-update) | async-done | bytes 16400 | tf_op jit(solution)/shard_map/reduce_scatter | solution.py:371
  952.0 0.9 copy.98
  953.0 1.2 fusion.61
  954.2 0.7 multiply_multiply_fusion
  954.9 1.1 fusion.108
  956.0 1.8 convert_add_fusion
  957.8 35.0 %reduce-scatter.6.cloned.1.call-done = f32[16,32,64]{2,1,0:T(8,128)} async-done(((f32[16,256,64]{2,1,0:T(8,128)}), f32[16,32,64]{2,1,0:T(8,128)}) %reduce-scatter.6.cloned.1.call-update) | async-done | bytes 131088 | tf_op jit(solution)/shard_map/reduce_scatter | solution.py:366
  992.8 1.8 fusion.63
  994.6 0.7 multiply_multiply_fusion.1
  995.3 1.5 fusion.106
  996.8 2.1 add_add_fusion.7
  (264 shorter events, 15.8 us)
Async XLA Ops:
  7.2 413.0 %copy-start = (bf16[1024,128]{1,0:T(8,128)(2,1)S(1)}, bf16[1024,128]{1,0:T(8,128)(2,1)}, u32[]{:S(2)}) copy-start(bf16[1024,128]{1,0:T(8,128)(2,1)} %param.25) | copy-start | bytes 786436
  7.2 62.7 %copy-start.18 = (bf16[32,16,128]{2,1,0:T(8,128)(2,1)S(1)}, bf16[32,16,128]{2,1,0:T(8,128)(2,1)}, u32[]{:S(2)}) copy-start(bf16[32,16,128]{2,1,0:T(8,128)(2,1)} %param.15) | copy-start | bytes 393220
  7.2 62.7 %copy-start.89 = (bf16[128,8]{0,1:T(8,128)(2,1)S(1)}, bf16[128,8]{0,1:T(8,128)(2,1)}, u32[]{:S(2)}) copy-start(bf16[128,8]{0,1:T(8,128)(2,1)} %param.20) | copy-start | bytes 6148
  7.2 412.9 %all-gather.3.cloned.1.call-start = ((), (), s32[]{:S(2)}) async-start(), calls=%async_computation.3 | async-start | bytes 2228224 | tf_op jit(solution)/shard_map/all_gather | solution.py:329
  7.9 710.3 %reduce-scatter.4.cloned.1.call-start = ((), (), s32[]{:S(2)}) async-start(), calls=%async_computation.4 | async-start | bytes 294912 | tf_op jit(solution)/shard_map/reduce_scatter | solution.py:345
  10.1 384.8 %copy-start.38 = (f32[16,32]{1,0:T(8,128)}, f32[16,32]{1,0:T(8,128)S(1)}, u32[]{:S(2)}) copy-start(f32[16,32]{1,0:T(8,128)S(1)} %get-tuple-element.23) | copy-start | bytes 6148
  33.4 91.9 %copy-start.71 = (pred[16,256]{1,0:T(8,128)(4,1)}, pred[16,256]{1,0:T(8,128)(4,1)S(1)}, u32[]{:S(2)}) copy-start(pred[16,256]{1,0:T(8,128)(4,1)S(1)} %fusion.138) | copy-start | bytes 12292
  34.6 31.8 %copy-start.51 = (f32[16,32]{1,0:T(8,128)}, f32[16,32]{1,0:T(8,128)S(1)}, u32[]{:S(2)}) copy-start(f32[16,32]{1,0:T(8,128)S(1)} %broadcast_multiply_fusion.6) | copy-start | bytes 6148
  36.4 79.0 %copy-start.56 = (bf16[64,256]{1,0:T(8,128)(2,1)S(1)}, bf16[64,256]{1,0:T(8,128)(2,1)}, u32[]{:S(2)}) copy-start(bf16[64,256]{1,0:T(8,128)(2,1)} %param.19) | copy-start | bytes 98308
  37.8 92.5 %copy-start.22 = (f32[16,32,64]{2,1,0:T(8,128)}, f32[16,32,64]{2,1,0:T(8,128)S(1)}, u32[]{:S(2)}) copy-start(f32[16,32,64]{2,1,0:T(8,128)S(1)} %fusion.34) | copy-start | bytes 393220
  39.6 79.6 %copy-start.14 = (f32[16,32,8,8]{1,3,2,0:T(8,128)}, f32[16,32,8,8]{1,3,2,0:T(8,128)S(1)}, u32[]{:S(2)}) copy-start(f32[16,32,8,8]{1,3,2,0:T(8,128)S(1)} %convolution_bitcast_fusion.1) | copy-start | bytes 393220
  67.6 45.6 %copy-start.49 = (f32[32,16]{1,0:T(8,128)}, f32[32,16]{1,0:T(8,128)S(1)}, u32[]{:S(2)}) copy-start(f32[32,16]{1,0:T(8,128)S(1)} %broadcast_multiply_fusion.2) | copy-start | bytes 6148
  125.6 293.9 %copy-start.40 = (f32[16,8,32]{2,1,0:T(8,128)}, f32[16,8,32]{2,1,0:T(8,128)S(1)}, u32[]{:S(2)}) copy-start(f32[16,8,32]{2,1,0:T(8,128)S(1)} %fusion.167) | copy-start | bytes 49156
  125.6 131.8 %copy-start.75 = (bf16[64,144]{1,0:T(8,128)(2,1)S(1)}, bf16[64,144]{1,0:T(8,128)(2,1)}, u32[]{:S(2)}) copy-start(bf16[64,144]{1,0:T(8,128)(2,1)} %param.22) | copy-start | bytes 55300
  130.1 262.5 %copy-start.86 = (bf16[64,64]{1,0:T(8,128)(2,1)S(1)}, bf16[64,64]{1,0:T(8,128)(2,1)}, u32[]{:S(2)}) copy-start(bf16[64,64]{1,0:T(8,128)(2,1)} %param.23) | copy-start | bytes 24580
  130.1 264.4 %copy-start.83 = (bf16[64,64]{1,0:T(8,128)(2,1)S(1)}, bf16[64,64]{1,0:T(8,128)(2,1)}, u32[]{:S(2)}) copy-start(bf16[64,64]{1,0:T(8,128)(2,1)} %param.24) | copy-start | bytes 24580
  130.3 264.8 %copy-start.20 = (f32[16,32,64]{2,1,0:T(8,128)}, f32[16,32,64]{2,1,0:T(8,128)S(1)}, u32[]{:S(2)}) copy-start(f32[16,32,64]{2,1,0:T(8,128)S(1)} %copy.67) | copy-start | bytes 393220
  130.7 264.6 %copy-start.6 = (f32[16,32,64]{2,1,0:T(8,128)}, f32[16,32,64]{2,1,0:T(8,128)S(1)}, u32[]{:S(2)}) copy-start(f32[16,32,64]{2,1,0:T(8,128)S(1)} %get-tuple-element.42) | copy-start | bytes 393220
  130.7 127.0 %copy-start.53 = (f32[16,32]{1,0:T(8,128)}, f32[16,32]{1,0:T(8,128)S(1)}, u32[]{:S(2)}) copy-start(f32[16,32]{1,0:T(8,128)S(1)} %broadcast_multiply_fusion.5) | copy-start | bytes 6148
  131.0 126.4 %copy-start.77 = (f32[16,32]{1,0:T(8,128)}, f32[16,32]{1,0:T(8,128)S(1)}, u32[]{:S(2)}) copy-start(f32[16,32]{1,0:T(8,128)S(1)} %multiply_reduce_fusion.6) | copy-start | bytes 6148
  131.0 126.7 %copy-start.67 = (f32[16,32]{1,0:T(8,128)}, f32[16,32]{1,0:T(8,128)S(1)}, u32[]{:S(2)}) copy-start(f32[16,32]{1,0:T(8,128)S(1)} %fusion.154) | copy-start | bytes 6148
  191.7 226.7 %copy-start.90 = (f32[32]{0:T(128)}, f32[32]{0:T(128)S(1)}, u32[]{:S(2)}) copy-start(f32[32]{0:T(128)S(1)} %convert_maximum_fusion) | copy-start | bytes 388
  191.8 132.7 %copy-start.69 = (pred[16,32]{0,1:T(8,128)(4,1)}, pred[16,32]{0,1:T(8,128)(4,1)S(1)}, u32[]{:S(2)}) copy-start(pred[16,32]{0,1:T(8,128)(4,1)S(1)} %copy.68) | copy-start | bytes 1540
  257.8 137.7 %copy-start.29 = (f32[32,8,8]{1,2,0:T(8,128)}, f32[32,8,8]{1,2,0:T(8,128)S(1)}, u32[]{:S(2)}) copy-start(f32[32,8,8]{1,2,0:T(8,128)S(1)} %copy.88) | copy-start | bytes 24580
  258.7 160.2 %copy-start.31 = (f32[16,32,8]{0,2,1:T(8,128)}, f32[16,32,8]{0,2,1:T(8,128)S(1)}, u32[]{:S(2)}) copy-start(f32[16,32,8]{0,2,1:T(8,128)S(1)} %copy.71) | copy-start | bytes 49156
  258.8 160.0 %copy-start.33 = (f32[16,32,8]{0,2,1:T(8,128)}, f32[16,32,8]{0,2,1:T(8,128)S(1)}, u32[]{:S(2)}) copy-start(f32[16,32,8]{0,2,1:T(8,128)S(1)} %copy.73) | copy-start | bytes 49156
  259.3 136.2 %copy-start.16 = (f32[32,16,8]{1,2,0:T(8,128)}, f32[32,16,8]{1,2,0:T(8,128)S(1)}, u32[]{:S(2)}) copy-start(f32[32,16,8]{1,2,0:T(8,128)S(1)} %get-tuple-element.44) | copy-start | bytes 49156
  391.9 42.5 %copy-start.61 = (f32[32,8]{1,0:T(8,128)}, f32[32,8]{1,0:T(8,128)S(1)}, u32[]{:S(2)}) copy-start(f32[32,8]{1,0:T(8,128)S(1)} %get-tuple-element.15) | copy-start | bytes 3076
  663.8 288.2 %reduce-scatter.8.cloned.1.call-start = ((), (), s32[]{:S(2)}) async-start(), calls=%async_computation.6 | async-start | bytes 1114112 | tf_op jit(solution)/shard_map/reduce_scatter | solution.py:371
  663.9 55.5 %copy-start.39 = (f32[16,32]{1,0:T(8,128)S(1)}, f32[16,32]{1,0:T(8,128)}, u32[]{:S(2)}) copy-start(f32[16,32]{1,0:T(8,128)} %copy-done.38) | copy-start | bytes 6148
  663.9 55.7 %copy-start.11 = (f32[16,32,64]{2,1,0:T(8,128)S(1)}, f32[16,32,64]{2,1,0:T(8,128)}, u32[]{:S(2)}) copy-start(f32[16,32,64]{2,1,0:T(8,128)} %copy-done.10) | copy-start | bytes 393220
  663.9 55.7 %copy-start.59 = (f32[16,32]{1,0:T(8,128)S(1)}, f32[16,32]{1,0:T(8,128)}, u32[]{:S(2)}) copy-start(f32[16,32]{1,0:T(8,128)} %copy-done.58) | copy-start | bytes 6148
  663.9 55.7 %copy-start.84 = (bf16[64,64]{1,0:T(8,128)(2,1)S(1)}, bf16[64,64]{1,0:T(8,128)(2,1)}, u32[]{:S(2)}) copy-start(bf16[64,64]{1,0:T(8,128)(2,1)} %param.24) | copy-start | bytes 24580
  663.9 56.1 %copy-start.80 = (f32[16,32]{1,0:T(8,128)S(1)}, f32[16,32]{1,0:T(8,128)}, u32[]{:S(2)}) copy-start(f32[16,32]{1,0:T(8,128)} %copy-done.79) | copy-start | bytes 6148
  664.0 56.1 %copy-start.74 = (f32[16,32]{1,0:T(8,128)S(1)}, f32[16,32]{1,0:T(8,128)}, u32[]{:S(2)}) copy-start(f32[16,32]{1,0:T(8,128)} %copy-done.73) | copy-start | bytes 6148
  664.0 56.5 %copy-start.25 = (f32[16,32,64]{2,1,0:T(8,128)S(1)}, f32[16,32,64]{2,1,0:T(8,128)}, u32[]{:S(2)}) copy-start(f32[16,32,64]{2,1,0:T(8,128)} %copy-done.24) | copy-start | bytes 393220
  664.0 56.5 %copy-start.45 = (bf16[16,32,64]{2,1,0:T(8,128)(2,1)S(1)}, bf16[16,32,64]{2,1,0:T(8,128)(2,1)}, u32[]{:S(2)}) copy-start(bf16[16,32,64]{2,1,0:T(8,128)(2,1)} %param.26) | copy-start | bytes 196612
  664.0 56.5 %copy-start.87 = (bf16[64,64]{1,0:T(8,128)(2,1)S(1)}, bf16[64,64]{1,0:T(8,128)(2,1)}, u32[]{:S(2)}) copy-start(bf16[64,64]{1,0:T(8,128)(2,1)} %param.23) | copy-start | bytes 24580
  718.2 76.2 %copy-start.17 = (f32[32,16,8]{1,2,0:T(8,128)S(1)}, f32[32,16,8]{1,2,0:T(8,128)}, u32[]{:S(2)}) copy-start(f32[32,16,8]{1,2,0:T(8,128)} %copy-done.16) | copy-start | bytes 49156
  718.2 76.2 %copy-start.48 = (f32[32,8]{1,0:T(8,128)S(1)}, f32[32,8]{1,0:T(8,128)}, u32[]{:S(2)}) copy-start(f32[32,8]{1,0:T(8,128)} %copy-done.47) | copy-start | bytes 3076
  718.2 76.2 %copy-start.70 = (pred[16,32]{0,1:T(8,128)(4,1)S(1)}, pred[16,32]{0,1:T(8,128)(4,1)}, u32[]{:S(2)}) copy-start(pred[16,32]{0,1:T(8,128)(4,1)} %copy-done.69) | copy-start | bytes 1540
  718.2 76.7 %copy-start.34 = (f32[16,32,8]{0,2,1:T(8,128)S(1)}, f32[16,32,8]{0,2,1:T(8,128)}, u32[]{:S(2)}) copy-start(f32[16,32,8]{0,2,1:T(8,128)} %copy-done.33) | copy-start | bytes 49156
  718.2 76.7 %copy-start.88 = (pred[32,16]{1,0:T(8,128)(4,1)S(1)}, pred[32,16]{1,0:T(8,128)(4,1)}, u32[]{:S(2)}) copy-start(pred[32,16]{1,0:T(8,128)(4,1)} %copy.85) | copy-start | bytes 1540
  718.2 77.1 %copy-start.32 = (f32[16,32,8]{0,2,1:T(8,128)S(1)}, f32[16,32,8]{0,2,1:T(8,128)}, u32[]{:S(2)}) copy-start(f32[16,32,8]{0,2,1:T(8,128)} %copy-done.31) | copy-start | bytes 49156
  718.2 77.5 %copy-start.30 = (f32[32,8,8]{1,2,0:T(8,128)S(1)}, f32[32,8,8]{1,2,0:T(8,128)}, u32[]{:S(2)}) copy-start(f32[32,8,8]{1,2,0:T(8,128)} %copy-done.29) | copy-start | bytes 24580
  718.2 145.6 %copy-start.7 = (f32[16,32,64]{2,1,0:T(8,128)S(1)}, f32[16,32,64]{2,1,0:T(8,128)}, u32[]{:S(2)}) copy-start(f32[16,32,64]{2,1,0:T(8,128)} %copy-done.6) | copy-start | bytes 393220
  718.2 145.6 %copy-start.54 = (f32[16,32]{1,0:T(8,128)S(1)}, f32[16,32]{1,0:T(8,128)}, u32[]{:S(2)}) copy-start(f32[16,32]{1,0:T(8,128)} %copy-done.53) | copy-start | bytes 6148
  719.6 145.5 %copy-start.78 = (f32[16,32]{1,0:T(8,128)S(1)}, f32[16,32]{1,0:T(8,128)}, u32[]{:S(2)}) copy-start(f32[16,32]{1,0:T(8,128)} %copy-done.77) | copy-start | bytes 6148
  719.6 145.5 %copy-start.68 = (f32[16,32]{1,0:T(8,128)S(1)}, f32[16,32]{1,0:T(8,128)}, u32[]{:S(2)}) copy-start(f32[16,32]{1,0:T(8,128)} %copy-done.67) | copy-start | bytes 6148
  720.1 145.8 %copy-start.46 = (bf16[16,32,64]{2,1,0:T(8,128)(2,1)S(1)}, bf16[16,32,64]{2,1,0:T(8,128)(2,1)}, u32[]{:S(2)}) copy-start(bf16[16,32,64]{2,1,0:T(8,128)(2,1)} %param.26) | copy-start | bytes 196612
  720.8 145.9 %copy-start.23 = (f32[16,32,64]{2,1,0:T(8,128)S(1)}, f32[16,32,64]{2,1,0:T(8,128)}, u32[]{:S(2)}) copy-start(f32[16,32,64]{2,1,0:T(8,128)} %copy-done.22) | copy-start | bytes 393220
  720.8 145.9 %copy-start.82 = (bf16[64,64]{1,0:T(8,128)(2,1)S(1)}, bf16[64,64]{1,0:T(8,128)(2,1)}, u32[]{:S(2)}) copy-start(bf16[64,64]{1,0:T(8,128)(2,1)} %param.21) | copy-start | bytes 24580
  795.3 73.5 %copy-start.13 = (f32[8,32,256]{2,1,0:T(8,128)S(1)}, f32[8,32,256]{2,1,0:T(8,128)}, u32[]{:S(2)}) copy-start(f32[8,32,256]{2,1,0:T(8,128)} %copy-done.12) | copy-start | bytes 786436
  795.3 73.5 %copy-start.36 = (f32[16,8,32]{2,1,0:T(8,128)S(1)}, f32[16,8,32]{2,1,0:T(8,128)}, u32[]{:S(2)}) copy-start(f32[16,8,32]{2,1,0:T(8,128)} %copy-done.35) | copy-start | bytes 49156
  795.3 73.5 %copy-start.41 = (f32[16,8,32]{2,1,0:T(8,128)S(1)}, f32[16,8,32]{2,1,0:T(8,128)}, u32[]{:S(2)}) copy-start(f32[16,8,32]{2,1,0:T(8,128)} %copy-done.40) | copy-start | bytes 49156
  886.5 106.2 %reduce-scatter.6.cloned.1.call-start = ((), (), s32[]{:S(2)}) async-start(), calls=%async_computation.5 | async-start | bytes 2359296 | tf_op jit(solution)/shard_map/reduce_scatter | solution.py:366
  903.6 49.4 %copy-start.19 = (bf16[32,16,128]{2,1,0:T(8,128)(2,1)S(1)}, bf16[32,16,128]{2,1,0:T(8,128)(2,1)}, u32[]{:S(2)}) copy-start(bf16[32,16,128]{2,1,0:T(8,128)(2,1)} %param.15) | copy-start | bytes 393220
  903.6 49.4 %copy-start.50 = (f32[32,16]{1,0:T(8,128)S(1)}, f32[32,16]{1,0:T(8,128)}, u32[]{:S(2)}) copy-start(f32[32,16]{1,0:T(8,128)} %copy-done.49) | copy-start | bytes 6148
  903.6 52.4 %copy-start.44 = (bf16[32,16,128]{2,1,0:T(8,128)(2,1)S(1)}, bf16[32,16,128]{2,1,0:T(8,128)(2,1)}, u32[]{:S(2)}) copy-start(bf16[32,16,128]{2,1,0:T(8,128)(2,1)} %param.27) | copy-start | bytes 393220
  904.7 88.1 %copy-start.9 = (bf16[16,32,64]{2,1,0:T(8,128)(2,1)S(1)}, bf16[16,32,64]{2,1,0:T(8,128)(2,1)}, u32[]{:S(2)}) copy-start(bf16[16,32,64]{2,1,0:T(8,128)(2,1)} %param.14) | copy-start | bytes 196612
  904.7 92.1 %copy-start.27 = (f32[16,32,64]{2,1,0:T(8,128)S(1)}, f32[16,32,64]{2,1,0:T(8,128)}, u32[]{:S(2)}) copy-start(f32[16,32,64]{2,1,0:T(8,128)} %copy-done.26) | copy-start | bytes 393220
  904.7 94.3 %copy-start.1 = (bf16[1024,128]{1,0:T(8,128)(2,1)S(1)}, bf16[1024,128]{1,0:T(8,128)(2,1)}, u32[]{:S(2)}) copy-start(bf16[1024,128]{1,0:T(8,128)(2,1)} %param.25) | copy-start | bytes 786436
  910.3 86.5 %copy-start.52 = (f32[16,32]{1,0:T(8,128)S(1)}, f32[16,32]{1,0:T(8,128)}, u32[]{:S(2)}) copy-start(f32[16,32]{1,0:T(8,128)} %copy-done.51) | copy-start | bytes 6148
  910.3 86.5 %copy-start.66 = (f32[16,32]{1,0:T(8,128)S(1)}, f32[16,32]{1,0:T(8,128)}, u32[]{:S(2)}) copy-start(f32[16,32]{1,0:T(8,128)} %copy-done.65) | copy-start | bytes 6148
  (31 other events, 146.1 us)
Sparse Core Ops, SparseCore 0:
  10.4 52.3 all-gather.2
  664.0 38.3 reduce-scatter.3
  886.6 65.3 reduce-scatter.7
  954.3 38.4 reduce-scatter.5
where the time goes:
time: 1020 us; the launch traced here: 1010 us
  blocking collectives  509 us (50%)
  local copies, waits for them, and re-layouts  219 us (21%)
  matrix products  158 us (15%)
  waiting for transfers between devices  77.4 us (8%)
  other arithmetic  26 us (3%)
  between operations  16.2 us (2%)
    dot_general x2, local copies, waits for them, and re-layouts, body(): jnp.einsum('sia,ijab->sjb', left_proj, pair_back, precision=highest_preci...  167 us
    psum x1, blocking collectives, body(): denom_total, numer_total = lax.psum((denom_grad, numer_grad), 'depth')  73.1 us
    psum x1, blocking collectives, body(): lax.psum((own_sums[0], own_sums[1]), 'depth')  66.6 us
    psum x1, blocking collectives, body(): query_grad_total = lax.psum(query_grad, 'depth')  65.4 us
    pmax x1, blocking collectives, body(): peak_value = lax.pmax(jnp.max(logits, 0), 'depth')  64.9 us
    psum x1, blocking collectives, body(): query_grand_total = lax.psum(query_portion, 'depth')  64.9 us
    psum x1, blocking collectives, body(): lax.psum(pairwise_portion.astype(jnp.bfloat16), 'depth').astype(jnp.float32)  59.9 us
    dot_general x1, matrix products, body(): jnp.einsum('ijab,sjb->sia', pair_back, right_whole, precision=highest_pre...  54.1 us
  transfers between devices with their start and end apart: 4, of which 2 were waited for; matrix products, arithmetic and copies ran while one was open for 12% of the time, Pallas kernels for 0%

commit v1 on v0

v1 whole, which is shorter than its diff:
```python
import jax
import jax.numpy as jnp
from jax import lax
from jax.experimental import pallas as pl
from jax.experimental.pallas import tpu as pltpu
from jax.sharding import PartitionSpec as P

f32 = jnp.float32
bf16 = jnp.bfloat16
EPS = 1e-05
NEG = -1000000000.0
SCALE = 8 ** (-0.5)
NN = (((1,), (0,)), ((), ()))
NT = (((1,), (1,)), ((), ()))
TN = (((0,), (0,)), ((), ()))
VMEM = pltpu.CompilerParams(vmem_limit_bytes=50 * 1024 * 1024)


def mm(a, b, dims=NN):
    return lax.dot_general(a, b, dims, preferred_element_type=f32)


def split(x):
    hi = x.astype(bf16)
    lo = (x - hi.astype(f32)).astype(bf16)
    return hi, lo


def split3(x):
    hi = x.astype(bf16)
    rest = x - hi.astype(f32)
    mid = rest.astype(bf16)
    lo = (rest - mid.astype(f32)).astype(bf16)
    return hi, mid, lo


def cat(parts, axis):
    return jnp.concatenate(parts, axis=axis)


def mm2(x, w, dims=NN):
    hi, lo = split(x)
    return mm(hi, w, dims) + mm(lo, w, dims)


def mm3(x, w):
    hi, mid, lo = split3(x)
    return mm(hi, w) + mm(mid, w) + mm(lo, w)


def norm_rows(x):
    center = x - jnp.mean(x, -1, keepdims=True)
    rstd = lax.rsqrt(jnp.mean(center * center, -1, keepdims=True) + EPS)
    return center * rstd, rstd


def norm_back(normed, rstd, grad):
    return rstd * (
        grad
        - jnp.mean(grad, -1, keepdims=True)
        - normed * jnp.mean(grad * normed, -1, keepdims=True)
    )


def pair2(x):
    hi, lo = split(x)
    return cat([hi, lo], 1)


def head_mask(rows, cols, row_div, col_div):
    a = lax.broadcasted_iota(jnp.int32, (rows, cols), 0) // row_div
    b = lax.broadcasted_iota(jnp.int32, (rows, cols), 1) // col_div
    return (a == b).astype(f32)


def bias_kernel(pair_ref, wb_ref, out_ref, scr):
    xn, _ = norm_rows(pair_ref[...].astype(f32).reshape(512, 128))
    scr[...] = xn.reshape(32, 16, 128)
    wbt = wb_ref[...].astype(f32).T
    w2 = cat([wbt, wbt], 1).astype(bf16)
    own = head_mask(8, 256, 1, 32)
    rows = []
    for j in range(16):
        x2 = pair2(scr[:, j, :])
        tiled = cat([x2] * 8, 0)
        full = mm(w2, tiled, NT)
        rows.append(jnp.sum(full * own, 0, keepdims=True))
    block = cat(rows, 0)
    for k in range(16):
        out_ref[k] = block


def row_fwd_kernel(
    g_ref, own_ref, bias_ref, win_ref, wo_ref,
    p_ref, o_ref, x2_ref, x2o_ref, m1_ref, any_ref, c1_ref,
    wqg, wvt2, wkk, wo2,
):
    s = pl.program_id(0)

    @pl.when(s == 0)
    def _():
        w = win_ref[...].astype(f32)
        wt = w.T
        qg = cat([wt[0:64], wt[192:256]], 0)
        wqg[...] = cat([qg, qg], 1).astype(bf16)
        wvt = wt[128:192]
        wvt2[...] = cat([wvt, wvt], 1).astype(bf16)
        wk = w[:, 64:128]
        row = cat([wk, wk], 1)
        wkk[...] = cat([row, row], 0).astype(bf16)
        wo = wo_ref[...].astype(f32)
        wo2[...] = cat([wo, wo], 0).astype(bf16)

    g = g_ref[...].reshape(256, 128).astype(f32)
    live = g[:, 64:65]
    xn, _ = norm_rows(g[:, :64])
    x2 = pair2(xn)
    x2_ref[0] = x2
    kk = mm(x2, wkk[...])
    khi = kk.astype(bf16)
    lane = lax.broadcasted_iota(jnp.int32, (256, 128), 1)
    k2 = jnp.where(lane < 64, kk, kk - khi.astype(f32)).astype(bf16)
    vt = mm(wvt2[...], x2, NT)

    own = own_ref[0].astype(f32)
    xo = own[:, :64]
    xon, _ = norm_rows(xo)
    x2o = pair2(xon)
    x2o_ref[0] = x2o
    qg = mm(wqg[...], cat([x2o] * 8, 0), NT)
    heads = head_mask(64, 256, 8, 32)
    q = qg[:64] * (heads * SCALE)
    gate = jax.nn.sigmoid(qg[64:])
    qhi, qlo = split(q)
    logits = mm(k2, cat([qhi, qhi], 0)) + mm(khi[:, :64], qlo)
    logits = logits + bias_ref[...].reshape(256, 256)
    logits = jnp.where(live > 0, logits, NEG)
    e = jnp.exp(logits - jnp.max(logits, 0, keepdims=True))
    p = e * (1.0 / jnp.sum(e, 0, keepdims=True))
    p_ref[0] = p
    any_ref[0] = jnp.broadcast_to(jnp.max(live, 0, keepdims=True), (8, 256))
    phi, plo = split(p)
    vhi, vlo = split(vt)
    first = mm(cat([vhi, vlo], 0), phi)
    o = (first[:64] + first[64:] + mm(vhi, plo)) * heads
    o_ref[0] = o
    ahi, alo = split(o * gate)
    y = mm(cat([ahi, alo], 0), wo2[...], TN)
    m1 = xo + jnp.sum(y.reshape(8, 32, 64), 0)
    m1_ref[0] = m1
    c1_ref[:, 0, s, :] = cat([m1[:16], m1[16:]], 1)
    lv = own[:, 64:]
    c1_ref[:, 1, s, :] = cat([lv[:16], lv[16:]], 1)


def diag2(w):
    z = jnp.zeros_like(w)
    return cat([cat([w, z], 1), cat([z, w], 1)], 0)


def col_kernel(c1_ref, cw_ref, out_ref):
    x = c1_ref[:, 0].reshape(256, 128)
    live = c1_ref[:, 1].reshape(256, 128)
    halves = (head_mask(128, 128, 64, 64) * (1.0 / 64)).astype(bf16)
    center = x - mm3(x, halves)
    xn = center * lax.rsqrt(mm3(center * center, halves) + EPS)
    cw = cw_ref[...].astype(f32)
    wq = diag2(cw[:, 0:64]).astype(bf16)
    wk = diag2(cw[:, 64:128]).astype(bf16)
    wv = diag2(cw[:, 128:192]).astype(bf16)
    total = jnp.sum(live * xn, 0, keepdims=True)
    count = jnp.sum(live, 0, keepdims=True)
    mean = total / jnp.maximum(count, 1.0)
    colq = mm3(jnp.broadcast_to(mean, (8, 128)), wq)[0:1] * SCALE
    kt = mm2(xn, wk)
    vt = mm2(xn, wv)
    groups = head_mask(128, 128, 8, 8).astype(bf16)
    logits = jnp.where(live > 0, mm3(kt * colq, groups), NEG)
    peak = jnp.max(logits, 0, keepdims=True)
    e = jnp.exp(logits - peak)
    den = jnp.sum(e, 0, keepdims=True)
    w = e / den
    wv_ = w * vt
    attended = jnp.sum(wv_, 0, keepdims=True)
    khi, klo = split(kt)

    def by_key(z):
        zhi, zlo = split(z)
        full = mm(khi, zhi, TN) + mm(klo, zhi, TN) + mm(khi, zlo, TN)
        lane = lax.broadcasted_iota(jnp.int32, (8, 128), 1)
        return jnp.where(lane < 64, full[0:8], full[64:72])

    lt = live.T
    rows = [
        by_key(wv_), by_key(w), attended, peak, den, colq, count, count, count, count,
        lt[0:1, :128], lt[0:1, 128:], lt[64:65, :128], lt[64:65, 128:],
        count, count, count, count,
    ]
    block = cat(rows, 0)
    for k in range(16):
        out_ref[k] = block


def unpair(x):
    return cat([x[:, 0:64], x[:, 64:128]], 0)


def spread(v):
    return jnp.broadcast_to(v[None], (16, 32, 64)).reshape(512, 64)


def factor_kernel(m1_ref, c2_ref, own_ref, cw_ref, wv_ref, wt_ref, m2_ref, d_ref):
    m1 = m1_ref[...].reshape(512, 64)
    live = own_ref[...].reshape(512, 128)[:, 64:].astype(f32)
    attended = unpair(c2_ref[:, 16, :])
    xn, _ = norm_rows(m1)
    gate = jax.nn.sigmoid(mm2(xn, cw_ref[:, 192:256]))
    m2 = m1 + mm2(gate * spread(attended), wv_ref[...])
    m2_ref[...] = m2.reshape(16, 32, 64)
    xn2, _ = norm_rows(m2)
    lr = live * mm2(xn2, wt_ref[...])
    lt = cat(
        [cat([c2_ref[:, 24, :], c2_ref[:, 25, :]], 1), cat([c2_ref[:, 26, :], c2_ref[:, 27, :]], 1)],
        0,
    )
    pad = jnp.zeros((12, 32, 64), f32)
    planes = [lt[None, :, 64 * k:64 * k + 64] for k in range(4)]
    right = cat(planes + [pad], 0).reshape(512, 64)
    block = cat([lr, right], 1).astype(bf16).reshape(16, 32, 128)
    for k in range(8):
        d_ref[k] = block


def outer_kernel(
    da_ref, own_ref, cta_ref, ctb_ref, w_ref, m2_ref, c2_ref, m1_ref, adj_ref, cw_ref, wv_ref,
    wt_ref, g2_ref, dcg_ref, e1_ref,
    inv, turned, stage, res, lrs,
):
    step = pl.program_id(0)
    steps = 8
    per = 4

    @pl.when(step == 0)
    def _():
        norm = jnp.zeros((256, 32), f32)
        for k in range(4):
            allk = da_ref[:, k, :, 64:].reshape(256, 64)
            ownk = own_ref[0, k, :, 64:]
            norm = norm + mm(allk, ownk, NT)
        value = 1.0 / jnp.maximum(norm, 1.0)
        for k in range(32):
            inv[k] = jnp.broadcast_to(value[:, k:k + 1], (256, 128))
        for s in range(16):
            piece = da_ref[:, s].reshape(256, 128).astype(f32).T
            for half in range(2):
                cols = piece[:, 128 * half:128 * half + 128]
                lrs[half, pl.ds(s, 32, stride=16), :] = cols[0:32]
                lrs[half, pl.ds(512 + s, 32, stride=16), :] = cols[32:64]
        for half in range(2):
            turned[0, :, 128 * half:128 * half + 128] = lrs[half, 512:1024].astype(bf16)
            turned[1, :, 128 * half:128 * half + 128] = lrs[half, 0:512].astype(bf16)

    for side in range(2):
        for k in range(per):
            one = step * per + k
            if side == 0:
                ct = cta_ref[:, 0, k].reshape(256, 128)
            else:
                ct = ctb_ref[:, 0, 0, k].reshape(256, 128)
            hi, lo = split(ct.astype(f32) * inv[one])
            both = mm(turned[side], cat([hi, lo], 1))
            u = both[:, :128] + both[:, 128:]
            uhi, ulo = split(u)
            stage[side, :, pl.ds(pl.multiple_of(one * 16, 16), 16), 0:128] = uhi.reshape(32, 16, 128)
            stage[side, :, pl.ds(pl.multiple_of(one * 16, 16), 16), 128:256] = ulo.reshape(32, 16, 128)

    @pl.when(step == steps - 1)
    def _():
        grads = []
        for side in range(2):
            def body(b, acc):
                return acc + mm(stage[side, b], w_ref[side, b], NT)

            acc = lax.fori_loop(0, 32, body, jnp.zeros((512, 32), f32))
            res[:, 0:32] = acc
            grads.append(cat([res[pl.ds(s, 32, stride=16), :] for s in range(16)], 0)[:, 0:32])
        live = own_ref[...].reshape(512, 128)
        lv = adj_ref[...].reshape(512, 128)[:, 64:].astype(f32)
        dlr = cat(grads, 1) * lv
        m2 = m2_ref[...].reshape(512, 64)
        xn2, rstd2 = norm_rows(m2)
        adj = adj_ref[...].reshape(512, 128)[:, :64].astype(f32)
        g2 = adj + norm_back(xn2, rstd2, mm2(dlr, wt_ref[...], NT))
        g2_ref[...] = g2.reshape(16, 32, 64)
        xn, _ = norm_rows(m1_ref[...].reshape(512, 64))
        gate = jax.nn.sigmoid(mm2(xn, cw_ref[:, 192:256]))
        dmix = mm2(g2, wv_ref[...], NT)
        attended = spread(unpair(c2_ref[:, 16, :]))
        dcg_ref[...] = (dmix * attended * gate * (1.0 - gate)).reshape(16, 32, 64)
        da = jnp.sum((gate * dmix).reshape(16, 32, 64), 0)
        packed = cat([da[:16], da[16:]], 1)
        for k in range(16):
            e1_ref[k] = packed


def row_bwd_kernel(
    e1_ref, c2_ref, m1_ref, own_ref, g2_ref, dcg_ref, cw_ref,
    p_ref, o_ref, x2_ref, x2o_ref, any_ref, win_ref, wo_ref,
    g1_ref, dxo_ref, f_ref, bias_ref,
    g1s, wqg, wkt2, wvv, wo2, wback, wown,
):
    s = pl.program_id(0)

    @pl.when(s == 0)
    def _():
        w = win_ref[...].astype(f32)
        wt = w.T
        qg = cat([wt[0:64], wt[192:256]], 0)
        wqg[...] = cat([qg, qg], 1).astype(bf16)
        wkt2[...] = cat([wt[64:128], wt[64:128]], 1).astype(bf16)
        wv = w[:, 128:192]
        row = cat([wv, wv], 1)
        wvv[...] = cat([row, row], 0).astype(bf16)
        wo = wo_ref[...].astype(f32)
        wo2[...] = cat([wo, wo], 1).astype(bf16)
        wback[...] = cat([wt[64:128], wt[64:128], wt[128:192], wt[128:192]], 0).astype(bf16)
        wown[...] = cat([qg, qg], 0).astype(bf16)

        cw = cw_ref[...]
        groups = head_mask(64, 64, 8, 8).astype(bf16)
        da = jnp.sum(e1_ref[...], 0)
        da = unpair(da)
        attended = unpair(c2_ref[:, 16, :])
        peak = unpair(c2_ref[:, 17, :])
        den = unpair(c2_ref[:, 18, :])
        colq = unpair(c2_ref[:, 19, :])
        count = unpair(c2_ref[:, 20, :])
        delta = mm3(da * attended, groups)
        feature = lax.broadcasted_iota(jnp.int32, (32, 64), 1) % 8
        dq = jnp.zeros((32, 64), f32)
        for k in range(8):
            z = mm3(da * unpair(c2_ref[:, k, :]), groups) - delta * unpair(c2_ref[:, 8 + k, :])
            dq = dq + jnp.where(feature == k, z, 0.0)
        dtotal = mm2(dq * SCALE, cw[:, 0:64], NT) / jnp.maximum(count, 1.0)
        live = own_ref[...].reshape(512, 128)[:, 64:].astype(f32)
        xn, rstd = norm_rows(m1_ref[...].reshape(512, 64))
        kt = mm2(xn, cw[:, 64:128])
        vt = mm2(xn, cw[:, 128:192])
        qs = spread(colq)
        logits = jnp.where(live > 0, mm3(kt * qs, groups), NEG)
        weights = jnp.exp(logits - spread(peak)) / spread(den)
        das = spread(da)
        dl = weights * (mm2(vt * das, groups) - spread(delta)) * live
        dxn = (
            mm2(dcg_ref[...].reshape(512, 64), cw[:, 192:256], NT)
            + mm2(dl * qs, cw[:, 64:128], NT)
            + mm2(weights * das, cw[:, 128:192], NT)
            + live * spread(dtotal)
        )
        g1 = g2_ref[...].reshape(512, 64) + norm_back(xn, rstd, dxn)
        g1s[...] = g1.reshape(16, 32, 64)
        bias_ref[...] = jnp.zeros_like(bias_ref)

    dm = g1s[s]
    g1_ref[0] = dm
    heads = head_mask(64, 256, 8, 32)
    p = p_ref[0]
    o = o_ref[0]
    x2 = x2_ref[0]
    x2o = x2o_ref[0]
    vv = mm(x2, wvv[...])
    vhi = vv.astype(bf16)
    lane = lax.broadcasted_iota(jnp.int32, (256, 128), 1)
    v2 = jnp.where(lane < 64, vv, vv - vhi.astype(f32)).astype(bf16)
    khi, klo = split(mm(wkt2[...], x2, NT))
    qg = mm(wqg[...], cat([x2o] * 8, 0), NT)
    q = qg[:64] * (heads * SCALE)
    gate = jax.nn.sigmoid(qg[64:])
    dout = mm(wo2[...], cat([pair2(dm)] * 8, 0), NT)
    dgate = dout * o * gate * (1.0 - gate)
    do = dout * gate * heads
    do_live = do * any_ref[0, 0:1, :]
    delta = jnp.sum(do_live * o, 0, keepdims=True)
    lhi, llo = split(do_live)
    dp = mm(v2, cat([lhi, lhi], 0)) + mm(vhi[:, :64], llo)
    ds = p * (dp - delta)
    bias_ref[...] += ds.reshape(16, 16, 256)
    shi, slo = split(ds)
    first = mm(cat([khi, klo], 0), shi)
    dq = (first[:64] + first[64:] + mm(khi, slo)) * (heads * SCALE)
    qhi, qlo = split(q)
    zero = jnp.zeros((64, 256), bf16)
    dk = mm(shi, cat([qhi, qlo], 0), NT) + mm(slo, cat([qhi, zero], 0), NT)
    phi, plo = split(p)
    dhi, dlo = split(do)
    dv = mm(phi, cat([dhi, dlo], 0), NT) + mm(plo, cat([dhi, zero], 0), NT)
    kv = cat([dk, dv], 1)
    dx = mm2(kv, wback[...]).reshape(8, 32, 64)
    f_ref[:, 0] = cat([dx[:, :16], dx[:, 16:]], 2)
    qhi2, qlo2 = split(cat([dq, dgate], 0))
    dxo = mm(cat([qhi2, qlo2], 0), wown[...], TN)
    dxo_ref[0] = jnp.sum(dxo.reshape(8, 32, 64), 0)


def final_rows_kernel(f_ref, dxo_ref, g1_ref, own_ref, out_ref):
    total = jnp.sum(f_ref[...], 0)
    total = cat([total[:, :, :64], total[:, :, 64:]], 1).reshape(512, 64)
    total = total + dxo_ref[...].reshape(512, 64)
    xn, rstd = norm_rows(own_ref[...].reshape(512, 128)[:, :64].astype(f32))
    out = g1_ref[...].reshape(512, 64) + norm_back(xn, rstd, total)
    out_ref[...] = out.reshape(16, 32, 64)


def final_pair_kernel(b_ref, pair_ref, wb_ref, ct_ref, out_ref, scr):
    total = jnp.sum(b_ref[...], 0)
    wbt = wb_ref[...].astype(f32).T
    w2 = cat([wbt, wbt], 0).astype(bf16)
    own = head_mask(8, 256, 1, 32)
    for j in range(16):
        wide = jnp.broadcast_to(total[j:j + 1, :], (8, 256)) * own
        hi, lo = split(wide)
        y = mm(cat([hi, lo], 0), w2, TN)
        scr[:, j, :] = jnp.sum(y.reshape(8, 32, 128), 0)
    xn, rstd = norm_rows(pair_ref[...].reshape(512, 128).astype(f32))
    out = norm_back(xn, rstd, scr[...].reshape(512, 128)) + ct_ref[...].reshape(512, 128).astype(f32)
    out_ref[...] = out.reshape(32, 16, 128)


def sds(shape, dtype=f32):
    return jax.ShapeDtypeStruct(shape, dtype)


def full(shape):
    zeros = (0,) * len(shape)
    return pl.BlockSpec(shape, lambda s: zeros)


def row(shape):
    rest = (0,) * (len(shape) - 1)
    return pl.BlockSpec((1,) + shape[1:], lambda s: (s,) + rest)


def whole_call(kernel, out_shape, *args, scratch=()):
    return pl.pallas_call(
        kernel, out_shape=out_shape, scratch_shapes=list(scratch), compiler_params=VMEM
    )(*args)


def body(
    alignment_state,
    pairwise_state,
    alignment_mask,
    residue_entry_mask,
    sequence_live_count,
    horizontal_intake_coefs,
    pairwise_bias_weights,
    horizontal_readout_coefs,
    column_input_weights,
    vertical_readout_coefs,
    tensor_factor_coefs,
    outer_output_weights,
    adjoint_of_result_track,
    pairwise_cotangent,
):
    seq = jnp.arange(16, dtype=jnp.int32)
    live = (
        alignment_mask
        * residue_entry_mask[None, :]
        * (seq < sequence_live_count[0]).astype(jnp.int32)[:, None]
    ).astype(bf16)
    live_lanes = jnp.broadcast_to(live[:, :, None], (16, 32, 64))
    own = cat([alignment_state, live_lanes], 2)
    adj = cat([adjoint_of_result_track, live_lanes], 2)
    cw = cat(
        [
            column_input_weights[:, :64],
            jnp.tile(column_input_weights[:, 64:72], (1, 8)),
            jnp.tile(column_input_weights[:, 72:80], (1, 8)),
            column_input_weights[:, 80:],
        ],
        1,
    )
    w3 = outer_output_weights.reshape(32, 32, 128)
    wouter = jnp.stack([w3.transpose(1, 0, 2), w3], 0)
    wouter = cat([wouter, wouter], 3)

    turned = pairwise_cotangent.transpose(1, 0, 2)
    perm = [(d * 8 + r, (2 * r + d % 2) * 8 + d // 2) for d in range(16) for r in range(8)]
    turned = lax.ppermute(turned, ("depth", "res"), perm)
    both = cat([pairwise_cotangent.reshape(512, 128), turned.reshape(512, 128)], 0)
    ct = lax.all_gather(both, "depth", axis=0, tiled=False)

    rows = lax.all_to_all(jnp.broadcast_to(own[None], (8, 16, 32, 128)), "res", 0, 0)
    bias_block = whole_call(
        bias_kernel, sds((16, 16, 256)), pairwise_state, pairwise_bias_weights,
        scratch=[pltpu.VMEM((32, 16, 128), f32)],
    )
    bias = lax.all_to_all(bias_block, "depth", 0, 0)

    grow = pl.BlockSpec((8, 1, 32, 128), lambda s: (0, s, 0, 0))
    p, o, x2, x2o, m1, any_live, c1 = pl.pallas_call(
        row_fwd_kernel,
        grid=(16,),
        in_specs=[grow, row((16, 32, 128)), full((16, 16, 256)), full((64, 256)), full((64, 64))],
        out_specs=[
            row((16, 256, 256)), row((16, 64, 256)), row((16, 256, 128)), row((16, 32, 128)),
            row((16, 32, 64)), row((16, 8, 256)), full((16, 2, 16, 128)),
        ],
        out_shape=[
            sds((16, 256, 256)), sds((16, 64, 256)), sds((16, 256, 128), bf16),
            sds((16, 32, 128), bf16), sds((16, 32, 64)), sds((16, 8, 256)), sds((16, 2, 16, 128)),
        ],
        scratch_shapes=[
            pltpu.VMEM((128, 128), bf16), pltpu.VMEM((64, 128), bf16),
            pltpu.VMEM((128, 128), bf16), pltpu.VMEM((128, 64), bf16),
        ],
        compiler_params=VMEM,
    )(rows, own, bias, horizontal_intake_coefs, horizontal_readout_coefs)

    c1 = lax.all_to_all(c1, "depth", 0, 0)
    c2 = whole_call(col_kernel, sds((16, 32, 128)), c1, cw)
    c2 = lax.all_to_all(c2, "depth", 0, 0)
    m2, dblock = whole_call(
        factor_kernel, [sds((16, 32, 64)), sds((8, 16, 32, 128), bf16)],
        m1, c2, own, cw, vertical_readout_coefs, tensor_factor_coefs,
    )
    factors = lax.all_to_all(dblock, "res", 0, 0)

    cta = ct.reshape(16, 2, 32, 16, 128)
    ctb = ct.reshape(8, 2, 2, 16, 32, 128)
    g2, dcg, e1 = pl.pallas_call(
        outer_kernel,
        grid=(8,),
        in_specs=[
            full((8, 16, 32, 128)),
            pl.BlockSpec((1, 16, 32, 128), lambda s: (0, 0, 0, 0)),
            pl.BlockSpec((16, 1, 4, 16, 128), lambda s: (0, 0, s, 0, 0)),
            pl.BlockSpec((8, 1, 1, 4, 32, 128), lambda s: (0, s // 4, 1, s % 4, 0, 0)),
            full((2, 32, 32, 256)),
            full((16, 32, 64)), full((16, 32, 128)), full((16, 32, 64)), full((16, 32, 128)),
            full((64, 256)), full((64, 64)), full((64, 64)),
        ],
        out_specs=[full((16, 32, 64)), full((16, 32, 64)), full((16, 16, 128))],
        out_shape=[sds((16, 32, 64)), sds((16, 32, 64)), sds((16, 16, 128))],
        scratch_shapes=[
            pltpu.VMEM((32, 256, 128), f32),
            pltpu.VMEM((2, 512, 256), bf16),
            pltpu.VMEM((2, 32, 512, 256), bf16),
            pltpu.VMEM((512, 128), f32),
            pltpu.VMEM((2, 1024, 128), f32),
        ],
        compiler_params=VMEM,
    )(
        factors, dblock, cta, ctb, wouter, m2, c2, m1, adj, cw, vertical_readout_coefs,
        tensor_factor_coefs,
    )
    e1 = lax.all_to_all(e1, "depth", 0, 0)

    g1, dxo, fblock, bblock = pl.pallas_call(
        row_bwd_kernel,
        grid=(16,),
        in_specs=[
            full((16, 16, 128)), full((16, 32, 128)), full((16, 32, 64)), full((16, 32, 128)),
            full((16, 32, 64)), full((16, 32, 64)), full((64, 256)),
            row((16, 256, 256)), row((16, 64, 256)), row((16, 256, 128)), row((16, 32, 128)),
            row((16, 8, 256)), full((64, 256)), full((64, 64)),
        ],
        out_specs=[
            row((16, 32, 64)), row((16, 32, 64)),
            pl.BlockSpec((8, 1, 16, 128), lambda s: (0, s, 0, 0)), full((16, 16, 256)),
        ],
        out_shape=[sds((16, 32, 64)), sds((16, 32, 64)), sds((8, 16, 16, 128)), sds((16, 16, 256))],
        scratch_shapes=[
            pltpu.VMEM((16, 32, 64), f32),
            pltpu.VMEM((128, 128), bf16), pltpu.VMEM((64, 128), bf16), pltpu.VMEM((128, 128), bf16),
            pltpu.VMEM((64, 128), bf16), pltpu.VMEM((256, 64), bf16), pltpu.VMEM((256, 64), bf16),
        ],
        compiler_params=VMEM,
    )(
        e1, c2, m1, own, g2, dcg, cw, p, o, x2, x2o, any_live,
        horizontal_intake_coefs, horizontal_readout_coefs,
    )
    fsum = lax.all_to_all(fblock, "res", 0, 0)
    bsum = lax.all_to_all(bblock, "depth", 0, 0)
    alignment_gradient = whole_call(final_rows_kernel, sds((16, 32, 64)), fsum, dxo, g1, own)
    pair_grad = whole_call(
        final_pair_kernel, sds((32, 16, 128)), bsum, pairwise_state, pairwise_bias_weights,
        pairwise_cotangent, scratch=[pltpu.VMEM((32, 16, 128), f32)],
    )
    return alignment_gradient, pair_grad


def solution(mesh):
    in_specs = (
        P("depth", "res", None),
        P("res", "depth", None),
        P("depth", "res"),
        P("res"),
        P("depth"),
        P(),
        P(),
        P(),
        P(),
        P(),
        P(),
        P(),
        P("depth", "res", None),
        P("res", "depth", None),
    )
    out_specs = (P("depth", "res", None), P("res", "depth", None))
    return jax.shard_map(body, mesh=mesh, in_specs=in_specs, out_specs=out_specs, check_vma=False)
```

time: 1020 us -> 243 us (0.24); the launches traced: 1010 us -> 242 us
  blocking collectives: 509 us -> 36.2 us
  local copies, waits for them, and re-layouts: 219 us -> 7.79 us
  matrix products: 158 us -> 0 us
  Pallas kernels: 0 us -> 77 us
  starting transfers between devices: 0.16 us -> 41 us
  other arithmetic: 26 us -> 3.76 us
  waiting for transfers between devices: 77.4 us -> 61.5 us
    psum x5 -> x0, blocking collectives: 330 us -> none  [the longest x1 73.1 us: body(): denom_total, numer_total = lax.psum((denom_grad, numer_grad), 'depth')]
    dot_general x3 -> x0, local copies, waits for them, and re-layouts: 167 us -> none  [the longest x2 167 us: body(): jnp.einsum('sia,ijab->sjb', left_proj, pair_back, precision=highest_preci...]
    dot_general x37 -> x0, matrix products: 158 us -> none  [the longest x1 54.1 us: body(): jnp.einsum('ijab,sjb->sia', pair_back, right_whole, precision=highest_pre...]
    all_gather x4 -> x0, blocking collectives: 114 us -> none  [the longest x1 42 us: body(): lax.all_gather(flat_bias, 'depth', axis=1, tiled=True)]
    pallas_call x0 -> x8, Pallas kernels: none -> 77 us  [the longest x1 26.2 us: body(): pl.pallas_call(outer_kernel, grid=(8,), in_specs=[full((8, 16, 32, 128)),...]
    reduce_scatter x3 -> x0, waiting for transfers between devices: 76.7 us -> none  [the longest x1 41.7 us: body(): lax.psum_scatter(bias_gradient_complete.reshape(residue_row_group, -1), '...]
    pmax x1 -> x0, blocking collectives: 64.9 us -> none  [body(): peak_value = lax.pmax(jnp.max(logits, 0), 'depth')]
    all_to_all x0 -> x5, waiting for transfers between devices: none -> 61.5 us  [the longest x1 17 us: body(): lax.all_to_all(jnp.broadcast_to(own[None], (8, 16, 32, 128)), 'res', 0, 0)]
  transfers between devices with their start and end apart: 4 -> 7, of which waited for: 2 -> 5; matrix products, arithmetic and copies ran while one was open for 12% -> 2% of each run, Pallas kernels for 0% -> 12%
where the time goes in v1:
time: 243 us; the launch traced here: 242 us
  Pallas kernels  77 us (32%)
  waiting for transfers between devices  61.5 us (25%)
  starting transfers between devices  41 us (17%)
  blocking collectives  36.2 us (15%)
  between operations  14.9 us (6%)
  local copies, waits for them, and re-layouts  7.79 us (3%)
  other arithmetic  3.76 us (2%)
    pallas_call x1, Pallas kernels, body(): pl.pallas_call(outer_kernel, grid=(8,), in_specs=[full((8, 16, 32, 128)),...  26.2 us
    all_to_all x1, starting transfers between devices, body(): bias = lax.all_to_all(bias_block, 'depth', 0, 0)  22.4 us
    pallas_call x1, Pallas kernels, body(): pl.pallas_call(row_fwd_kernel, grid=(16,), in_specs=[grow, row((16, 32, 1...  22.1 us
    pallas_call x1, Pallas kernels, body(): pl.pallas_call(row_bwd_kernel, grid=(16,), in_specs=[full((16, 16, 128)),...  20.7 us
    all_to_all x1, waiting for transfers between devices, body(): lax.all_to_all(jnp.broadcast_to(own[None], (8, 16, 32, 128)), 'res', 0, 0)  17 us
    all_to_all x1, waiting for transfers between devices, body(): factors = lax.all_to_all(dblock, 'res', 0, 0)  13.3 us
    all_to_all x1, waiting for transfers between devices, body(): fsum = lax.all_to_all(fblock, 'res', 0, 0)  13.1 us
    all_to_all x1, blocking collectives, body(): e1 = lax.all_to_all(e1, 'depth', 0, 0)  12.2 us
  transfers between devices with their start and end apart: 7, of which 5 were waited for; matrix products, arithmetic and copies ran while one was open for 2% of the time, Pallas kernels for 12%

profile of v1, /device:TPU:1, one launch (start us, length us, event | category | flops | bytes accessed | tf_op | source)
XLA Modules:
  0.0 242.1 jit_solution(7045415267034698074)
XLA Ops:
  7.2 0.0 copy-start.11
  7.2 0.0 copy-start.12
  7.2 0.0 all-gather.3.cloned.1.call-start
  7.2 1.0 copy.29
  8.2 0.7 collective-permute-start
  8.9 0.0 collective-permute-done
  8.9 1.6 pad_maximum_fusion
  10.5 0.0 all-gather.3.cloned.1.call-update
  10.6 0.8 copy.18.wb_ref
  11.4 0.0 copy-start.3
  11.4 0.9 copy-done.3
  12.3 1.8 shard_map.149
  14.1 22.4 %all-to-all-start.1 = ((f32[16,16,256]{2,1,0:T(8,128)}), f32[16,16,256]{2,1,0:T(8,128)S(1)}, u32[]{:S(2)}, u32[]{:S(2)}) async-start(f32[16,16,256]{2,1,0:T(8,128)} %shard_map.149), calls=%async_computation.1 | async-start | bytes 524288 | tf_op jit(solution)/shard_map/all_to_all | solution.py:498
  36.5 0.0 copy-start.13
  37.1 0.8 multiply_convert_fusion
  37.9 0.1 broadcast_in_dim.4
  38.0 0.0 copy-done.11
  38.1 0.0 copy-done.12
  38.1 0.0 copy-start.5
  38.1 0.0 copy-start.6
  38.1 0.1 pad_maximum_fusion.1
  38.2 9.6 %all-to-all-done.1.bias_ref = f32[16,16,256]{2,1,0:T(8,128)S(1)} async-done(((f32[16,16,256]{2,1,0:T(8,128)}), f32[16,16,256]{2,1,0:T(8,128)S(1)}, u32[]{:S(2)}, u32[]{:S(2)}) %all-to-all-start.1) | async-done | bytes 262176 | tf_op jit(solution)/shard_map/all_to_all | solution.py:498
  47.8 1.2 broadcast_in_dim.5
  49.0 3.6 %all-to-all-start = ((bf16[8,16,32,128]{3,2,1,0:T(8,128)(2,1)}), bf16[8,16,32,128]{3,2,1,0:T(8,128)(2,1)S(1)}, u32[]{:S(2)}, u32[]{:S(2)}) async-start(bf16[8,16,32,128]{3,2,1,0:T(8,128)(2,1)} %broadcast_in_dim.5), calls=%async_computation | async-start | bytes 2097152 | tf_op jit(solution)/shard_map/all_to_all | solution.py:493
  52.6 0.0 copy-done.13
  52.6 0.0 copy-start.7
  52.6 0.0 copy-start.8
  52.6 0.1 fusion.1
  52.7 0.1 copy.19
  52.8 0.1 copy.20
  52.9 0.1 copy.22
  53.0 0.1 copy.21
  53.1 17.0 %all-to-all-done.g_ref = bf16[8,16,32,128]{3,2,1,0:T(8,128)(2,1)S(1)} async-done(((bf16[8,16,32,128]{3,2,1,0:T(8,128)(2,1)}), bf16[8,16,32,128]{3,2,1,0:T(8,128)(2,1)S(1)}, u32[]{:S(2)}, u32[]{:S(2)}) %all-to-all-start) | async-done | bytes 1048608 | tf_op jit(solution)/shard_map/all_to_all | solution.py:493
  70.0 0.0 copy-start.9
  70.1 1.0 copy-done.9
  71.1 0.0 copy-done.5
  71.1 0.0 copy-done.6
  71.1 22.1 %shard_map.150 = (f32[16,256,256]{2,1,0:T(8,128)}, f32[16,64,256]{2,1,0:T(8,128)S(1)}, bf16[16,256,128]{2,1,0:T(8,128)(2,1)S(1)}, bf16[16,32,128]{2,1,0:T(8,128)...) custom-call(bf16[8,16,32,128]{3,2,1,0:T(8,128)(2,1)} %copy-done.9, ...), custom_call_target="tpu_custom_call" | custom-call | tf_op jit(solution)/shard_map/pallas_call | solution.py:501
  93.2 1.0 copy-done.1
  94.2 1.0 copy-done.2
  95.2 6.8 %all-to-all-start.2 = ((f32[16,2,16,128]{3,2,1,0:T(8,128)}), f32[16,2,16,128]{3,2,1,0:T(8,128)S(1)}, u32[]{:S(2)}, u32[]{:S(2)}) async-start(f32[16,2,16,128]{3,2,1,0:T(8,128)} %get-tuple-element.19), calls=%async_computation.2 | async-start | bytes 524288 | tf_op jit(solution)/shard_map/all_to_all | solution.py:520
  102.1 0.1 fusion
  102.2 0.1 pad_maximum_fusion.3.cw_ref
  102.3 8.6 %all-to-all-done.2.c1_ref = f32[16,2,16,128]{3,2,1,0:T(8,128)S(1)} async-done(((f32[16,2,16,128]{3,2,1,0:T(8,128)}), f32[16,2,16,128]{3,2,1,0:T(8,128)S(1)}, u32[]{:S(2)}, u32[]{:S(2)}) %all-to-all-start.2) | async-done | bytes 262176 | tf_op jit(solution)/shard_map/all_to_all | solution.py:520
  110.8 1.2 shard_map.151
  112.0 12.1 %all_to_all.40.c2_ref = f32[16,32,128]{2,1,0:T(8,128)S(1)} all-to-all(f32[16,32,128]{2,1,0:T(8,128)S(1)} %shard_map.151), channel_id=1, replica_groups=mesh['depth'=16,'res'=8] {'depth'}, dimensions={0} | all-to-all | bytes 524288 | tf_op jit(solution)/shard_map/all_to_all | solution.py:522
  124.2 0.0 copy-done.7
  124.2 0.0 copy-done.8
  124.2 2.2 shard_map.152
  126.4 3.9 %all-to-all-start.4 = ((bf16[8,16,32,128]{3,2,1,0:T(8,128)(2,1)}), bf16[8,16,32,128]{3,2,1,0:T(8,128)(2,1)S(1)}, u32[]{:S(2)}, u32[]{:S(2)}) async-start(bf16[8,16,32,128]{3,2,1,0:T(8,128)(2,1)} %get-tuple-element.20.own_ref), calls=%async_computation.4 | async-start | bytes 2097152 | tf_op jit(solution)/shard_map/all_to_all | solution.py:527
  130.3 0.0 copy-done.10
  130.3 0.1 copy.28
  130.4 1.1 maximum_maximum_fusion.w_ref
  131.6 13.3 %all-to-all-done.4.da_ref = bf16[8,16,32,128]{3,2,1,0:T(8,128)(2,1)S(1)} async-done(((bf16[8,16,32,128]{3,2,1,0:T(8,128)(2,1)}), bf16[8,16,32,128]{3,2,1,0:T(8,128)(2,1)S(1)}, u32[]{:S(2)}, u32[]{:S(2)}) %all-to-all-start.4) | async-done | bytes 1048608 | tf_op jit(solution)/shard_map/all_to_all | solution.py:527
  144.8 26.2 %shard_map.153 = (f32[16,32,64]{2,1,0:T(8,128)S(1)}, f32[16,32,64]{2,1,0:T(8,128)S(1)}, f32[16,16,128]{2,1,0:T(8,128)S(1)}) custom-call(bf16[8,16,32,128]{3,2,1,0:T(8,128)(2,1)S(1)} %all-to-all-done.4.da_ref, bf16[8,16,32,128]{3,2,1,0:T(8,128)(2,1)} %get-tuple-element.20.own_ref, bf16[16,2,32,16,128]{4,3,2,1,0:T(8,128)(2,1)} %bitcast.21, ...), custom_call_target="tpu_custom_call" | custom-call | tf_op jit(solution)/shard_map/pallas_call | solution.py:531
  171.1 12.2 %all_to_all.41.e1_ref = f32[16,16,128]{2,1,0:T(8,128)S(1)} all-to-all(f32[16,16,128]{2,1,0:T(8,128)S(1)} %get-tuple-element.22), channel_id=1, replica_groups=mesh['depth'=16,'res'=8] {'depth'}, dimensions={0} | all-to-all | bytes 262144 | tf_op jit(solution)/shard_map/all_to_all | solution.py:557
  183.2 20.7 %shard_map.154 = (f32[16,32,64]{2,1,0:T(8,128)S(1)}, f32[16,32,64]{2,1,0:T(8,128)S(1)}, f32[8,16,16,128]{3,2,1,0:T(8,128)}, f32[16,16,256]{2,1,0:T(8,128)S(1)}) custom-call(f32[16,16,128]{2,1,0:T(8,128)S(1)} %all_to_all.41.e1_ref, f32[16,32,128]{2,1,0:T(8,128)S(1)} %all_to_all.40.c2_ref, f32[16,32,64]{2,1,0:T(8,128)S(1)} %get-tuple-element.18.m1_ref, ...), custom_call_target="tpu_custom_call" | custom-call | tf_op jit(solution)/shard_map/pallas_call | solution.py:559
  203.9 11.9 %all_to_all.42.b_ref = f32[16,16,256]{2,1,0:T(8,128)S(1)} all-to-all(f32[16,16,256]{2,1,0:T(8,128)S(1)} %get-tuple-element.33), channel_id=1, replica_groups=mesh['depth'=16,'res'=8] {'depth'}, dimensions={0} | all-to-all | bytes 524288 | tf_op jit(solution)/shard_map/all_to_all | solution.py:584
  215.8 3.6 %all-to-all-start.6 = ((f32[8,16,16,128]{3,2,1,0:T(8,128)}), f32[8,16,16,128]{3,2,1,0:T(8,128)S(1)}, u32[]{:S(2)}, u32[]{:S(2)}) async-start(f32[8,16,16,128]{3,2,1,0:T(8,128)} %get-tuple-element.30), calls=%async_computation.6 | async-start | bytes 2097152 | tf_op jit(solution)/shard_map/all_to_all | solution.py:583
  219.4 0.0 copy-done
  219.4 0.0 copy-done.4
  219.4 1.6 shard_map.156
  221.0 13.1 %all-to-all-done.6.f_ref = f32[8,16,16,128]{3,2,1,0:T(8,128)S(1)} async-done(((f32[8,16,16,128]{3,2,1,0:T(8,128)}), f32[8,16,16,128]{3,2,1,0:T(8,128)S(1)}, u32[]{:S(2)}, u32[]{:S(2)}) %all-to-all-start.6) | async-done | bytes 1048608 | tf_op jit(solution)/shard_map/all_to_all | solution.py:583
  234.1 1.1 shard_map.155
  (9 shorter events, 0.0 us)
Async XLA Ops:
  7.2 30.9 %copy-start.11 = (bf16[16,32,64]{2,1,0:T(8,128)(2,1)S(1)}, bf16[16,32,64]{2,1,0:T(8,128)(2,1)}, u32[]{:S(2)}) copy-start(bf16[16,32,64]{2,1,0:T(8,128)(2,1)} %param.26) | copy-start | bytes 196612
  7.2 30.9 %copy-start.12 = (bf16[16,32,64]{2,1,0:T(8,128)(2,1)S(1)}, bf16[16,32,64]{2,1,0:T(8,128)(2,1)}, u32[]{:S(2)}) copy-start(bf16[16,32,64]{2,1,0:T(8,128)(2,1)} %param.14) | copy-start | bytes 196612
  7.2 137.7 %all-gather.3.cloned.1.call-start = ((), (), s32[]{:S(2)}) async-start(), calls=%async_computation.8 | async-start | bytes 4456448 | tf_op jit(solution)/shard_map/all_gather | solution.py:491
  8.2 0.7 collective-permute-start
  11.4 0.9 copy-start.3
  14.1 33.7 %all-to-all-start.1 = ((f32[16,16,256]{2,1,0:T(8,128)}), f32[16,16,256]{2,1,0:T(8,128)S(1)}, u32[]{:S(2)}, u32[]{:S(2)}) async-start(f32[16,16,256]{2,1,0:T(8,128)} %shard_map.149), calls=%async_computation.1 | async-start | bytes 524288 | tf_op jit(solution)/shard_map/all_to_all | solution.py:498
  36.5 16.1 %copy-start.13 = (bf16[64,144]{1,0:T(8,128)(2,1)S(1)}, bf16[64,144]{1,0:T(8,128)(2,1)}, u32[]{:S(2)}) copy-start(bf16[64,144]{1,0:T(8,128)(2,1)} %param.22) | copy-start | bytes 55300
  38.1 33.0 %copy-start.5 = (bf16[64,256]{1,0:T(8,128)(2,1)S(1)}, bf16[64,256]{1,0:T(8,128)(2,1)}, u32[]{:S(2)}) copy-start(bf16[64,256]{1,0:T(8,128)(2,1)} %win_ref.3) | copy-start | bytes 98308
  38.1 33.0 %copy-start.6 = (bf16[64,64]{1,0:T(8,128)(2,1)S(1)}, bf16[64,64]{1,0:T(8,128)(2,1)}, u32[]{:S(2)}) copy-start(bf16[64,64]{1,0:T(8,128)(2,1)} %wo_ref.3) | copy-start | bytes 24580
  49.0 21.0 %all-to-all-start = ((bf16[8,16,32,128]{3,2,1,0:T(8,128)(2,1)}), bf16[8,16,32,128]{3,2,1,0:T(8,128)(2,1)S(1)}, u32[]{:S(2)}, u32[]{:S(2)}) async-start(bf16[8,16,32,128]{3,2,1,0:T(8,128)(2,1)} %broadcast_in_dim.5), calls=%async_computation | async-start | bytes 2097152 | tf_op jit(solution)/shard_map/all_to_all | solution.py:493
  52.6 71.6 %copy-start.7 = (bf16[64,64]{1,0:T(8,128)(2,1)S(1)}, bf16[64,64]{1,0:T(8,128)(2,1)}, u32[]{:S(2)}) copy-start(bf16[64,64]{1,0:T(8,128)(2,1)} %wv_ref.3) | copy-start | bytes 24580
  52.6 71.6 %copy-start.8 = (bf16[64,64]{1,0:T(8,128)(2,1)S(1)}, bf16[64,64]{1,0:T(8,128)(2,1)}, u32[]{:S(2)}) copy-start(bf16[64,64]{1,0:T(8,128)(2,1)} %wt_ref.3) | copy-start | bytes 24580
  70.0 1.0 copy-start.9
  93.2 1.0 copy-start.1
  94.2 1.0 copy-start.2
  95.2 15.6 %all-to-all-start.2 = ((f32[16,2,16,128]{3,2,1,0:T(8,128)}), f32[16,2,16,128]{3,2,1,0:T(8,128)S(1)}, u32[]{:S(2)}, u32[]{:S(2)}) async-start(f32[16,2,16,128]{3,2,1,0:T(8,128)} %get-tuple-element.19), calls=%async_computation.2 | async-start | bytes 524288 | tf_op jit(solution)/shard_map/all_to_all | solution.py:520
  102.1 28.2 %copy-start.10 = (bf16[1024,128]{1,0:T(8,128)(2,1)S(1)}, bf16[1024,128]{1,0:T(8,128)(2,1)}, u32[]{:S(2)}) copy-start(bf16[1024,128]{1,0:T(8,128)(2,1)} %param.25) | copy-start | bytes 786436
  126.4 18.5 %all-to-all-start.4 = ((bf16[8,16,32,128]{3,2,1,0:T(8,128)(2,1)}), bf16[8,16,32,128]{3,2,1,0:T(8,128)(2,1)S(1)}, u32[]{:S(2)}, u32[]{:S(2)}) async-start(bf16[8,16,32,128]{3,2,1,0:T(8,128)(2,1)} %get-tuple-element.20.own_ref), calls=%async_computation.4 | async-start | bytes 2097152 | tf_op jit(solution)/shard_map/all_to_all | solution.py:527
  203.9 15.5 %copy-start = (bf16[32,16,128]{2,1,0:T(8,128)(2,1)S(1)}, bf16[32,16,128]{2,1,0:T(8,128)(2,1)}, u32[]{:S(2)}) copy-start(bf16[32,16,128]{2,1,0:T(8,128)(2,1)} %ct_ref.1) | copy-start | bytes 393220
  203.9 15.5 %copy-start.4 = (bf16[32,16,128]{2,1,0:T(8,128)(2,1)S(1)}, bf16[32,16,128]{2,1,0:T(8,128)(2,1)}, u32[]{:S(2)}) copy-start(bf16[32,16,128]{2,1,0:T(8,128)(2,1)} %pair_ref.3) | copy-start | bytes 393220
  215.8 18.3 %all-to-all-start.6 = ((f32[8,16,16,128]{3,2,1,0:T(8,128)}), f32[8,16,16,128]{3,2,1,0:T(8,128)S(1)}, u32[]{:S(2)}, u32[]{:S(2)}) async-start(f32[8,16,16,128]{3,2,1,0:T(8,128)} %get-tuple-element.30), calls=%async_computation.6 | async-start | bytes 2097152 | tf_op jit(solution)/shard_map/all_to_all | solution.py:583
Sparse Core Ops, SparseCore 0:
  11.1 72.5 all-gather.2

commit v2 on v1

--- a/solution.py
+++ b/solution.py
@@ -13,6 +13,8 @@
 NN = (((1,), (0,)), ((), ()))
 NT = (((1,), (1,)), ((), ()))
 TN = (((0,), (0,)), ((), ()))
+GROUP = 4
+OWN_STEP = 8
 VMEM = pltpu.CompilerParams(vmem_limit_bytes=50 * 1024 * 1024)
 
 
@@ -111,46 +113,47 @@
         wo = wo_ref[...].astype(f32)
         wo2[...] = cat([wo, wo], 0).astype(bf16)
 
-    g = g_ref[...].reshape(256, 128).astype(f32)
-    live = g[:, 64:65]
-    xn, _ = norm_rows(g[:, :64])
-    x2 = pair2(xn)
-    x2_ref[0] = x2
-    kk = mm(x2, wkk[...])
-    khi = kk.astype(bf16)
-    lane = lax.broadcasted_iota(jnp.int32, (256, 128), 1)
-    k2 = jnp.where(lane < 64, kk, kk - khi.astype(f32)).astype(bf16)
-    vt = mm(wvt2[...], x2, NT)
-
-    own = own_ref[0].astype(f32)
-    xo = own[:, :64]
-    xon, _ = norm_rows(xo)
-    x2o = pair2(xon)
-    x2o_ref[0] = x2o
-    qg = mm(wqg[...], cat([x2o] * 8, 0), NT)
-    heads = head_mask(64, 256, 8, 32)
-    q = qg[:64] * (heads * SCALE)
-    gate = jax.nn.sigmoid(qg[64:])
-    qhi, qlo = split(q)
-    logits = mm(k2, cat([qhi, qhi], 0)) + mm(khi[:, :64], qlo)
-    logits = logits + bias_ref[...].reshape(256, 256)
-    logits = jnp.where(live > 0, logits, NEG)
-    e = jnp.exp(logits - jnp.max(logits, 0, keepdims=True))
-    p = e * (1.0 / jnp.sum(e, 0, keepdims=True))
-    p_ref[0] = p
-    any_ref[0] = jnp.broadcast_to(jnp.max(live, 0, keepdims=True), (8, 256))
-    phi, plo = split(p)
-    vhi, vlo = split(vt)
-    first = mm(cat([vhi, vlo], 0), phi)
-    o = (first[:64] + first[64:] + mm(vhi, plo)) * heads
-    o_ref[0] = o
-    ahi, alo = split(o * gate)
-    y = mm(cat([ahi, alo], 0), wo2[...], TN)
-    m1 = xo + jnp.sum(y.reshape(8, 32, 64), 0)
-    m1_ref[0] = m1
-    c1_ref[:, 0, s, :] = cat([m1[:16], m1[16:]], 1)
-    lv = own[:, 64:]
-    c1_ref[:, 1, s, :] = cat([lv[:16], lv[16:]], 1)
+    for u in range(GROUP):
+        g = g_ref[:, u].reshape(256, 128).astype(f32)
+        live = g[:, 64:65]
+        xn, _ = norm_rows(g[:, :64])
+        x2 = pair2(xn)
+        x2_ref[u] = x2
+        kk = mm(x2, wkk[...])
+        khi = kk.astype(bf16)
+        lane = lax.broadcasted_iota(jnp.int32, (256, 128), 1)
+        k2 = jnp.where(lane < 64, kk, kk - khi.astype(f32)).astype(bf16)
+        vt = mm(wvt2[...], x2, NT)
+
+        own = own_ref[u].astype(f32)
+        xo = own[:, :64]
+        xon, _ = norm_rows(xo)
+        x2o = pair2(xon)
+        x2o_ref[u] = x2o
+        qg = mm(wqg[...], cat([x2o] * 8, 0), NT)
+        heads = head_mask(64, 256, 8, 32)
+        q = qg[:64] * (heads * SCALE)
+        gate = jax.nn.sigmoid(qg[64:])
+        qhi, qlo = split(q)
+        logits = mm(k2, cat([qhi, qhi], 0)) + mm(khi[:, :64], qlo)
+        logits = logits + bias_ref[...].reshape(256, 256)
+        logits = jnp.where(live > 0, logits, NEG)
+        e = jnp.exp(logits - jnp.max(logits, 0, keepdims=True))
+        p = e * (1.0 / jnp.sum(e, 0, keepdims=True))
+        p_ref[u] = p
+        any_ref[u] = jnp.broadcast_to(jnp.max(live, 0, keepdims=True), (8, 256))
+        phi, plo = split(p)
+        vhi, vlo = split(vt)
+        first = mm(cat([vhi, vlo], 0), phi)
+        o = (first[:64] + first[64:] + mm(vhi, plo)) * heads
+        o_ref[u] = o
+        ahi, alo = split(o * gate)
+        y = mm(cat([ahi, alo], 0), wo2[...], TN)
+        m1 = xo + jnp.sum(y.reshape(8, 32, 64), 0)
+        m1_ref[u] = m1
+        c1_ref[:, 0, s * GROUP + u, :] = cat([m1[:16], m1[16:]], 1)
+        lv = own[:, 64:]
+        c1_ref[:, 1, s * GROUP + u, :] = cat([lv[:16], lv[16:]], 1)
 
 
 def diag2(w):
@@ -237,8 +240,6 @@
     inv, turned, stage, res, lrs,
 ):
     step = pl.program_id(0)
-    steps = 8
-    per = 4
 
     @pl.when(step == 0)
     def _():
@@ -261,30 +262,26 @@
             turned[1, :, 128 * half:128 * half + 128] = lrs[half, 0:512].astype(bf16)
 
     for side in range(2):
-        for k in range(per):
-            one = step * per + k
+        for k in range(OWN_STEP):
+            one = step * OWN_STEP + k
             if side == 0:
                 ct = cta_ref[:, 0, k].reshape(256, 128)
             else:
                 ct = ctb_ref[:, 0, 0, k].reshape(256, 128)
             hi, lo = split(ct.astype(f32) * inv[one])
             both = mm(turned[side], cat([hi, lo], 1))
-            u = both[:, :128] + both[:, 128:]
-            uhi, ulo = split(u)
-            stage[side, :, pl.ds(pl.multiple_of(one * 16, 16), 16), 0:128] = uhi.reshape(32, 16, 128)
-            stage[side, :, pl.ds(pl.multiple_of(one * 16, 16), 16), 128:256] = ulo.reshape(32, 16, 128)
-
-    @pl.when(step == steps - 1)
+            uhi, ulo = split(both[:, :128] + both[:, 128:])
+            at = pl.ds(pl.multiple_of(one * 16, 16), 16)
+            for b in range(32):
+                stage[side, at, 256 * b:256 * b + 128] = uhi[16 * b:16 * b + 16]
+                stage[side, at, 256 * b + 128:256 * b + 256] = ulo[16 * b:16 * b + 16]
+
+    @pl.when(step == 32 // OWN_STEP - 1)
     def _():
         grads = []
         for side in range(2):
-            def body(b, acc):
-                return acc + mm(stage[side, b], w_ref[side, b], NT)
-
-            acc = lax.fori_loop(0, 32, body, jnp.zeros((512, 32), f32))
-            res[:, 0:32] = acc
+            res[:, 0:32] = mm(stage[side], w_ref[side], NT)
             grads.append(cat([res[pl.ds(s, 32, stride=16), :] for s in range(16)], 0)[:, 0:32])
-        live = own_ref[...].reshape(512, 128)
         lv = adj_ref[...].reshape(512, 128)[:, 64:].astype(f32)
         dlr = cat(grads, 1) * lv
         m2 = m2_ref[...].reshape(512, 64)
@@ -361,45 +358,46 @@
         g1s[...] = g1.reshape(16, 32, 64)
         bias_ref[...] = jnp.zeros_like(bias_ref)
 
-    dm = g1s[s]
-    g1_ref[0] = dm
-    heads = head_mask(64, 256, 8, 32)
-    p = p_ref[0]
-    o = o_ref[0]
-    x2 = x2_ref[0]
-    x2o = x2o_ref[0]
-    vv = mm(x2, wvv[...])
-    vhi = vv.astype(bf16)
-    lane = lax.broadcasted_iota(jnp.int32, (256, 128), 1)
-    v2 = jnp.where(lane < 64, vv, vv - vhi.astype(f32)).astype(bf16)
-    khi, klo = split(mm(wkt2[...], x2, NT))
-    qg = mm(wqg[...], cat([x2o] * 8, 0), NT)
-    q = qg[:64] * (heads * SCALE)
-    gate = jax.nn.sigmoid(qg[64:])
-    dout = mm(wo2[...], cat([pair2(dm)] * 8, 0), NT)
-    dgate = dout * o * gate * (1.0 - gate)
-    do = dout * gate * heads
-    do_live = do * any_ref[0, 0:1, :]
-    delta = jnp.sum(do_live * o, 0, keepdims=True)
-    lhi, llo = split(do_live)
-    dp = mm(v2, cat([lhi, lhi], 0)) + mm(vhi[:, :64], llo)
-    ds = p * (dp - delta)
-    bias_ref[...] += ds.reshape(16, 16, 256)
-    shi, slo = split(ds)
-    first = mm(cat([khi, klo], 0), shi)
-    dq = (first[:64] + first[64:] + mm(khi, slo)) * (heads * SCALE)
-    qhi, qlo = split(q)
-    zero = jnp.zeros((64, 256), bf16)
-    dk = mm(shi, cat([qhi, qlo], 0), NT) + mm(slo, cat([qhi, zero], 0), NT)
-    phi, plo = split(p)
-    dhi, dlo = split(do)
-    dv = mm(phi, cat([dhi, dlo], 0), NT) + mm(plo, cat([dhi, zero], 0), NT)
-    kv = cat([dk, dv], 1)
-    dx = mm2(kv, wback[...]).reshape(8, 32, 64)
-    f_ref[:, 0] = cat([dx[:, :16], dx[:, 16:]], 2)
-    qhi2, qlo2 = split(cat([dq, dgate], 0))
-    dxo = mm(cat([qhi2, qlo2], 0), wown[...], TN)
-    dxo_ref[0] = jnp.sum(dxo.reshape(8, 32, 64), 0)
+    for u in range(GROUP):
+        dm = g1s[s * GROUP + u]
+        g1_ref[u] = dm
+        heads = head_mask(64, 256, 8, 32)
+        p = p_ref[u]
+        o = o_ref[u]
+        x2 = x2_ref[u]
+        x2o = x2o_ref[u]
+        vv = mm(x2, wvv[...])
+        vhi = vv.astype(bf16)
+        lane = lax.broadcasted_iota(jnp.int32, (256, 128), 1)
+        v2 = jnp.where(lane < 64, vv, vv - vhi.astype(f32)).astype(bf16)
+        khi, klo = split(mm(wkt2[...], x2, NT))
+        qg = mm(wqg[...], cat([x2o] * 8, 0), NT)
+        q = qg[:64] * (heads * SCALE)
+        gate = jax.nn.sigmoid(qg[64:])
+        dout = mm(wo2[...], cat([pair2(dm)] * 8, 0), NT)
+        dgate = dout * o * gate * (1.0 - gate)
+        do = dout * gate * heads
+        do_live = do * any_ref[u, 0:1, :]
+        delta = jnp.sum(do_live * o, 0, keepdims=True)
+        lhi, llo = split(do_live)
+        dp = mm(v2, cat([lhi, lhi], 0)) + mm(vhi[:, :64], llo)
+        ds = p * (dp - delta)
+        bias_ref[...] += ds.reshape(16, 16, 256)
+        shi, slo = split(ds)
+        first = mm(cat([khi, klo], 0), shi)
+        dq = (first[:64] + first[64:] + mm(khi, slo)) * (heads * SCALE)
+        qhi, qlo = split(q)
+        zero = jnp.zeros((64, 256), bf16)
+        dk = mm(shi, cat([qhi, qlo], 0), NT) + mm(slo, cat([qhi, zero], 0), NT)
+        phi, plo = split(p)
+        dhi, dlo = split(do)
+        dv = mm(phi, cat([dhi, dlo], 0), NT) + mm(plo, cat([dhi, zero], 0), NT)
+        kv = cat([dk, dv], 1)
+        dx = mm2(kv, wback[...]).reshape(8, 32, 64)
+        f_ref[:, u] = cat([dx[:, :16], dx[:, 16:]], 2)
+        qhi2, qlo2 = split(cat([dq, dgate], 0))
+        dxo = mm(cat([qhi2, qlo2], 0), wown[...], TN)
+        dxo_ref[u] = jnp.sum(dxo.reshape(8, 32, 64), 0)
 
 
 def final_rows_kernel(f_ref, dxo_ref, g1_ref, own_ref, out_ref):
@@ -437,13 +435,95 @@
 
 def row(shape):
     rest = (0,) * (len(shape) - 1)
-    return pl.BlockSpec((1,) + shape[1:], lambda s: (s,) + rest)
+    return pl.BlockSpec((GROUP,) + shape[1:], lambda s: (s,) + rest)
 
 
 def whole_call(kernel, out_shape, *args, scratch=()):
     return pl.pallas_call(
         kernel, out_shape=out_shape, scratch_shapes=list(scratch), compiler_params=VMEM
     )(*args)
+
+
+def row_forward(rows, own, bias, win, wo):
+    grow = pl.BlockSpec((8, GROUP, 32, 128), lambda s: (0, s, 0, 0))
+    return pl.pallas_call(
+        row_fwd_kernel,
+        grid=(16 // GROUP,),
+        in_specs=[grow, row((16, 32, 128)), full((16, 16, 256)), full((64, 256)), full((64, 64))],
+        out_specs=[
+            row((16, 256, 256)), row((16, 64, 256)), row((16, 256, 128)), row((16, 32, 128)),
+            row((16, 32, 64)), row((16, 8, 256)), full((16, 2, 16, 128)),
+        ],
+        out_shape=[
+            sds((16, 256, 256)), sds((16, 64, 256)), sds((16, 256, 128), bf16),
+            sds((16, 32, 128), bf16), sds((16, 32, 64)), sds((16, 8, 256)), sds((16, 2, 16, 128)),
+        ],
+        scratch_shapes=[
+            pltpu.VMEM((128, 128), bf16), pltpu.VMEM((64, 128), bf16),
+            pltpu.VMEM((128, 128), bf16), pltpu.VMEM((128, 64), bf16),
+        ],
+        compiler_params=VMEM,
+    )(rows, own, bias, win, wo)
+
+
+def outer_product(ct, factors, dblock, wouter, m2, c2, m1, adj, cw, wvo, wtf):
+    cta = ct.reshape(16, 2, 32, 16, 128)
+    ctb = ct.reshape(8, 2, 2, 16, 32, 128)
+    return pl.pallas_call(
+        outer_kernel,
+        grid=(32 // OWN_STEP,),
+        in_specs=[
+            full((8, 16, 32, 128)),
+            pl.BlockSpec((1, 16, 32, 128), lambda s: (0, 0, 0, 0)),
+            pl.BlockSpec((16, 1, OWN_STEP, 16, 128), lambda s: (0, 0, s, 0, 0)),
+            pl.BlockSpec(
+                (8, 1, 1, OWN_STEP, 32, 128),
+                lambda s: (0, s // (16 // OWN_STEP), 1, s % (16 // OWN_STEP), 0, 0),
+            ),
+            full((2, 32, 8192)),
+            full((16, 32, 64)), full((16, 32, 128)), full((16, 32, 64)), full((16, 32, 128)),
+            full((64, 256)), full((64, 64)), full((64, 64)),
+        ],
+        out_specs=[full((16, 32, 64)), full((16, 32, 64)), full((16, 16, 128))],
+        out_shape=[sds((16, 32, 64)), sds((16, 32, 64)), sds((16, 16, 128))],
+        scratch_shapes=[
+            pltpu.VMEM((32, 256, 128), f32),
+            pltpu.VMEM((2, 512, 256), bf16),
+            pltpu.VMEM((2, 512, 8192), bf16),
+            pltpu.VMEM((512, 128), f32),
+            pltpu.VMEM((2, 1024, 128), f32),
+        ],
+        compiler_params=VMEM,
+    )(
+        factors, dblock, cta, ctb, wouter, m2, c2, m1, adj, cw, wvo, wtf,
+    )
+
+
+def row_backward(e1, c2, m1, own, g2, dcg, cw, p, o, x2, x2o, any_live, win, wo):
+    return pl.pallas_call(
+        row_bwd_kernel,
+        grid=(16 // GROUP,),
+        in_specs=[
+            full((16, 16, 128)), full((16, 32, 128)), full((16, 32, 64)), full((16, 32, 128)),
+            full((16, 32, 64)), full((16, 32, 64)), full((64, 256)),
+            row((16, 256, 256)), row((16, 64, 256)), row((16, 256, 128)), row((16, 32, 128)),
+            row((16, 8, 256)), full((64, 256)), full((64, 64)),
+        ],
+        out_specs=[
+            row((16, 32, 64)), row((16, 32, 64)),
+            pl.BlockSpec((8, GROUP, 16, 128), lambda s: (0, s, 0, 0)), full((16, 16, 256)),
+        ],
+        out_shape=[sds((16, 32, 64)), sds((16, 32, 64)), sds((8, 16, 16, 128)), sds((16, 16, 256))],
+        scratch_shapes=[
+            pltpu.VMEM((16, 32, 64), f32),
+            pltpu.VMEM((128, 128), bf16), pltpu.VMEM((64, 128), bf16), pltpu.VMEM((128, 128), bf16),
+            pltpu.VMEM((64, 128), bf16), pltpu.VMEM((256, 64), bf16), pltpu.VMEM((256, 64), bf16),
+        ],
+        compiler_params=VMEM,
+    )(
+        e1, c2, m1, own, g2, dcg, cw, p, o, x2, x2o, any_live,
+        win, wo,
+    )
 
 
 def body(
@@ -481,41 +561,26 @@
         1,
     )
     w3 = outer_output_weights.reshape(32, 32, 128)
-    wouter = jnp.stack([w3.transpose(1, 0, 2), w3], 0)
-    wouter = cat([wouter, wouter], 3)
+    wouter = jnp.stack([w3, w3.transpose(1, 0, 2)], 0)
+    wouter = cat([wouter, wouter], 3).reshape(2, 32, 8192)
 
     turned = pairwise_cotangent.transpose(1, 0, 2)
     perm = [(d * 8 + r, (2 * r + d % 2) * 8 + d // 2) for d in range(16) for r in range(8)]
     turned = lax.ppermute(turned, ("depth", "res"), perm)
     both = cat([pairwise_cotangent.reshape(512, 128), turned.reshape(512, 128)], 0)
-    ct = lax.all_gather(both, "depth", axis=0, tiled=False)
 
     rows = lax.all_to_all(jnp.broadcast_to(own[None], (8, 16, 32, 128)), "res", 0, 0)
     bias_block = whole_call(
         bias_kernel, sds((16, 16, 256)), pairwise_state, pairwise_bias_weights,
         scratch=[pltpu.VMEM((32, 16, 128), f32)],
     )
+    bias_block, rows, both = lax.optimization_barrier((bias_block, rows, both))
+    ct = lax.all_gather(both, "depth", axis=0, tiled=False)
     bias = lax.all_to_all(bias_block, "depth", 0, 0)
 
-    grow = pl.BlockSpec((8, 1, 32, 128), lambda s: (0, s, 0, 0))
-    p, o, x2, x2o, m1, any_live, c1 = pl.pallas_call(
-        row_fwd_kernel,
-        grid=(16,),
-        in_specs=[grow, row((16, 32, 128)), full((16, 16, 256)), full((64, 256)), full((64, 64))],
-        out_specs=[
-            row((16, 256, 256)), row((16, 64, 256)), row((16, 256, 128)), row((16, 32, 128)),
-            row((16, 32, 64)), row((16, 8, 256)), full((16, 2, 16, 128)),
-        ],
-        out_shape=[
-            sds((16, 256, 256)), sds((16, 64, 256)), sds((16, 256, 128), bf16),
-            sds((16, 32, 128), bf16), sds((16, 32, 64)), sds((16, 8, 256)), sds((16, 2, 16, 128)),
-        ],
-        scratch_shapes=[
-            pltpu.VMEM((128, 128), bf16), pltpu.VMEM((64, 128), bf16),
-            pltpu.VMEM((128, 128), bf16), pltpu.VMEM((128, 64), bf16),
-        ],
-        compiler_params=VMEM,
-    )(rows, own, bias, horizontal_intake_coefs, horizontal_readout_coefs)
+    p, o, x2, x2o, m1, any_live, c1 = row_forward(
+        rows, own, bias, horizontal_intake_coefs, horizontal_readout_coefs
+    )
 
     c1 = lax.all_to_all(c1, "depth", 0, 0)
     c2 = whole_call(col_kernel, sds((16, 32, 128)), c1, cw)
@@ -526,57 +591,13 @@
     )
     factors = lax.all_to_all(dblock, "res", 0, 0)
 
-    cta = ct.reshape(16, 2, 32, 16, 128)
-    ctb = ct.reshape(8, 2, 2, 16, 32, 128)
-    g2, dcg, e1 = pl.pallas_call(
-        outer_kernel,
-        grid=(8,),
-        in_specs=[
-            full((8, 16, 32, 128)),
-            pl.BlockSpec((1, 16, 32, 128), lambda s: (0, 0, 0, 0)),
-            pl.BlockSpec((16, 1, 4, 16, 128), lambda s: (0, 0, s, 0, 0)),
-            pl.BlockSpec((8, 1, 1, 4, 32, 128), lambda s: (0, s // 4, 1, s % 4, 0, 0)),
-            full((2, 32, 32, 256)),
-            full((16, 32, 64)), full((16, 32, 128)), full((16, 32, 64)), full((16, 32, 128)),
-            full((64, 256)), full((64, 64)), full((64, 64)),
-        ],
-        out_specs=[full((16, 32, 64)), full((16, 32, 64)), full((16, 16, 128))],
-        out_shape=[sds((16, 32, 64)), sds((16, 32, 64)), sds((16, 16, 128))],
-        scratch_shapes=[
-            pltpu.VMEM((32, 256, 128), f32),
-            pltpu.VMEM((2, 512, 256), bf16),
-            pltpu.VMEM((2, 32, 512, 256), bf16),
-            pltpu.VMEM((512, 128), f32),
-            pltpu.VMEM((2, 1024, 128), f32),
-        ],
-        compiler_params=VMEM,
-    )(
-        factors, dblock, cta, ctb, wouter, m2, c2, m1, adj, cw, vertical_readout_coefs,
+    g2, dcg, e1 = outer_product(
+        ct, factors, dblock, wouter, m2, c2, m1, adj, cw, vertical_readout_coefs,
         tensor_factor_coefs,
     )
     e1 = lax.all_to_all(e1, "depth", 0, 0)
 
-    g1, dxo, fblock, bblock = pl.pallas_call(
-        row_bwd_kernel,
-        grid=(16,),
-        in_specs=[
-            full((16, 16, 128)), full((16, 32, 128)), full((16, 32, 64)), full((16, 32, 128)),
-            full((16, 32, 64)), full((16, 32, 64)), full((64, 256)),
-            row((16, 256, 256)), row((16, 64, 256)), row((16, 256, 128)), row((16, 32, 128)),
-            row((16, 8, 256)), full((64, 256)), full((64, 64)),
-        ],
-        out_specs=[
-            row((16, 32, 64)), row((16, 32, 64)),
-            pl.BlockSpec((8, 1, 16, 128), lambda s: (0, s, 0, 0)), full((16, 16, 256)),
-        ],
-        out_shape=[sds((16, 32, 64)), sds((16, 32, 64)), sds((8, 16, 16, 128)), sds((16, 16, 256))],
-        scratch_shapes=[
-            pltpu.VMEM((16, 32, 64), f32),
-            pltpu.VMEM((128, 128), bf16), pltpu.VMEM((64, 128), bf16), pltpu.VMEM((128, 128), bf16),
-            pltpu.VMEM((64, 128), bf16), pltpu.VMEM((256, 64), bf16), pltpu.VMEM((256, 64), bf16),
-        ],
-        compiler_params=VMEM,
-    )(
+    g1, dxo, fblock, bblock = row_backward(
         e1, c2, m1, own, g2, dcg, cw, p, o, x2, x2o, any_live,
         horizontal_intake_coefs, horizontal_readout_coefs,
     )

time: 243 us -> 209 us (0.86)
  Pallas kernels: 77 us -> 58.5 us
  starting transfers between devices: 41 us -> 32 us
  waiting for transfers between devices: 61.5 us -> 56.3 us
    pallas_call x3, Pallas kernels: 69 us -> 50.5 us  [the longest x1 18.6 us: row_backward(): pl.pallas_call(row_bwd_kernel, grid=(16 // GROUP,), in_specs=[full((16, 1...]
    all_to_all x1, starting transfers between devices: 22.4 us -> 9.77 us  [body(): bias = lax.all_to_all(bias_block, 'depth', 0, 0)]
    all_to_all x1, waiting for transfers between devices: 17 us -> 12.4 us  [body(): lax.all_to_all(jnp.broadcast_to(own[None], (8, 16, 32, 128)), 'res', 0, 0)]
    all_to_all x1, starting transfers between devices: 3.94 us -> 7.62 us  [body(): factors = lax.all_to_all(dblock, 'res', 0, 0)]
    unnamed x30 -> x26, local copies, waits for them, and re-layouts: 5.82 us -> 2.23 us
    all_to_all x1, waiting for transfers between devices: 8.55 us -> 11.5 us  [body(): c1 = lax.all_to_all(c1, 'depth', 0, 0)]
    all_to_all x1, starting transfers between devices: 6.84 us -> 4.31 us  [body(): c1 = lax.all_to_all(c1, 'depth', 0, 0)]
    all_to_all x1, starting transfers between devices: 3.56 us -> 6.08 us  [body(): lax.all_to_all(jnp.broadcast_to(own[None], (8, 16, 32, 128)), 'res', 0, 0)]
  transfers between devices with their start and end apart: 7 -> 7, of which waited for: 5 -> 5; matrix products, arithmetic and copies ran while one was open for 2% -> 2% of each run, Pallas kernels for 12% -> 11%
where the time goes in v2:
time: 209 us
  Pallas kernels  58.5 us (28%)
  waiting for transfers between devices  56.3 us (27%)
  blocking collectives  36.5 us (17%)
  starting transfers between devices  32 us (15%)
  between operations  14.9 us (7%)
  local copies, waits for them, and re-layouts  6.49 us (3%)
  other arithmetic  3.85 us (2%)
    pallas_call x1, Pallas kernels, row_backward(): pl.pallas_call(row_bwd_kernel, grid=(16 // GROUP,), in_specs=[full((16, 1...  18.6 us
    pallas_call x1, Pallas kernels, row_forward(): pl.pallas_call(row_fwd_kernel, grid=(16 // GROUP,), in_specs=[grow, row((...  16.7 us
    pallas_call x1, Pallas kernels, outer_product(): pl.pallas_call(outer_kernel, grid=(32 // OWN_STEP,), in_specs=[full((8, 1...  15.2 us
    all_to_all x1, waiting for transfers between devices, body(): fsum = lax.all_to_all(fblock, 'res', 0, 0)  13.1 us
    all_to_all x1, waiting for transfers between devices, body(): lax.all_to_all(jnp.broadcast_to(own[None], (8, 16, 32, 128)), 'res', 0, 0)  12.4 us
    all_to_all x1, blocking collectives, body(): c2 = lax.all_to_all(c2, 'depth', 0, 0)  12.4 us
    all_to_all x1, blocking collectives, body(): e1 = lax.all_to_all(e1, 'depth', 0, 0)  12.4 us
    all_to_all x1, blocking collectives, body(): bsum = lax.all_to_all(bblock, 'depth', 0, 0)  11.8 us
  transfers between devices with their start and end apart: 7, of which 5 were waited for; matrix products, arithmetic and copies ran while one was open for 2% of the time, Pallas kernels for 11%

profile of v2, /device:TPU:1, one launch (start us, length us, event | category | flops | bytes accessed | tf_op | source)
XLA Modules:
  0.0 208.6 jit_solution(12438314888361197150)
XLA Ops:
  7.2 0.0 copy-start
  7.9 0.8 multiply_convert_fusion
  8.6 0.1 broadcast_in_dim.4
  8.8 0.0 copy-start.11
  8.8 0.0 copy-start.3
  8.8 1.1 pad_maximum_fusion.1
  9.9 1.2 broadcast_in_dim.5
  11.1 0.0 copy-start.10
  11.1 0.0 copy-start.4
  11.1 0.0 copy-start.5
  11.1 6.1 %all-to-all-start = ((bf16[8,16,32,128]{3,2,1,0:T(8,128)(2,1)}), bf16[8,16,32,128]{3,2,1,0:T(8,128)(2,1)S(1)}, u32[]{:S(2)}, u32[]{:S(2)}) async-start(bf16[8,16,32,128]{3,2,1,0:T(8,128)(2,1)} %broadcast_in_dim.5), calls=%async_computation | async-start | bytes 2097152 | tf_op jit(solution)/shard_map/all_to_all | solution.py:572
  17.2 0.0 all-gather.3.cloned.1.call-start
  17.2 0.0 copy-done
  17.3 0.7 collective-permute-start
  18.0 0.0 copy-done.11
  18.0 0.1 copy.19.wb_ref
  18.1 0.0 copy-done.3
  18.1 1.8 shard_map.149
  19.9 0.0 collective-permute-done
  19.9 0.7 pad_maximum_fusion
  20.6 0.0 copy-start.6
  20.6 0.0 copy-start.7
  20.6 12.4 %all-to-all-done.g_ref = bf16[8,16,32,128]{3,2,1,0:T(8,128)(2,1)S(1)} async-done(((bf16[8,16,32,128]{3,2,1,0:T(8,128)(2,1)}), bf16[8,16,32,128]{3,2,1,0:T(8,128)(2,1)S(1)}, u32[]{:S(2)}, u32[]{:S(2)}) %all-to-all-start) | async-done | bytes 1048608 | tf_op jit(solution)/shard_map/all_to_all | solution.py:572
  33.1 0.0 copy-start.8
  33.1 0.0 all-gather.3.cloned.1.call-update
  33.1 0.0 copy-done.10
  33.1 0.1 fusion.1
  33.2 0.1 copy.22
  33.3 9.8 %all-to-all-start.1 = ((f32[16,16,256]{2,1,0:T(8,128)}), f32[16,16,256]{2,1,0:T(8,128)S(1)}, u32[]{:S(2)}, u32[]{:S(2)}) async-start(f32[16,16,256]{2,1,0:T(8,128)} %shard_map.149), calls=%async_computation.1 | async-start | bytes 524288 | tf_op jit(solution)/shard_map/all_to_all | solution.py:579
  43.0 0.1 copy.21
  43.1 0.1 copy.24
  43.2 0.1 copy.23
  43.3 8.4 %all-to-all-done.1.bias_ref = f32[16,16,256]{2,1,0:T(8,128)S(1)} async-done(((f32[16,16,256]{2,1,0:T(8,128)}), f32[16,16,256]{2,1,0:T(8,128)S(1)}, u32[]{:S(2)}, u32[]{:S(2)}) %all-to-all-start.1) | async-done | bytes 262176 | tf_op jit(solution)/shard_map/all_to_all | solution.py:579
  51.7 0.0 copy-done.8
  51.7 0.0 copy-done.4
  51.7 0.0 copy-done.5
  51.7 16.7 %shard_map.150 = (f32[16,256,256]{2,1,0:T(8,128)}, f32[16,64,256]{2,1,0:T(8,128)S(1)}, bf16[16,256,128]{2,1,0:T(8,128)(2,1)S(1)}, bf16[16,32,128]{2,1,0:T(8,128)...) custom-call(bf16[8,16,32,128]{3,2,1,0:T(8,128)(2,1)} %copy-done.8, ...), custom_call_target="tpu_custom_call" | custom-call | tf_op jit(solution)/shard_map/pallas_call | solution.py:449
  68.4 0.0 copy-start.1
  68.4 1.0 copy-done.1
  69.5 0.0 copy-start.2
  69.5 1.0 copy-done.2
  70.5 4.3 %all-to-all-start.2 = ((f32[16,2,16,128]{3,2,1,0:T(8,128)}), f32[16,2,16,128]{3,2,1,0:T(8,128)S(1)}, u32[]{:S(2)}, u32[]{:S(2)}) async-start(f32[16,2,16,128]{3,2,1,0:T(8,128)} %get-tuple-element.24), calls=%async_computation.2 | async-start | bytes 524288 | tf_op jit(solution)/shard_map/all_to_all | solution.py:585
  74.8 0.1 fusion
  74.9 0.1 pad_maximum_fusion.3.cw_ref
  75.0 11.5 %all-to-all-done.2.c1_ref = f32[16,2,16,128]{3,2,1,0:T(8,128)S(1)} async-done(((f32[16,2,16,128]{3,2,1,0:T(8,128)}), f32[16,2,16,128]{3,2,1,0:T(8,128)S(1)}, u32[]{:S(2)}, u32[]{:S(2)}) %all-to-all-start.2) | async-done | bytes 262176 | tf_op jit(solution)/shard_map/all_to_all | solution.py:585
  86.4 1.2 shard_map.151
  87.6 12.4 %all_to_all.40.c2_ref = f32[16,32,128]{2,1,0:T(8,128)S(1)} all-to-all(f32[16,32,128]{2,1,0:T(8,128)S(1)} %shard_map.151), channel_id=1, replica_groups=mesh['depth'=16,'res'=8] {'depth'}, dimensions={0} | all-to-all | bytes 524288 | tf_op jit(solution)/shard_map/all_to_all | solution.py:587
  100.0 0.0 copy-done.6
  100.0 0.0 copy-done.7
  100.0 2.2 %shard_map.152 = (f32[16,32,64]{2,1,0:T(8,128)S(1)}, bf16[8,16,32,128]{3,2,1,0:T(8,128)(2,1)}) custom-call(f32[16,32,64]{2,1,0:T(8,128)S(1)} %get-tuple-element.23.m1_ref, f32[16,32,128]{2,1,0:T(8,128)S(1)} %all_to_all.40.c2_ref, bf16[16,32,128]{2,1,0:T(8,128)(2,1)S(1)} %get-tuple-element.41.own_ref, bf16[64,256]{1,0:T(8,128)(2,1)S(1)} %pad_maximum_fusion.3.cw_ref, ...), custom_call_target="tpu_custom_call" | custom-call | tf_op jit(solution)/shard_map/pallas_call | solution.py:442
  102.2 7.6 %all-to-all-start.4 = ((bf16[8,16,32,128]{3,2,1,0:T(8,128)(2,1)}), bf16[8,16,32,128]{3,2,1,0:T(8,128)(2,1)S(1)}, u32[]{:S(2)}, u32[]{:S(2)}) async-start(bf16[8,16,32,128]{3,2,1,0:T(8,128)(2,1)} %get-tuple-element.25.own_ref), calls=%async_computation.4 | async-start | bytes 2097152 | tf_op jit(solution)/shard_map/all_to_all | solution.py:592
  109.8 0.0 copy-done.9
  109.8 0.1 copy.29
  110.0 1.1 maximum_maximum_fusion
  111.1 2.4 %reshape.43.w_ref = bf16[2,32,8192]{2,1,0:T(8,128)(2,1)} reshape(bf16[2,32,32,256]{3,2,1,0:T(8,128)(2,1)} %maximum_maximum_fusion) | data formatting | bytes 2097152 | tf_op jit(solution)/shard_map/reshape | solution.py:565
  113.5 10.9 %all-to-all-done.4.da_ref = bf16[8,16,32,128]{3,2,1,0:T(8,128)(2,1)S(1)} async-done(((bf16[8,16,32,128]{3,2,1,0:T(8,128)(2,1)}), bf16[8,16,32,128]{3,2,1,0:T(8,128)(2,1)S(1)}, u32[]{:S(2)}, u32[]{:S(2)}) %all-to-all-start.4) | async-done | bytes 1048608 | tf_op jit(solution)/shard_map/all_to_all | solution.py:592
  124.4 15.2 %shard_map.153 = (f32[16,32,64]{2,1,0:T(8,128)S(1)}, f32[16,32,64]{2,1,0:T(8,128)S(1)}, f32[16,16,128]{2,1,0:T(8,128)S(1)}) custom-call(bf16[8,16,32,128]{3,2,1,0:T(8,128)(2,1)S(1)} %all-to-all-done.4.da_ref, bf16[8,16,32,128]{3,2,1,0:T(8,128)(2,1)} %get-tuple-element.25.own_ref, bf16[16,2,32,16,128]{4,3,2,1,0:T(8,128)(2,1)} %bitcast.23, ...), custom_call_target="tpu_custom_call" | custom-call | tf_op jit(solution)/shard_map/pallas_call | solution.py:472
  139.6 12.4 %all_to_all.41.e1_ref = f32[16,16,128]{2,1,0:T(8,128)S(1)} all-to-all(f32[16,16,128]{2,1,0:T(8,128)S(1)} %get-tuple-element.28), channel_id=1, replica_groups=mesh['depth'=16,'res'=8] {'depth'}, dimensions={0} | all-to-all | bytes 262144 | tf_op jit(solution)/shard_map/all_to_all | solution.py:598
  152.0 18.6 %shard_map.154 = (f32[16,32,64]{2,1,0:T(8,128)S(1)}, f32[16,32,64]{2,1,0:T(8,128)S(1)}, f32[8,16,16,128]{3,2,1,0:T(8,128)}, f32[16,16,256]{2,1,0:T(8,128)S(1)}) custom-call(f32[16,16,128]{2,1,0:T(8,128)S(1)} %all_to_all.41.e1_ref, f32[16,32,128]{2,1,0:T(8,128)S(1)} %all_to_all.40.c2_ref, f32[16,32,64]{2,1,0:T(8,128)S(1)} %get-tuple-element.23.m1_ref, ...), custom_call_target="tpu_custom_call" | custom-call | tf_op jit(solution)/shard_map/pallas_call | solution.py:503
  170.5 11.8 %all_to_all.42.b_ref = f32[16,16,256]{2,1,0:T(8,128)S(1)} all-to-all(f32[16,16,256]{2,1,0:T(8,128)S(1)} %get-tuple-element.39), channel_id=1, replica_groups=mesh['depth'=16,'res'=8] {'depth'}, dimensions={0} | all-to-all | bytes 524288 | tf_op jit(solution)/shard_map/all_to_all | solution.py:605
  182.3 3.6 %all-to-all-start.6 = ((f32[8,16,16,128]{3,2,1,0:T(8,128)}), f32[8,16,16,128]{3,2,1,0:T(8,128)S(1)}, u32[]{:S(2)}, u32[]{:S(2)}) async-start(f32[8,16,16,128]{3,2,1,0:T(8,128)} %get-tuple-element.36), calls=%async_computation.6 | async-start | bytes 2097152 | tf_op jit(solution)/shard_map/all_to_all | solution.py:604
  185.9 1.6 shard_map.156
  187.5 13.1 %all-to-all-done.6.f_ref = f32[8,16,16,128]{3,2,1,0:T(8,128)S(1)} async-done(((f32[8,16,16,128]{3,2,1,0:T(8,128)}), f32[8,16,16,128]{3,2,1,0:T(8,128)S(1)}, u32[]{:S(2)}, u32[]{:S(2)}) %all-to-all-start.6) | async-done | bytes 1048608 | tf_op jit(solution)/shard_map/all_to_all | solution.py:604
  200.6 1.1 shard_map.155
  (6 shorter events, 0.0 us)
Async XLA Ops:
  7.2 10.1 %copy-start = (bf16[32,16,128]{2,1,0:T(8,128)(2,1)S(1)}, bf16[32,16,128]{2,1,0:T(8,128)(2,1)}, u32[]{:S(2)}) copy-start(bf16[32,16,128]{2,1,0:T(8,128)(2,1)} %ct_ref.1) | copy-start | bytes 393220
  8.8 9.2 %copy-start.11 = (bf16[128,8]{0,1:T(8,128)(2,1)S(1)}, bf16[128,8]{0,1:T(8,128)(2,1)}, u32[]{:S(2)}) copy-start(bf16[128,8]{0,1:T(8,128)(2,1)} %param.20) | copy-start | bytes 6148
  8.8 9.3 %copy-start.3 = (bf16[32,16,128]{2,1,0:T(8,128)(2,1)S(1)}, bf16[32,16,128]{2,1,0:T(8,128)(2,1)}, u32[]{:S(2)}) copy-start(bf16[32,16,128]{2,1,0:T(8,128)(2,1)} %pair_ref.3) | copy-start | bytes 393220
  11.1 22.0 %copy-start.10 = (bf16[64,144]{1,0:T(8,128)(2,1)S(1)}, bf16[64,144]{1,0:T(8,128)(2,1)}, u32[]{:S(2)}) copy-start(bf16[64,144]{1,0:T(8,128)(2,1)} %param.22) | copy-start | bytes 55300
  11.1 40.6 %copy-start.4 = (bf16[64,256]{1,0:T(8,128)(2,1)S(1)}, bf16[64,256]{1,0:T(8,128)(2,1)}, u32[]{:S(2)}) copy-start(bf16[64,256]{1,0:T(8,128)(2,1)} %win_ref.3) | copy-start | bytes 98308
  11.1 40.6 %copy-start.5 = (bf16[64,64]{1,0:T(8,128)(2,1)S(1)}, bf16[64,64]{1,0:T(8,128)(2,1)}, u32[]{:S(2)}) copy-start(bf16[64,64]{1,0:T(8,128)(2,1)} %wo_ref.3) | copy-start | bytes 24580
  11.1 22.0 %all-to-all-start = ((bf16[8,16,32,128]{3,2,1,0:T(8,128)(2,1)}), bf16[8,16,32,128]{3,2,1,0:T(8,128)(2,1)S(1)}, u32[]{:S(2)}, u32[]{:S(2)}) async-start(bf16[8,16,32,128]{3,2,1,0:T(8,128)(2,1)} %broadcast_in_dim.5), calls=%async_computation | async-start | bytes 2097152 | tf_op jit(solution)/shard_map/all_to_all | solution.py:572
  17.2 107.2 %all-gather.3.cloned.1.call-start = ((), (), s32[]{:S(2)}) async-start(), calls=%async_computation.8 | async-start | bytes 4456448 | tf_op jit(solution)/shard_map/all_gather | solution.py:578
  17.3 2.6 %collective-permute-start = (bf16[16,32,128]{2,1,0:T(8,128)(2,1)S(1)}, bf16[16,32,128]{2,1,0:T(8,128)(2,1)S(1)}, u32[]{:S(2)}, u32[]{:S(2)}) collective-permute-start(bf16[16,32,128]{2,1,0:T(8,128)(2,1)S(1)} %bitcast.28), channel_id=1, source_target_pairs={{0,0},{1,16},{2,32},{3,48},{4,64},{5,80},{6,96},{7,112},{8,8},{9,2... | collective-permute-start | bytes 393224 | tf_op jit(solution)/shard_map/ppermute | solution.py:569
  20.6 79.4 %copy-start.6 = (bf16[64,64]{1,0:T(8,128)(2,1)S(1)}, bf16[64,64]{1,0:T(8,128)(2,1)}, u32[]{:S(2)}) copy-start(bf16[64,64]{1,0:T(8,128)(2,1)} %wv_ref.3) | copy-start | bytes 24580
  20.6 79.4 %copy-start.7 = (bf16[64,64]{1,0:T(8,128)(2,1)S(1)}, bf16[64,64]{1,0:T(8,128)(2,1)}, u32[]{:S(2)}) copy-start(bf16[64,64]{1,0:T(8,128)(2,1)} %wt_ref.3) | copy-start | bytes 24580
  33.1 18.6 %copy-start.8 = (bf16[8,16,32,128]{3,2,1,0:T(8,128)(2,1)}, bf16[8,16,32,128]{3,2,1,0:T(8,128)(2,1)S(1)}, u32[]{:S(2)}) copy-start(bf16[8,16,32,128]{3,2,1,0:T(8,128)(2,1)S(1)} %all-to-all-done.g_ref) | copy-start | bytes 3145732
  33.3 18.4 %all-to-all-start.1 = ((f32[16,16,256]{2,1,0:T(8,128)}), f32[16,16,256]{2,1,0:T(8,128)S(1)}, u32[]{:S(2)}, u32[]{:S(2)}) async-start(f32[16,16,256]{2,1,0:T(8,128)} %shard_map.149), calls=%async_computation.1 | async-start | bytes 524288 | tf_op jit(solution)/shard_map/all_to_all | solution.py:579
  68.4 1.0 copy-start.1
  69.5 1.0 copy-start.2
  70.5 16.0 %all-to-all-start.2 = ((f32[16,2,16,128]{3,2,1,0:T(8,128)}), f32[16,2,16,128]{3,2,1,0:T(8,128)S(1)}, u32[]{:S(2)}, u32[]{:S(2)}) async-start(f32[16,2,16,128]{3,2,1,0:T(8,128)} %get-tuple-element.24), calls=%async_computation.2 | async-start | bytes 524288 | tf_op jit(solution)/shard_map/all_to_all | solution.py:585
  74.8 35.1 %copy-start.9 = (bf16[1024,128]{1,0:T(8,128)(2,1)S(1)}, bf16[1024,128]{1,0:T(8,128)(2,1)}, u32[]{:S(2)}) copy-start(bf16[1024,128]{1,0:T(8,128)(2,1)} %param.25) | copy-start | bytes 786436
  102.2 22.1 %all-to-all-start.4 = ((bf16[8,16,32,128]{3,2,1,0:T(8,128)(2,1)}), bf16[8,16,32,128]{3,2,1,0:T(8,128)(2,1)S(1)}, u32[]{:S(2)}, u32[]{:S(2)}) async-start(bf16[8,16,32,128]{3,2,1,0:T(8,128)(2,1)} %get-tuple-element.25.own_ref), calls=%async_computation.4 | async-start | bytes 2097152 | tf_op jit(solution)/shard_map/all_to_all | solution.py:592
  182.3 18.3 %all-to-all-start.6 = ((f32[8,16,16,128]{3,2,1,0:T(8,128)}), f32[8,16,16,128]{3,2,1,0:T(8,128)S(1)}, u32[]{:S(2)}, u32[]{:S(2)}) async-start(f32[8,16,16,128]{3,2,1,0:T(8,128)} %get-tuple-element.36), calls=%async_computation.6 | async-start | bytes 2097152 | tf_op jit(solution)/shard_map/all_to_all | solution.py:604
Sparse Core Ops, SparseCore 0:
  33.2 67.3 all-gather.2

commit v3 on v2

v3 whole, which is shorter than its diff:
```python
import jax
import jax.numpy as jnp
from jax import lax
from jax.experimental import pallas as pl
from jax.experimental.pallas import tpu as pltpu
from jax.sharding import PartitionSpec as P

f32 = jnp.float32
bf16 = jnp.bfloat16
EPS = 1e-05
NEG = -1000000000.0
SCALE = 8 ** (-0.5)
NN = (((1,), (0,)), ((), ()))
NT = (((1,), (1,)), ((), ()))
TN = (((0,), (0,)), ((), ()))
GROUP = 4
OWN_STEP = 8
VMEM = pltpu.CompilerParams(vmem_limit_bytes=50 * 1024 * 1024)


def mm(a, b, dims=NN):
    return lax.dot_general(a, b, dims, preferred_element_type=f32)


def split(x):
    hi = x.astype(bf16)
    lo = (x - hi.astype(f32)).astype(bf16)
    return hi, lo


def split3(x):
    hi = x.astype(bf16)
    rest = x - hi.astype(f32)
    mid = rest.astype(bf16)
    lo = (rest - mid.astype(f32)).astype(bf16)
    return hi, mid, lo


def cat(parts, axis):
    return jnp.concatenate(parts, axis=axis)


def mm2(x, w, dims=NN):
    hi, lo = split(x)
    return mm(hi, w, dims) + mm(lo, w, dims)


def mm3(x, w):
    hi, mid, lo = split3(x)
    return mm(hi, w) + mm(mid, w) + mm(lo, w)


def norm_rows(x):
    center = x - jnp.mean(x, -1, keepdims=True)
    rstd = lax.rsqrt(jnp.mean(center * center, -1, keepdims=True) + EPS)
    return center * rstd, rstd


def norm_back(normed, rstd, grad):
    return rstd * (
        grad
        - jnp.mean(grad, -1, keepdims=True)
        - normed * jnp.mean(grad * normed, -1, keepdims=True)
    )


def pair2(x):
    hi, lo = split(x)
    return cat([hi, lo], 1)


def head_mask(rows, cols, row_div, col_div):
    a = lax.broadcasted_iota(jnp.int32, (rows, cols), 0) // row_div
    b = lax.broadcasted_iota(jnp.int32, (rows, cols), 1) // col_div
    return (a == b).astype(f32)


def bias_kernel(pair_ref, wb_ref, out_ref, scr):
    xn, _ = norm_rows(pair_ref[...].astype(f32).reshape(512, 128))
    scr[...] = xn.reshape(32, 16, 128)
    wbt = wb_ref[...].astype(f32).T
    w2 = cat([wbt, wbt], 1).astype(bf16)
    own = head_mask(8, 256, 1, 32)
    rows = []
    for j in range(16):
        x2 = pair2(scr[:, j, :])
        tiled = cat([x2] * 8, 0)
        full = mm(w2, tiled, NT)
        rows.append(jnp.sum(full * own, 0, keepdims=True))
    block = cat(rows, 0)
    for k in range(16):
        out_ref[k] = block


def pack_kernel(x_ref, mask_ref, res_ref, count_ref, rows_ref, own_ref):
    seq = lax.broadcasted_iota(jnp.int32, (16, 32), 0)
    alive = (seq < count_ref[0]).astype(f32)
    live = mask_ref[...].astype(f32) * res_ref[...].astype(f32) * alive
    x = x_ref[...]
    diag = head_mask(32, 32, 1, 1)
    cols = [
        jnp.broadcast_to(jnp.sum(diag * live[k:k + 1, :], 1, keepdims=True), (32, 64))[None]
        for k in range(16)
    ]
    own_ref[...] = cat([x.astype(f32), cat(cols, 0)], 2).astype(bf16)
    dense = cat([x[:, :16], x[:, 16:]], 2)
    plane = cat([live, jnp.zeros((16, 96), f32)], 1).astype(bf16)
    for k in range(8):
        rows_ref[k, 0:16] = dense
        rows_ref[k, 16] = plane


def unpack(p):
    return cat([p[:, :, :64], p[:, :, 64:]], 1).reshape(256, 64)


def proj_kernel(
    g_ref, plane_ref, own_ref, win_ref,
    k2_ref, v2_ref, kt_ref, vt_ref, q_ref, gate_ref, live_ref,
    wqg, wkvt, wkk, wvv,
):
    s = pl.program_id(0)

    @pl.when(s == 0)
    def _():
        w = win_ref[...].astype(f32)
        wt = w.T
        qg = cat([wt[0:64], wt[192:256]], 0)
        wqg[...] = cat([qg, qg], 1).astype(bf16)
        kv = wt[64:192]
        wkvt[...] = cat([kv, kv], 1).astype(bf16)
        for at, ref in ((64, wkk), (128, wvv)):
            one = w[:, at:at + 64]
            row = cat([one, one], 1)
            ref[...] = cat([row, row], 0).astype(bf16)
        live_ref[...] = cat([plane_ref[k, 0, :, 0:32] for k in range(8)], 1)

    lane = lax.broadcasted_iota(jnp.int32, (256, 128), 1)
    heads = head_mask(64, 256, 8, 32) * SCALE

    def two(x):
        hi = x.astype(bf16).astype(f32)
        return jnp.where(lane < 64, hi, x - hi).astype(bf16)

    for u in range(GROUP):
        xn, _ = norm_rows(unpack(g_ref[:, u].astype(f32)))
        x2 = pair2(xn)
        k2_ref[u] = two(mm(x2, wkk[...]))
        v2_ref[u] = two(mm(x2, wvv[...]))
        hi, lo = split(mm(wkvt[...], x2, NT))
        kt_ref[u] = cat([hi[:64], lo[:64]], 0)
        vt_ref[u] = cat([hi[64:], lo[64:]], 0)
        xon, _ = norm_rows(own_ref[u].astype(f32)[:, :64])
        qg = mm(wqg[...], cat([pair2(xon)] * 8, 0), NT)
        qhi, qlo = split(qg[:64] * heads)
        q_ref[u] = cat([qhi, qlo], 0)
        gate_ref[u] = jax.nn.sigmoid(qg[64:])


def row_fwd_kernel(
    k2_ref, vt_ref, q_ref, gate_ref, live_ref, own_ref, bias_ref, wo_ref,
    p_ref, o_ref, m1_ref, any_ref, c1_ref,
):
    s = pl.program_id(0)
    heads = head_mask(64, 256, 8, 32)
    wo = wo_ref[...]
    wo2 = cat([wo, wo], 0)
    seq = lax.broadcasted_iota(jnp.int32, (16, 128), 0)
    for u in range(GROUP):
        pick = (seq == s * GROUP + u).astype(bf16)
        live = mm(live_ref[...], pick, TN)
        k2 = k2_ref[u]
        qhi, qlo = q_ref[u, 0:64], q_ref[u, 64:128]
        logits = mm(k2, cat([qhi, qhi], 0)) + mm(k2[:, :64], qlo)
        logits = logits + bias_ref[...].reshape(256, 256)
        logits = jnp.where(cat([live, live], 1) > 0, logits, NEG)
        e = jnp.exp(logits - jnp.max(logits, 0, keepdims=True))
        p = e * (1.0 / jnp.sum(e, 0, keepdims=True))
        p_ref[u] = p
        some = jnp.max(live, 0, keepdims=True)
        any_ref[u] = jnp.broadcast_to(cat([some, some], 1), (8, 256))
        phi, plo = split(p)
        vt = vt_ref[u]
        first = mm(vt, phi)
        o = (first[:64] + first[64:] + mm(vt[:64], plo)) * heads
        o_ref[u] = o
        ahi, alo = split(o * gate_ref[u])
        y = mm(cat([ahi, alo], 0), wo2, TN)
        own = own_ref[u].astype(f32)
        m1 = own[:, :64] + jnp.sum(y.reshape(8, 32, 64), 0)
        m1_ref[u] = m1
        c1_ref[:, 0, s * GROUP + u, :] = cat([m1[:16], m1[16:]], 1)
        lv = own[:, 64:]
        c1_ref[:, 1, s * GROUP + u, :] = cat([lv[:16], lv[16:]], 1)


def diag2(w):
    z = jnp.zeros_like(w)
    return cat([cat([w, z], 1), cat([z, w], 1)], 0)


def col_kernel(c1_ref, cw_ref, out_ref):
    x = c1_ref[:, 0].reshape(256, 128)
    live = c1_ref[:, 1].reshape(256, 128)
    halves = (head_mask(128, 128, 64, 64) * (1.0 / 64)).astype(bf16)
    center = x - mm3(x, halves)
    xn = center * lax.rsqrt(mm3(center * center, halves) + EPS)
    cw = cw_ref[...].astype(f32)
    wq = diag2(cw[:, 0:64]).astype(bf16)
    wk = diag2(cw[:, 64:128]).astype(bf16)
    wv = diag2(cw[:, 128:192]).astype(bf16)
    total = jnp.sum(live * xn, 0, keepdims=True)
    count = jnp.sum(live, 0, keepdims=True)
    mean = total / jnp.maximum(count, 1.0)
    colq = mm3(jnp.broadcast_to(mean, (8, 128)), wq)[0:1] * SCALE
    kt = mm2(xn, wk)
    vt = mm2(xn, wv)
    groups = head_mask(128, 128, 8, 8).astype(bf16)
    logits = jnp.where(live > 0, mm3(kt * colq, groups), NEG)
    peak = jnp.max(logits, 0, keepdims=True)
    e = jnp.exp(logits - peak)
    den = jnp.sum(e, 0, keepdims=True)
    w = e / den
    wv_ = w * vt
    attended = jnp.sum(wv_, 0, keepdims=True)
    khi, klo = split(kt)

    def by_key(z):
        zhi, zlo = split(z)
        full = mm(khi, zhi, TN) + mm(klo, zhi, TN) + mm(khi, zlo, TN)
        lane = lax.broadcasted_iota(jnp.int32, (8, 128), 1)
        return jnp.where(lane < 64, full[0:8], full[64:72])

    lt = live.T
    rows = [
        by_key(wv_), by_key(w), attended, peak, den, colq, count, count, count, count,
        lt[0:1, :128], lt[0:1, 128:], lt[64:65, :128], lt[64:65, 128:],
        count, count, count, count,
    ]
    block = cat(rows, 0)
    for k in range(16):
        out_ref[k] = block


def unpair(x):
    return cat([x[:, 0:64], x[:, 64:128]], 0)


def spread(v):
    return jnp.broadcast_to(v[None], (16, 32, 64)).reshape(512, 64)


def factor_kernel(m1_ref, c2_ref, own_ref, cw_ref, wv_ref, wt_ref, m2_ref, d_ref):
    m1 = m1_ref[...].reshape(512, 64)
    live = own_ref[...].reshape(512, 128)[:, 64:].astype(f32)
    attended = unpair(c2_ref[:, 16, :])
    xn, _ = norm_rows(m1)
    gate = jax.nn.sigmoid(mm2(xn, cw_ref[:, 192:256]))
    m2 = m1 + mm2(gate * spread(attended), wv_ref[...])
    m2_ref[...] = m2.reshape(16, 32, 64)
    xn2, _ = norm_rows(m2)
    lr = live * mm2(xn2, wt_ref[...])
    lr = lr.reshape(16, 32, 64)
    lr = cat([lr[:, :16], lr[:, 16:]], 2).astype(bf16)
    lt = [c2_ref[:, 24 + k, :].astype(bf16) for k in range(4)]
    for k in range(8):
        d_ref[k, 0:16] = lr
        for q in range(4):
            d_ref[k, 16 + q] = lt[q]


def masks_by_row(p):
    low = cat([p[:, 0], p[:, 1]], 2)
    high = cat([p[:, 2], p[:, 3]], 2)
    return cat([low, high], 1)


def outer_kernel(
    core_ref, da_ref, own_ref, cta_ref, ctb_ref, cta2_ref, ctb2_ref, w_ref, m2_ref, c2_ref, m1_ref,
    ownx_ref, adj_ref, cw_ref, wv_ref, wt_ref, g2_ref, dcg_ref, e1_ref,
    inv, turned, stage, res, lrs, wide, wf,
):
    step = pl.program_id(0)
    core = core_ref[0]

    @pl.when(step == 0)
    def _():
        every = masks_by_row(da_ref[:, 16:20]).reshape(256, 256)
        mine = masks_by_row(own_ref[:, 16:20]).reshape(32, 256)
        value = 1.0 / jnp.maximum(mm(every, mine, NT), 1.0)
        for k in range(32):
            inv[k] = jnp.broadcast_to(value[:, k:k + 1], (256, 128))
        for s in range(16):
            piece = unpack(da_ref[:, s].astype(f32)).T
            for half in range(2):
                cols = piece[:, 128 * half:128 * half + 128]
                lrs[half, pl.ds(s, 32, stride=16), :] = cols[0:32]
                lrs[half, pl.ds(512 + s, 32, stride=16), :] = cols[32:64]
        for half in range(2):
            turned[0, :, 128 * half:128 * half + 128] = lrs[half, 512:1024].astype(bf16)
            turned[1, :, 128 * half:128 * half + 128] = lrs[half, 0:512].astype(bf16)
        wf[...] = w_ref[...].astype(f32)
        for k in range(32):
            first = wf[pl.ds(k, 32, stride=32), :].astype(bf16)
            second = w_ref[32 * k:32 * k + 32]
            for part in range(2):
                wide[0, :, 256 * k + 128 * part:256 * k + 128 * part + 128] = first
                wide[1, :, 256 * k + 128 * part:256 * k + 128 * part + 128] = second

    for side in range(2):
        for k in range(OWN_STEP):
            if side == 0:
                one = step * OWN_STEP + k
                x = cta_ref[:, 0, k].astype(f32)
                y = cta2_ref[:, 0, k].astype(f32)
                ct = cat([jnp.where(core == 0, x, y), jnp.where(core == 0, y, x)], 1)
            else:
                slot, at = k // (OWN_STEP // 2), k % (OWN_STEP // 2)
                one = (slot + core) % 2 * 16 + step * (OWN_STEP // 2) + at
                ct = (ctb_ref if slot == 0 else ctb2_ref)[:, 0, at].astype(f32)
            hi, lo = split(ct.reshape(256, 128) * inv[one])
            both = mm(turned[side], cat([hi, lo], 1))
            uhi, ulo = split(both[:, :128] + both[:, 128:])
            rows = pl.ds(pl.multiple_of(one * 16, 16), 16)
            for b in range(32):
                stage[side, rows, 256 * b:256 * b + 128] = uhi[16 * b:16 * b + 16]
                stage[side, rows, 256 * b + 128:256 * b + 256] = ulo[16 * b:16 * b + 16]

    @pl.when(step == 32 // OWN_STEP - 1)
    def _():
        grads = []
        for side in range(2):
            res[:, 0:32] = mm(stage[side], wide[side], NT)
            grads.append(cat([res[pl.ds(s, 32, stride=16), :] for s in range(16)], 0)[:, 0:32])
        lv = ownx_ref[...].reshape(512, 128)[:, 64:].astype(f32)
        dlr = cat(grads, 1) * lv
        m2 = m2_ref[...].reshape(512, 64)
        xn2, rstd2 = norm_rows(m2)
        adj = adj_ref[...].reshape(512, 64).astype(f32)
        g2 = adj + norm_back(xn2, rstd2, mm2(dlr, wt_ref[...], NT))
        g2_ref[...] = g2.reshape(16, 32, 64)
        xn, _ = norm_rows(m1_ref[...].reshape(512, 64))
        gate = jax.nn.sigmoid(mm2(xn, cw_ref[:, 192:256]))
        dmix = mm2(g2, wv_ref[...], NT)
        attended = spread(unpair(c2_ref[:, 16, :]))
        dcg_ref[...] = (dmix * attended * gate * (1.0 - gate)).reshape(16, 32, 64)
        da = jnp.sum((gate * dmix).reshape(16, 32, 64), 0)
        packed = cat([da[:16], da[16:]], 1)
        for k in range(16):
            e1_ref[k] = packed


def row_bwd_kernel(
    e1_ref, c2_ref, m1_ref, own_ref, g2_ref, dcg_ref, cw_ref,
    p_ref, o_ref, v2_ref, gate_ref, any_ref, wo_ref,
    g1_ref, ds_ref, do_ref, dg_ref, bias_ref,
    g1s,
):
    s = pl.program_id(0)

    @pl.when(s == 0)
    def _():
        cw = cw_ref[...]
        groups = head_mask(64, 64, 8, 8).astype(bf16)
        da = jnp.sum(e1_ref[...], 0)
        da = unpair(da)
        attended = unpair(c2_ref[:, 16, :])
        peak = unpair(c2_ref[:, 17, :])
        den = unpair(c2_ref[:, 18, :])
        colq = unpair(c2_ref[:, 19, :])
        count = unpair(c2_ref[:, 20, :])
        delta = mm3(da * attended, groups)
        feature = lax.broadcasted_iota(jnp.int32, (32, 64), 1) % 8
        dq = jnp.zeros((32, 64), f32)
        for k in range(8):
            z = mm3(da * unpair(c2_ref[:, k, :]), groups) - delta * unpair(c2_ref[:, 8 + k, :])
            dq = dq + jnp.where(feature == k, z, 0.0)
        dtotal = mm2(dq * SCALE, cw[:, 0:64], NT) / jnp.maximum(count, 1.0)
        live = own_ref[...].reshape(512, 128)[:, 64:].astype(f32)
        xn, rstd = norm_rows(m1_ref[...].reshape(512, 64))
        kt = mm2(xn, cw[:, 64:128])
        vt = mm2(xn, cw[:, 128:192])
        qs = spread(colq)
        logits = jnp.where(live > 0, mm3(kt * qs, groups), NEG)
        weights = jnp.exp(logits - spread(peak)) / spread(den)
        das = spread(da)
        dl = weights * (mm2(vt * das, groups) - spread(delta)) * live
        dxn = (
            mm2(dcg_ref[...].reshape(512, 64), cw[:, 192:256], NT)
            + mm2(dl * qs, cw[:, 64:128], NT)
            + mm2(weights * das, cw[:, 128:192], NT)
            + live * spread(dtotal)
        )
        g1 = g2_ref[...].reshape(512, 64) + norm_back(xn, rstd, dxn)
        g1s[...] = g1.reshape(16, 32, 64)
        bias_ref[...] = jnp.zeros_like(bias_ref)

    heads = head_mask(64, 256, 8, 32)
    wo = wo_ref[...]
    wo2 = cat([wo, wo], 1)
    for u in range(GROUP):
        dm = g1s[s * GROUP + u]
        g1_ref[u] = dm
        o = o_ref[u]
        v2 = v2_ref[u]
        gate = gate_ref[u]
        dout = mm(wo2, cat([pair2(dm)] * 8, 0), NT)
        hi, lo = split(dout * o * gate * (1.0 - gate))
        dg_ref[u] = cat([hi, lo], 0)
        do = dout * gate * heads
        hi, lo = split(do)
        do_ref[u] = cat([hi, lo], 0)
        do_live = do * any_ref[u, 0:1, :]
        delta = jnp.sum(do_live * o, 0, keepdims=True)
        lhi, llo = split(do_live)
        dp = mm(v2, cat([lhi, lhi], 0)) + mm(v2[:, :64], llo)
        ds = p_ref[u] * (dp - delta)
        bias_ref[...] += ds.reshape(16, 16, 256)
        shi, slo = split(ds)
        ds_ref[u, :, 0:256] = shi
        ds_ref[u, :, 256:512] = slo


def row_inputs_kernel(
    p_ref, ds_ref, do_ref, dg_ref, q_ref, kt_ref, win_ref, dxo_ref, f_ref, wback, wown
):
    @pl.when(pl.program_id(0) == 0)
    def _():
        wt = win_ref[...].astype(f32).T
        qg = cat([wt[0:64], wt[192:256]], 0)
        wback[...] = cat([wt[64:128], wt[64:128], wt[128:192], wt[128:192]], 0).astype(bf16)
        wown[...] = cat([qg, qg], 0).astype(bf16)

    heads = head_mask(64, 256, 8, 32) * SCALE
    zero = jnp.zeros((64, 256), bf16)
    for u in range(GROUP):
        shi, slo = ds_ref[u, :, 0:256], ds_ref[u, :, 256:512]
        kt = kt_ref[u]
        q = q_ref[u]
        do = do_ref[u]
        dg = dg_ref[u]
        first = mm(kt, shi)
        dq = (first[:64] + first[64:] + mm(kt[:64], slo)) * heads
        dk = mm(shi, q, NT) + mm(slo, cat([q[:64], zero], 0), NT)
        phi, plo = split(p_ref[u])
        dv = mm(phi, do, NT) + mm(plo, cat([do[:64], zero], 0), NT)
        dx = mm2(cat([dk, dv], 1), wback[...]).reshape(8, 32, 64)
        f_ref[:, u] = cat([dx[:, :16], dx[:, 16:]], 2)
        qhi, qlo = split(dq)
        dxo = mm(cat([qhi, dg[:64], qlo, dg[64:]], 0), wown[...], TN)
        dxo_ref[u] = jnp.sum(dxo.reshape(8, 32, 64), 0)


def final_rows_kernel(f_ref, dxo_ref, g1_ref, own_ref, out_ref):
    total = jnp.sum(f_ref[...], 0)
    total = cat([total[:, :, :64], total[:, :, 64:]], 1).reshape(512, 64)
    total = total + dxo_ref[...].reshape(512, 64)
    xn, rstd = norm_rows(own_ref[...].reshape(512, 128)[:, :64].astype(f32))
    out = g1_ref[...].reshape(512, 64) + norm_back(xn, rstd, total)
    out_ref[...] = out.reshape(16, 32, 64)


def final_pair_kernel(b_ref, pair_ref, wb_ref, ct_ref, out_ref, scr):
    total = jnp.sum(b_ref[...], 0)
    wbt = wb_ref[...].astype(f32).T
    w2 = cat([wbt, wbt], 0).astype(bf16)
    own = head_mask(8, 256, 1, 32)
    for j in range(16):
        wide = jnp.broadcast_to(total[j:j + 1, :], (8, 256)) * own
        hi, lo = split(wide)
        y = mm(cat([hi, lo], 0), w2, TN)
        scr[:, j, :] = jnp.sum(y.reshape(8, 32, 128), 0)
    xn, rstd = norm_rows(pair_ref[...].reshape(512, 128).astype(f32))
    out = norm_back(xn, rstd, scr[...].reshape(512, 128)) + ct_ref[...].reshape(512, 128).astype(f32)
    out_ref[...] = out.reshape(32, 16, 128)


def sds(shape, dtype=f32):
    return jax.ShapeDtypeStruct(shape, dtype)


def full(shape):
    zeros = (0,) * len(shape)
    return pl.BlockSpec(shape, lambda s: zeros)


def row(shape):
    rest = (0,) * (len(shape) - 1)
    return pl.BlockSpec((GROUP,) + shape[1:], lambda s: (s,) + rest)


def whole_call(kernel, out_shape, *args, scratch=()):
    return pl.pallas_call(
        kernel, out_shape=out_shape, scratch_shapes=list(scratch), compiler_params=VMEM
    )(*args)


def project(rows, own, win):
    return pl.pallas_call(
        proj_kernel,
        grid=(16 // GROUP,),
        in_specs=[
            pl.BlockSpec((8, GROUP, 16, 128), lambda s: (0, s, 0, 0)),
            pl.BlockSpec((8, 1, 16, 128), lambda s: (0, 16, 0, 0)),
            row((16, 32, 128)), full((64, 256)),
        ],
        out_specs=[
            row((16, 256, 128)), row((16, 256, 128)), row((16, 128, 256)), row((16, 128, 256)),
            row((16, 128, 256)), row((16, 64, 256)), full((16, 256)),
        ],
        out_shape=[
            sds((16, 256, 128), bf16), sds((16, 256, 128), bf16), sds((16, 128, 256), bf16),
            sds((16, 128, 256), bf16), sds((16, 128, 256), bf16), sds((16, 64, 256)),
            sds((16, 256), bf16),
        ],
        scratch_shapes=[
            pltpu.VMEM((128, 128), bf16), pltpu.VMEM((128, 128), bf16),
            pltpu.VMEM((128, 128), bf16), pltpu.VMEM((128, 128), bf16),
        ],
        compiler_params=VMEM,
    )(rows, rows, own, win)


def row_forward(k2, vt, q, gate, live, own, bias, wo):
    return pl.pallas_call(
        row_fwd_kernel,
        grid=(16 // GROUP,),
        in_specs=[
            row((16, 256, 128)), row((16, 128, 256)), row((16, 128, 256)), row((16, 64, 256)),
            full((16, 256)), row((16, 32, 128)), full((16, 16, 256)), full((64, 64)),
        ],
        out_specs=[
            row((16, 256, 256)), row((16, 64, 256)), row((16, 32, 64)), row((16, 8, 256)),
            full((16, 2, 16, 128)),
        ],
        out_shape=[
            sds((16, 256, 256)), sds((16, 64, 256)), sds((16, 32, 64)), sds((16, 8, 256)),
            sds((16, 2, 16, 128)),
        ],
        compiler_params=VMEM,
    )(k2, vt, q, gate, live, own, bias, wo)


def outer_product(core, ct, ct2, factors, dblock, w, m2, c2, m1, own, adj, cw, wvo, wtf):
    half = OWN_STEP // 2
    one = pl.BlockSpec((8, 1, OWN_STEP, 16, 128), lambda s: (0, 0, s, 0, 0))
    two = pl.BlockSpec((8, 1, half, 32, 128), lambda s: (0, 1, s, 0, 0))
    return pl.pallas_call(
        outer_kernel,
        grid=(32 // OWN_STEP,),
        in_specs=[
            pl.BlockSpec(memory_space=pltpu.SMEM),
            full((8, 20, 16, 128)),
            pl.BlockSpec((1, 20, 16, 128), lambda s: (0, 0, 0, 0)),
            one, two, one, two,
            full((1024, 128)),
            full((16, 32, 64)), full((16, 32, 128)), full((16, 32, 64)), full((16, 32, 128)),
            full((16, 32, 64)), full((64, 256)), full((64, 64)), full((64, 64)),
        ],
        out_specs=[full((16, 32, 64)), full((16, 32, 64)), full((16, 16, 128))],
        out_shape=[sds((16, 32, 64)), sds((16, 32, 64)), sds((16, 16, 128))],
        scratch_shapes=[
            pltpu.VMEM((32, 256, 128), f32),
            pltpu.VMEM((2, 512, 256), bf16),
            pltpu.VMEM((2, 512, 8192), bf16),
            pltpu.VMEM((512, 128), f32),
            pltpu.VMEM((2, 1024, 128), f32),
            pltpu.VMEM((2, 32, 8192), bf16),
            pltpu.VMEM((1024, 128), f32),
        ],
        compiler_params=VMEM,
    )(
        core, factors, dblock, ct.reshape(8, 2, 32, 16, 128), ct.reshape(8, 2, 16, 32, 128),
        ct2.reshape(8, 2, 32, 16, 128), ct2.reshape(8, 2, 16, 32, 128), w, m2, c2, m1, own, adj,
        cw, wvo, wtf,
    )


def row_backward(e1, c2, m1, own, g2, dcg, cw, p, o, v2, gate, any_live, wo):
    return pl.pallas_call(
        row_bwd_kernel,
        grid=(16 // GROUP,),
        in_specs=[
            full((16, 16, 128)), full((16, 32, 128)), full((16, 32, 64)), full((16, 32, 128)),
            full((16, 32, 64)), full((16, 32, 64)), full((64, 256)),
            row((16, 256, 256)), row((16, 64, 256)), row((16, 256, 128)), row((16, 64, 256)),
            row((16, 8, 256)), full((64, 64)),
        ],
        out_specs=[
            row((16, 32, 64)), row((16, 256, 512)), row((16, 128, 256)), row((16, 128, 256)),
            full((16, 16, 256)),
        ],
        out_shape=[
            sds((16, 32, 64)), sds((16, 256, 512), bf16), sds((16, 128, 256), bf16),
            sds((16, 128, 256), bf16), sds((16, 16, 256)),
        ],
        scratch_shapes=[pltpu.VMEM((16, 32, 64), f32)],
        compiler_params=VMEM,
    )(e1, c2, m1, own, g2, dcg, cw, p, o, v2, gate, any_live, wo)


def row_inputs(p, ds, do, dg, q, kt, win):
    return pl.pallas_call(
        row_inputs_kernel,
        grid=(16 // GROUP,),
        in_specs=[
            row((16, 256, 256)), row((16, 256, 512)), row((16, 128, 256)), row((16, 128, 256)),
            row((16, 128, 256)), row((16, 128, 256)), full((64, 256)),
        ],
        out_specs=[row((16, 32, 64)), pl.BlockSpec((8, GROUP, 16, 128), lambda s: (0, s, 0, 0))],
        out_shape=[sds((16, 32, 64)), sds((8, 16, 16, 128))],
        scratch_shapes=[pltpu.VMEM((256, 64), bf16), pltpu.VMEM((256, 64), bf16)],
        compiler_params=VMEM,
    )(p, ds, do, dg, q, kt, win)


def body(
    alignment_state,
    pairwise_state,
    alignment_mask,
    residue_entry_mask,
    sequence_live_count,
    horizontal_intake_coefs,
    pairwise_bias_weights,
    horizontal_readout_coefs,
    column_input_weights,
    vertical_readout_coefs,
    tensor_factor_coefs,
    outer_output_weights,
    adjoint_of_result_track,
    pairwise_cotangent,
):
    smem = pl.BlockSpec(memory_space=pltpu.SMEM)
    vmem = pl.BlockSpec(memory_space=pltpu.VMEM)
    row_block, own = pl.pallas_call(
        pack_kernel,
        in_specs=[vmem, vmem, vmem, smem],
        out_shape=[sds((8, 17, 16, 128), bf16), sds((16, 32, 128), bf16)],
        compiler_params=VMEM,
    )(alignment_state, alignment_mask, residue_entry_mask.reshape(1, 32), sequence_live_count)
    rows = lax.all_to_all(row_block, "res", 0, 0)
    bias_block = whole_call(
        bias_kernel, sds((16, 16, 256)), pairwise_state, pairwise_bias_weights,
        scratch=[pltpu.VMEM((32, 16, 128), f32)],
    )
    cw = cat(
        [
            column_input_weights[:, :64],
            jnp.tile(column_input_weights[:, 64:72], (1, 8)),
            jnp.tile(column_input_weights[:, 72:80], (1, 8)),
            column_input_weights[:, 80:],
        ],
        1,
    )

    turned = pairwise_cotangent.transpose(1, 0, 2)
    perm = [(d * 8 + r, (2 * r + d % 2) * 8 + d // 2) for d in range(16) for r in range(8)]
    turned = lax.ppermute(turned, ("depth", "res"), perm)
    both = cat([pairwise_cotangent.reshape(512, 128), turned.reshape(512, 128)], 0)
    both = jnp.broadcast_to(both[None], (8, 1024, 128))

    bias_block, rows = lax.optimization_barrier((bias_block, rows))
    bias = lax.all_to_all(bias_block, "depth", 0, 0)
    k2, v2, kt, vt, q, gate, live = project(rows, own, horizontal_intake_coefs)
    bias, both = lax.optimization_barrier((bias, both))
    same_core = [[c + 2 * k for k in range(8)] for c in range(2)]
    ct = lax.all_to_all(both, "depth", 0, 0, axis_index_groups=same_core)
    p, o, m1, any_live, c1 = row_forward(
        k2, vt, q, gate, live, own, bias, horizontal_readout_coefs
    )
    c1, ct = lax.optimization_barrier((c1, ct))
    ct2 = lax.ppermute(ct, "depth", [(d, d ^ 1) for d in range(16)])
    c1 = lax.all_to_all(c1, "depth", 0, 0)
    c2 = whole_call(col_kernel, sds((16, 32, 128)), c1, cw)
    c2 = lax.all_to_all(c2, "depth", 0, 0)
    m2, dblock = whole_call(
        factor_kernel, [sds((16, 32, 64)), sds((8, 20, 16, 128), bf16)],
        m1, c2, own, cw, vertical_readout_coefs, tensor_factor_coefs,
    )
    factors = lax.all_to_all(dblock, "res", 0, 0)
    core = (lax.axis_index("depth") % 2).astype(jnp.int32).reshape(1)
    g2, dcg, e1 = outer_product(
        core, ct, ct2, factors, dblock, outer_output_weights, m2, c2, m1, own,
        adjoint_of_result_track, cw, vertical_readout_coefs, tensor_factor_coefs,
    )
    e1 = lax.all_to_all(e1, "depth", 0, 0)
    g1, ds, do, dg, bblock = row_backward(
        e1, c2, m1, own, g2, dcg, cw, p, o, v2, gate, any_live, horizontal_readout_coefs
    )
    bsum = lax.all_to_all(bblock, "depth", 0, 0)
    dxo, fblock = row_inputs(p, ds, do, dg, q, kt, horizontal_intake_coefs)
    fblock, bsum = lax.optimization_barrier((fblock, bsum))
    fsum = lax.all_to_all(fblock, "res", 0, 0)
    alignment_gradient = whole_call(final_rows_kernel, sds((16, 32, 64)), fsum, dxo, g1, own)
    pair_grad = whole_call(
        final_pair_kernel, sds((32, 16, 128)), bsum, pairwise_state, pairwise_bias_weights,
        pairwise_cotangent, scratch=[pltpu.VMEM((32, 16, 128), f32)],
    )
    return alignment_gradient, pair_grad


def solution(mesh):
    in_specs = (
        P("depth", "res", None),
        P("res", "depth", None),
        P("depth", "res"),
        P("res"),
        P("depth"),
        P(),
        P(),
        P(),
        P(),
        P(),
        P(),
        P(),
        P("depth", "res", None),
        P("res", "depth", None),
    )
    out_specs = (P("depth", "res", None), P("res", "depth", None))
    return jax.shard_map(body, mesh=mesh, in_specs=in_specs, out_specs=out_specs, check_vma=False)
```

time: 209 us -> 191 us (0.914)
  between operations: 14.9 us -> 1.5 us
  starting transfers between devices: 32 us -> 42.4 us
  blocking collectives: 36.5 us -> 26.2 us
  waiting for transfers between devices: 56.3 us -> 47.1 us
  other arithmetic: 3.85 us -> 0.11 us
  local copies, waits for them, and re-layouts: 6.49 us -> 10.1 us
  Pallas kernels: 58.5 us -> 62.1 us
    pallas_call x2 -> x5, Pallas kernels: 32 us -> 45.2 us  [the longest x1 15.4 us: outer_product(): pl.pallas_call(outer_kernel, grid=(32 // OWN_STEP,), in_specs=[pl.BlockSp...]
    all_to_all x1 -> x0, blocking collectives: 11.8 us -> none  [body(): bsum = lax.all_to_all(bblock, 'depth', 0, 0)]
    pallas_call x1, Pallas kernels: 18.6 us -> 9.15 us  [row_backward(): pl.pallas_call(row_bwd_kernel, grid=(16 // GROUP,), in_specs=[full((16, 1...]
    all_to_all x1 -> x3, starting transfers between devices: 6.08 us -> 14.4 us  [the longest x1 5.95 us: body(): rows = lax.all_to_all(row_block, 'res', 0, 0)]
    unnamed x26 -> x36, local copies, waits for them, and re-layouts: 2.23 us -> 7.92 us
    all_to_all x1 -> x3, waiting for transfers between devices: 12.4 us -> 8.17 us  [the longest x1 5.35 us: body(): ct = lax.all_to_all(both, 'depth', 0, 0, axis_index_groups=same_core)]
    all_to_all x1, waiting for transfers between devices: 11.5 us -> 8.45 us  [body(): c1 = lax.all_to_all(c1, 'depth', 0, 0)]
    concatenate x4 -> x2, other arithmetic: 3.08 us -> 0.11 us  [cat(): return jnp.concatenate(parts, axis=axis)]
  transfers between devices with their start and end apart: 7 -> 9, of which waited for: 5 -> 6; matrix products, arithmetic and copies ran while one was open for 2% -> 1% of each run, Pallas kernels for 11% -> 19%
where the time goes in v3:
time: 191 us; the launch traced here: 190 us
  Pallas kernels  62.1 us (33%)
  waiting for transfers between devices  47.1 us (25%)
  starting transfers between devices  42.4 us (22%)
  blocking collectives  26.2 us (14%)
  local copies, waits for them, and re-layouts  10.1 us (5%)
    pallas_call x1, Pallas kernels, outer_product(): pl.pallas_call(outer_kernel, grid=(32 // OWN_STEP,), in_specs=[pl.BlockSp...  15.4 us
    all_to_all x1, blocking collectives, body(): e1 = lax.all_to_all(e1, 'depth', 0, 0)  14.1 us
    all_to_all x1, waiting for transfers between devices, body(): fsum = lax.all_to_all(fblock, 'res', 0, 0)  13.3 us
    pallas_call x1, Pallas kernels, row_forward(): pl.pallas_call(row_fwd_kernel, grid=(16 // GROUP,), in_specs=[row((16, 25...  13.1 us
    all_to_all x1, blocking collectives, body(): c2 = lax.all_to_all(c2, 'depth', 0, 0)  12.1 us
    all_to_all x1, starting transfers between devices, body(): bias = lax.all_to_all(bias_block, 'depth', 0, 0)  10.3 us
    pallas_call x1, Pallas kernels, row_backward(): pl.pallas_call(row_bwd_kernel, grid=(16 // GROUP,), in_specs=[full((16, 1...  9.15 us
    all_to_all x1, waiting for transfers between devices, body(): bias = lax.all_to_all(bias_block, 'depth', 0, 0)  8.63 us
  transfers between devices with their start and end apart: 9, of which 6 were waited for; matrix products, arithmetic and copies ran while one was open for 1% of the time, Pallas kernels for 19%

profile of v3, /device:TPU:1, one launch (start us, length us, event | category | flops | bytes accessed | tf_op | source)
XLA Modules:
  0.0 189.5 jit_solution(17538288818014263109)
XLA Ops:
  0.6 0.0 copy-start
  1.3 0.0 copy-start.10
  1.3 0.9 copy-done.10
  2.2 0.0 copy-start.14
  2.2 0.7 copy-done.14
  2.9 0.0 copy-start.15
  2.9 0.7 copy-done.15
  3.6 1.1 shard_map.150
  4.6 5.9 %all-to-all-start = ((bf16[8,17,16,128]{3,2,1,0:T(8,128)(2,1)}), bf16[8,17,16,128]{3,2,1,0:T(8,128)(2,1)S(1)}, u32[]{:S(2)}, u32[]{:S(2)}) async-start(bf16[8,17,16,128]{3,2,1,0:T(8,128)(2,1)} %get-tuple-element.36), calls=%async_computation | async-start | bytes 1114112 | tf_op jit(solution)/shard_map/all_to_all | solution.py:641
  10.6 0.9 copy.26
  11.5 0.7 collective-permute-start
  12.2 0.8 copy.18.wb_ref
  13.0 0.9 copy-done.5
  13.9 1.8 shard_map.149
  15.7 2.8 %all-to-all-done.g_ref.plane_ref = bf16[8,17,16,128]{3,2,1,0:T(8,128)(2,1)S(1)} async-done(((bf16[8,17,16,128]{3,2,1,0:T(8,128)(2,1)}), bf16[8,17,16,128]{3,2,1,0:T(8,128)(2,1)S(1)}, u32[]{:S(2)}, u32[]{:S(2)}) %all-to-all-start) | async-done | bytes 557088 | tf_op jit(solution)/shard_map/all_to_all | solution.py:641
  18.6 10.3 %all-to-all-start.1 = ((f32[16,16,256]{2,1,0:T(8,128)}), f32[16,16,256]{2,1,0:T(8,128)S(1)}, u32[]{:S(2)}, u32[]{:S(2)}) async-start(f32[16,16,256]{2,1,0:T(8,128)} %shard_map.149), calls=%async_computation.1 | async-start | bytes 524288 | tf_op jit(solution)/shard_map/all_to_all | solution.py:663
  28.9 0.0 collective-permute-done
  28.9 0.0 copy-done
  28.9 8.6 %all-to-all-done.1.bias_ref = f32[16,16,256]{2,1,0:T(8,128)S(1)} async-done(((f32[16,16,256]{2,1,0:T(8,128)}), f32[16,16,256]{2,1,0:T(8,128)S(1)}, u32[]{:S(2)}, u32[]{:S(2)}) %all-to-all-start.1) | async-done | bytes 262176 | tf_op jit(solution)/shard_map/all_to_all | solution.py:663
  37.5 1.7 broadcast_in_dim.2
  39.2 4.5 %all-to-all-start.2 = ((bf16[8,1024,128]{2,1,0:T(8,128)(2,1)}), bf16[8,1024,128]{2,1,0:T(8,128)(2,1)}, u32[]{:S(2)}, u32[]{:S(2)}) async-start(bf16[8,1024,128]{2,1,0:T(8,128)(2,1)} %broadcast_in_dim.2), calls=%async_computation.2 | async-start | bytes 4194304 | tf_op jit(solution)/shard_map/all_to_all | solution.py:667
  43.7 0.0 copy-done.9
  43.7 7.1 %shard_map.151 = (bf16[16,256,128]{2,1,0:T(8,128)(2,1)S(1)}, bf16[16,256,128]{2,1,0:T(8,128)(2,1)S(1)}, bf16[16,128,256]{2,1,0:T(8,128)(2,1)S(1)}, bf16[16,128,2...) custom-call(bf16[8,17,16,128]{3,2,1,0:T(8,128)(2,1)S(1)} %all-to-all-don, ...), custom_call_target="tpu_custom_call" | custom-call | tf_op jit(solution)/shard_map/pallas_call | solution.py:499
  50.8 1.0 copy-done.1
  51.8 1.0 copy-done.2
  52.8 0.0 copy-done.11
  52.8 13.1 %shard_map.152 = (f32[16,256,256]{2,1,0:T(8,128)}, f32[16,64,256]{2,1,0:T(8,128)S(1)}, f32[16,32,64]{2,1,0:T(8,128)S(1)}, f32[16,8,256]{2,1,0:T(8,128)S(1)}, f32[16,2,16,128]{3,2,1,0:T(8,128)}) custom-call(bf16[16,256,128]{2,1,0:T(8,128)(2,1)S(1)} %get-tuple-element.39.k2_ref, bf16[16,128,256]{2,1,0:T(8,128)(2,1)} %get-tuple-element.40.vt_ref, ...), custom_call_target="tpu_custom_call" | custom-call | tf_op jit(solution)/shard_map/pallas_call | solution.py:525
  65.9 0.0 copy-start.8
  65.9 5.3 %all-to-all-done.2 = bf16[8,1024,128]{2,1,0:T(8,128)(2,1)} async-done(((bf16[8,1024,128]{2,1,0:T(8,128)(2,1)}), bf16[8,1024,128]{2,1,0:T(8,128)(2,1)}, u32[]{:S(2)}, u32[]{:S(2)}) %all-to-all-start.2) | async-done | bytes 2097184 | tf_op jit(solution)/shard_map/all_to_all | solution.py:667
  71.2 1.9 %collective-permute-start.1 = (bf16[8,1024,128]{2,1,0:T(8,128)(2,1)}, bf16[8,1024,128]{2,1,0:T(8,128)(2,1)}, u32[]{:S(2)}, u32[]{:S(2)}) collective-permute-start(bf16[8,1024,128]{2,1,0:T(8,128)(2,1)} %all-to-all-done.2), channel_id=1, source_target_pairs={{0,8},{8,0},{16,24},{24,16},{32,40},{40,32},{48,56},{56,48},{64,72... | collective-permute-start | bytes 6291464 | tf_op jit(solution)/shard_map/ppermute | solution.py:672
  73.2 0.0 copy-done.16
  73.2 0.1 fusion.1
  73.2 0.1 copy.20
  73.3 0.1 copy.21
  73.4 0.1 copy.23
  73.5 0.1 copy.22
  73.6 3.4 %all-to-all-start.3 = ((f32[16,2,16,128]{3,2,1,0:T(8,128)}), f32[16,2,16,128]{3,2,1,0:T(8,128)S(1)}, u32[]{:S(2)}, u32[]{:S(2)}) async-start(f32[16,2,16,128]{3,2,1,0:T(8,128)} %get-tuple-element.50), calls=%async_computation.3 | async-start | bytes 524288 | tf_op jit(solution)/shard_map/all_to_all | solution.py:673
  77.1 0.1 fusion
  77.2 0.1 pad_maximum_fusion.1.cw_ref
  77.3 8.4 %all-to-all-done.3.c1_ref = f32[16,2,16,128]{3,2,1,0:T(8,128)S(1)} async-done(((f32[16,2,16,128]{3,2,1,0:T(8,128)}), f32[16,2,16,128]{3,2,1,0:T(8,128)S(1)}, u32[]{:S(2)}, u32[]{:S(2)}) %all-to-all-start.3) | async-done | bytes 262176 | tf_op jit(solution)/shard_map/all_to_all | solution.py:673
  85.7 1.2 shard_map.153
  86.9 12.1 %all_to_all.45.c2_ref = f32[16,32,128]{2,1,0:T(8,128)S(1)} all-to-all(f32[16,32,128]{2,1,0:T(8,128)S(1)} %shard_map.153), channel_id=1, replica_groups=mesh['depth'=16,'res'=8] {'depth'}, dimensions={0} | all-to-all | bytes 524288 | tf_op jit(solution)/shard_map/all_to_all | solution.py:675
  99.1 0.0 copy-done.12
  99.1 0.0 copy-done.13
  99.1 2.0 %shard_map.154 = (f32[16,32,64]{2,1,0:T(8,128)S(1)}, bf16[8,20,16,128]{3,2,1,0:T(8,128)(2,1)}) custom-call(f32[16,32,64]{2,1,0:T(8,128)S(1)} %get-tuple-element.47.m1_ref, f32[16,32,128]{2,1,0:T(8,128)S(1)} %all_to_all.45.c2_ref, bf16[16,32,128]{2,1,0:T(8,128)(2,1)S(1)} %get-tuple-element.38.own_ref.ownx_ref, bf16[64,256]{1,0:T(8,128)(2,1)S(1)} %pad_maximum_fusion.1.cw_ref, ...), custom_call_target="tpu_custom_call" | custom-call | tf_op jit(solution)/shard_map/pallas_call | solution.py:493
  101.1 0.0 copy-done.3
  101.1 7.9 %all-to-all-start.5 = ((bf16[8,20,16,128]{3,2,1,0:T(8,128)(2,1)}), bf16[8,20,16,128]{3,2,1,0:T(8,128)(2,1)S(1)}, u32[]{:S(2)}, u32[]{:S(2)}) async-start(bf16[8,20,16,128]{3,2,1,0:T(8,128)(2,1)} %get-tuple-element.51.own_ref), calls=%async_computation.5 | async-start | bytes 1310720 | tf_op jit(solution)/shard_map/all_to_all | solution.py:680
  109.0 8.6 %all-to-all-done.5.da_ref = bf16[8,20,16,128]{3,2,1,0:T(8,128)(2,1)S(1)} async-done(((bf16[8,20,16,128]{3,2,1,0:T(8,128)(2,1)}), bf16[8,20,16,128]{3,2,1,0:T(8,128)(2,1)S(1)}, u32[]{:S(2)}, u32[]{:S(2)}) %all-to-all-start.5) | async-done | bytes 655392 | tf_op jit(solution)/shard_map/all_to_all | solution.py:680
  117.6 0.0 collective-permute-done.1
  117.6 0.0 copy-done.7
  117.6 0.0 copy-done.8
  117.6 15.4 %shard_map.155 = (f32[16,32,64]{2,1,0:T(8,128)S(1)}, f32[16,32,64]{2,1,0:T(8,128)S(1)}, f32[16,16,128]{2,1,0:T(8,128)S(1)}) custom-call(s32[1]{0:T(128)} %bitcast.4.core_ref, bf16[8,20,16,128]{3,2,1,0:T(8,128)(2,1)S(1)} %all-to-all-done.5.da_ref, bf16[8,20,16,128]{3,2,1,0:T(8,128)(2,1)} %get-tuple-element.51.own_ref, ...), custom_call_target="tpu_custom_call" | custom-call | tf_op jit(solution)/shard_map/pallas_call | solution.py:548
  133.0 14.1 %all_to_all.46.e1_ref = f32[16,16,128]{2,1,0:T(8,128)S(1)} all-to-all(f32[16,16,128]{2,1,0:T(8,128)S(1)} %get-tuple-element.54), channel_id=1, replica_groups=mesh['depth'=16,'res'=8] {'depth'}, dimensions={0} | all-to-all | bytes 262144 | tf_op jit(solution)/shard_map/all_to_all | solution.py:686
  147.1 9.2 %shard_map.156 = (f32[16,32,64]{2,1,0:T(8,128)S(1)}, bf16[16,256,512]{2,1,0:T(8,128)(2,1)}, bf16[16,128,256]{2,1,0:T(8,128)(2,1)S(1)}, bf16[16,128,256]{2,1,0:T(8,128)(2,1)S(1)}, f32[16,16,256]{2,1,0:T(8,128)}) custom-call(f32[16,16,128]{2,1,0:T(8,128)S(1)} %all_to_all.46.e1_ref, f32[16,32,128]{2,1,0:T(8,128)S(1)} %all_to_all.45.c2_ref, ...), custom_call_target="tpu_custom_call" | custom-call | tf_op jit(solution)/shard_map/pallas_call | solution.py:580
  156.3 4.0 %all-to-all-start.7 = ((f32[16,16,256]{2,1,0:T(8,128)}), f32[16,16,256]{2,1,0:T(8,128)S(1)}, u32[]{:S(2)}, u32[]{:S(2)}) async-start(f32[16,16,256]{2,1,0:T(8,128)} %get-tuple-element.65), calls=%async_computation.7 | async-start | bytes 524288 | tf_op jit(solution)/shard_map/all_to_all | solution.py:690
  160.2 8.6 %shard_map.157 = (f32[16,32,64]{2,1,0:T(8,128)S(1)}, f32[8,16,16,128]{3,2,1,0:T(8,128)S(1)}) custom-call(f32[16,256,256]{2,1,0:T(8,128)} %get-tuple-element.46.p_ref, bf16[16,256,512]{2,1,0:T(8,128)(2,1)} %get-tuple-element.60.ds_ref, bf16[16,128,256]{2,1,0:T(8,128)(2,1)S(1)} %get-tuple-element.61.do_ref, ...), custom_call_target="tpu_custom_call" | custom-call | tf_op jit(solution)/shard_map/pallas_call | solution.py:603
  168.8 0.0 copy-start.4
  168.8 1.0 copy-done.4
  169.8 0.0 all-to-all-done.7.b_ref
  169.8 3.7 %all-to-all-start.8 = ((f32[8,16,16,128]{3,2,1,0:T(8,128)}), f32[8,16,16,128]{3,2,1,0:T(8,128)S(1)}, u32[]{:S(2)}, u32[]{:S(2)}) async-start(f32[8,16,16,128]{3,2,1,0:T(8,128)} %copy-done.4), calls=%async_computation.8 | async-start | bytes 2097152 | tf_op jit(solution)/shard_map/all_to_all | solution.py:693
  173.5 0.0 copy-done.6
  173.5 1.6 shard_map.159
  175.1 13.3 %all-to-all-done.8.f_ref = f32[8,16,16,128]{3,2,1,0:T(8,128)S(1)} async-done(((f32[8,16,16,128]{3,2,1,0:T(8,128)}), f32[8,16,16,128]{3,2,1,0:T(8,128)S(1)}, u32[]{:S(2)}, u32[]{:S(2)}) %all-to-all-start.8) | async-done | bytes 1048608 | tf_op jit(solution)/shard_map/all_to_all | solution.py:693
  188.4 1.1 shard_map.158
  (14 shorter events, 0.0 us)
Async XLA Ops:
  0.6 28.2 %copy-start = (bf16[32,16,128]{2,1,0:T(8,128)(2,1)S(1)}, bf16[32,16,128]{2,1,0:T(8,128)(2,1)}, u32[]{:S(2)}) copy-start(bf16[32,16,128]{2,1,0:T(8,128)(2,1)} %ct_ref.1) | copy-start | bytes 393220
  1.3 0.9 copy-start.10
  2.2 0.7 copy-start.14
  2.9 0.7 copy-start.15
  4.6 13.9 %all-to-all-start = ((bf16[8,17,16,128]{3,2,1,0:T(8,128)(2,1)}), bf16[8,17,16,128]{3,2,1,0:T(8,128)(2,1)S(1)}, u32[]{:S(2)}, u32[]{:S(2)}) async-start(bf16[8,17,16,128]{3,2,1,0:T(8,128)(2,1)} %get-tuple-element.36), calls=%async_computation | async-start | bytes 1114112 | tf_op jit(solution)/shard_map/all_to_all | solution.py:641
  11.5 17.3 %collective-permute-start = (bf16[16,32,128]{2,1,0:T(8,128)(2,1)S(1)}, bf16[16,32,128]{2,1,0:T(8,128)(2,1)S(1)}, u32[]{:S(2)}, u32[]{:S(2)}) collective-permute-start(bf16[16,32,128]{2,1,0:T(8,128)(2,1)S(1)} %bitcast.17), channel_id=1, source_target_pairs={{0,0},{1,16},{2,32},{3,48},{4,64},{5,80},{6,96},{7,112},{8,8},{9,2... | collective-permute-start | bytes 393224 | tf_op jit(solution)/shard_map/ppermute | solution.py:658
  13.0 0.9 copy-start.5
  18.6 19.0 %all-to-all-start.1 = ((f32[16,16,256]{2,1,0:T(8,128)}), f32[16,16,256]{2,1,0:T(8,128)S(1)}, u32[]{:S(2)}, u32[]{:S(2)}) async-start(f32[16,16,256]{2,1,0:T(8,128)} %shard_map.149), calls=%async_computation.1 | async-start | bytes 524288 | tf_op jit(solution)/shard_map/all_to_all | solution.py:663
  39.2 4.5 %copy-start.9 = (bf16[64,256]{1,0:T(8,128)(2,1)S(1)}, bf16[64,256]{1,0:T(8,128)(2,1)}, u32[]{:S(2)}) copy-start(bf16[64,256]{1,0:T(8,128)(2,1)} %win_ref.3) | copy-start | bytes 98308
  39.2 13.6 %copy-start.11 = (bf16[64,64]{1,0:T(8,128)(2,1)S(1)}, bf16[64,64]{1,0:T(8,128)(2,1)}, u32[]{:S(2)}) copy-start(bf16[64,64]{1,0:T(8,128)(2,1)} %wo_ref.3) | copy-start | bytes 24580
  39.2 32.0 %all-to-all-start.2 = ((bf16[8,1024,128]{2,1,0:T(8,128)(2,1)}), bf16[8,1024,128]{2,1,0:T(8,128)(2,1)}, u32[]{:S(2)}, u32[]{:S(2)}) async-start(bf16[8,1024,128]{2,1,0:T(8,128)(2,1)} %broadcast_in_dim.2), calls=%async_computation.2 | async-start | bytes 4194304 | tf_op jit(solution)/shard_map/all_to_all | solution.py:667
  50.8 1.0 copy-start.1
  51.8 1.0 copy-start.2
  52.8 20.4 %copy-start.16 = (bf16[64,144]{1,0:T(8,128)(2,1)S(1)}, bf16[64,144]{1,0:T(8,128)(2,1)}, u32[]{:S(2)}) copy-start(bf16[64,144]{1,0:T(8,128)(2,1)} %param.22) | copy-start | bytes 55300
  52.8 46.3 %copy-start.12 = (bf16[64,64]{1,0:T(8,128)(2,1)S(1)}, bf16[64,64]{1,0:T(8,128)(2,1)}, u32[]{:S(2)}) copy-start(bf16[64,64]{1,0:T(8,128)(2,1)} %wv_ref.3) | copy-start | bytes 24580
  52.8 46.3 %copy-start.13 = (bf16[64,64]{1,0:T(8,128)(2,1)S(1)}, bf16[64,64]{1,0:T(8,128)(2,1)}, u32[]{:S(2)}) copy-start(bf16[64,64]{1,0:T(8,128)(2,1)} %wt_ref.3) | copy-start | bytes 24580
  65.9 35.2 %copy-start.3 = (f32[16,64,256]{2,1,0:T(8,128)}, f32[16,64,256]{2,1,0:T(8,128)S(1)}, u32[]{:S(2)}) copy-start(f32[16,64,256]{2,1,0:T(8,128)S(1)} %get-tuple-element.57.o_ref) | copy-start | bytes 3145732
  65.9 51.7 %copy-start.7 = (bf16[1024,128]{1,0:T(8,128)(2,1)S(1)}, bf16[1024,128]{1,0:T(8,128)(2,1)}, u32[]{:S(2)}) copy-start(bf16[1024,128]{1,0:T(8,128)(2,1)} %w_ref.1) | copy-start | bytes 786436
  65.9 51.7 %copy-start.8 = (bf16[16,32,64]{2,1,0:T(8,128)(2,1)S(1)}, bf16[16,32,64]{2,1,0:T(8,128)(2,1)}, u32[]{:S(2)}) copy-start(bf16[16,32,64]{2,1,0:T(8,128)(2,1)} %adj_ref.1) | copy-start | bytes 196612
  71.2 46.4 %collective-permute-start.1 = (bf16[8,1024,128]{2,1,0:T(8,128)(2,1)}, bf16[8,1024,128]{2,1,0:T(8,128)(2,1)}, u32[]{:S(2)}, u32[]{:S(2)}) collective-permute-start(bf16[8,1024,128]{2,1,0:T(8,128)(2,1)} %all-to-all-done.2), channel_id=1, source_target_pairs={{0,8},{8,0},{16,24},{24,16},{32,40},{40,32},{48,56},{56,48},{64,72... | collective-permute-start | bytes 6291464 | tf_op jit(solution)/shard_map/ppermute | solution.py:672
  73.6 12.1 %all-to-all-start.3 = ((f32[16,2,16,128]{3,2,1,0:T(8,128)}), f32[16,2,16,128]{3,2,1,0:T(8,128)S(1)}, u32[]{:S(2)}, u32[]{:S(2)}) async-start(f32[16,2,16,128]{3,2,1,0:T(8,128)} %get-tuple-element.50), calls=%async_computation.3 | async-start | bytes 524288 | tf_op jit(solution)/shard_map/all_to_all | solution.py:673
  101.1 16.5 %all-to-all-start.5 = ((bf16[8,20,16,128]{3,2,1,0:T(8,128)(2,1)}), bf16[8,20,16,128]{3,2,1,0:T(8,128)(2,1)S(1)}, u32[]{:S(2)}, u32[]{:S(2)}) async-start(bf16[8,20,16,128]{3,2,1,0:T(8,128)(2,1)} %get-tuple-element.51.own_ref), calls=%async_computation.5 | async-start | bytes 1310720 | tf_op jit(solution)/shard_map/all_to_all | solution.py:680
  156.3 13.5 %all-to-all-start.7 = ((f32[16,16,256]{2,1,0:T(8,128)}), f32[16,16,256]{2,1,0:T(8,128)S(1)}, u32[]{:S(2)}, u32[]{:S(2)}) async-start(f32[16,16,256]{2,1,0:T(8,128)} %get-tuple-element.65), calls=%async_computation.7 | async-start | bytes 524288 | tf_op jit(solution)/shard_map/all_to_all | solution.py:690
  168.8 1.0 copy-start.4
  169.8 3.7 %copy-start.6 = (bf16[32,16,128]{2,1,0:T(8,128)(2,1)S(1)}, bf16[32,16,128]{2,1,0:T(8,128)(2,1)}, u32[]{:S(2)}) copy-start(bf16[32,16,128]{2,1,0:T(8,128)(2,1)} %pair_ref.3) | copy-start | bytes 393220
  169.8 18.6 %all-to-all-start.8 = ((f32[8,16,16,128]{3,2,1,0:T(8,128)}), f32[8,16,16,128]{3,2,1,0:T(8,128)S(1)}, u32[]{:S(2)}, u32[]{:S(2)}) async-start(f32[8,16,16,128]{3,2,1,0:T(8,128)} %copy-done.4), calls=%async_computation.8 | async-start | bytes 2097152 | tf_op jit(solution)/shard_map/all_to_all | solution.py:693

commit v4 on v3

--- a/solution.py
+++ b/solution.py
@@ -14,6 +14,7 @@
 NT = (((1,), (1,)), ((), ()))
 TN = (((0,), (0,)), ((), ()))
 GROUP = 4
+SMEM = pl.BlockSpec(memory_space=pltpu.SMEM)
 OWN_STEP = 8
 VMEM = pltpu.CompilerParams(vmem_limit_bytes=50 * 1024 * 1024)
 
@@ -92,6 +93,10 @@
         out_ref[k] = block
 
 
+def res_order(place_ref):
+    return [jnp.bitwise_xor(place_ref[1], k) for k in range(8)]
+
+
 def pack_kernel(x_ref, mask_ref, res_ref, count_ref, rows_ref, own_ref):
     seq = lax.broadcasted_iota(jnp.int32, (16, 32), 0)
     alive = (seq < count_ref[0]).astype(f32)
@@ -105,20 +110,24 @@
     own_ref[...] = cat([x.astype(f32), cat(cols, 0)], 2).astype(bf16)
     dense = cat([x[:, :16], x[:, 16:]], 2)
     plane = cat([live, jnp.zeros((16, 96), f32)], 1).astype(bf16)
-    for k in range(8):
-        rows_ref[k, 0:16] = dense
-        rows_ref[k, 16] = plane
+    rows_ref[0:16] = dense
+    rows_ref[16] = plane
 
 
 def unpack(p):
     return cat([p[:, :, :64], p[:, :, 64:]], 1).reshape(256, 64)
 
 
-def proj_kernel(
-    g_ref, plane_ref, own_ref, win_ref,
-    k2_ref, v2_ref, kt_ref, vt_ref, q_ref, gate_ref, live_ref,
-    wqg, wkvt, wkk, wvv,
-):
+def turn_kernel(ct_ref, turned_ref, out_ref):
+    for k in range(8):
+        out_ref[k, 0:512] = ct_ref[...].reshape(512, 128)
+        out_ref[k, 512:1024] = turned_ref[...].reshape(512, 128)
+
+
+def proj_kernel(*refs):
+    g_refs, plane_refs = refs[0:8], refs[8:16]
+    own_ref, win_ref, k2_ref, v2_ref, kt_ref, vt_ref, q_ref, gate_ref, live_ref = refs[16:25]
+    wqg, wkvt, wkk, wvv = refs[25:]
     s = pl.program_id(0)
 
     @pl.when(s == 0)
@@ -133,7 +142,7 @@
             one = w[:, at:at + 64]
             row = cat([one, one], 1)
             ref[...] = cat([row, row], 0).astype(bf16)
-        live_ref[...] = cat([plane_ref[k, 0, :, 0:32] for k in range(8)], 1)
+        live_ref[...] = cat([ref[0, :, 0:32] for ref in plane_refs], 1)
 
     lane = lax.broadcasted_iota(jnp.int32, (256, 128), 1)
     heads = head_mask(64, 256, 8, 32) * SCALE
@@ -143,7 +152,7 @@
         return jnp.where(lane < 64, hi, x - hi).astype(bf16)
 
     for u in range(GROUP):
-        xn, _ = norm_rows(unpack(g_ref[:, u].astype(f32)))
+        xn, _ = norm_rows(unpack(cat([ref[u][None] for ref in g_refs], 0).astype(f32)))
         x2 = pair2(xn)
         k2_ref[u] = two(mm(x2, wkk[...]))
         v2_ref[u] = two(mm(x2, wvv[...]))
@@ -158,7 +167,7 @@
 
 
 def row_fwd_kernel(
-    k2_ref, vt_ref, q_ref, gate_ref, live_ref, own_ref, bias_ref, wo_ref,
+    place_ref, k2_ref, vt_ref, q_ref, gate_ref, live_ref, own_ref, bias_ref, wo_ref,
     p_ref, o_ref, m1_ref, any_ref, c1_ref,
 ):
     s = pl.program_id(0)
@@ -166,13 +175,14 @@
     wo = wo_ref[...]
     wo2 = cat([wo, wo], 0)
     seq = lax.broadcasted_iota(jnp.int32, (16, 128), 0)
+    bias = cat([bias_ref[pl.ds(2 * at, 2)].reshape(32, 256) for at in res_order(place_ref)], 0)
     for u in range(GROUP):
         pick = (seq == s * GROUP + u).astype(bf16)
         live = mm(live_ref[...], pick, TN)
         k2 = k2_ref[u]
         qhi, qlo = q_ref[u, 0:64], q_ref[u, 64:128]
         logits = mm(k2, cat([qhi, qhi], 0)) + mm(k2[:, :64], qlo)
-        logits = logits + bias_ref[...].reshape(256, 256)
+        logits = logits + bias
         logits = jnp.where(cat([live, live], 1) > 0, logits, NEG)
         e = jnp.exp(logits - jnp.max(logits, 0, keepdims=True))
         p = e * (1.0 / jnp.sum(e, 0, keepdims=True))
@@ -276,12 +286,12 @@
 
 
 def outer_kernel(
-    core_ref, da_ref, own_ref, cta_ref, ctb_ref, cta2_ref, ctb2_ref, w_ref, m2_ref, c2_ref, m1_ref,
+    place_ref, da_ref, own_ref, cta_ref, ctb_ref, cta2_ref, ctb2_ref, w_ref, m2_ref, c2_ref, m1_ref,
     ownx_ref, adj_ref, cw_ref, wv_ref, wt_ref, g2_ref, dcg_ref, e1_ref,
     inv, turned, stage, res, lrs, wide, wf,
 ):
     step = pl.program_id(0)
-    core = core_ref[0]
+    core = place_ref[0] % 2
 
     @pl.when(step == 0)
     def _():
@@ -351,7 +361,7 @@
 
 
 def row_bwd_kernel(
-    e1_ref, c2_ref, m1_ref, own_ref, g2_ref, dcg_ref, cw_ref,
+    place_ref, e1_ref, c2_ref, m1_ref, own_ref, g2_ref, dcg_ref, cw_ref,
     p_ref, o_ref, v2_ref, gate_ref, any_ref, wo_ref,
     g1_ref, ds_ref, do_ref, dg_ref, bias_ref,
     g1s,
@@ -415,14 +425,15 @@
         lhi, llo = split(do_live)
         dp = mm(v2, cat([lhi, lhi], 0)) + mm(v2[:, :64], llo)
         ds = p_ref[u] * (dp - delta)
-        bias_ref[...] += ds.reshape(16, 16, 256)
+        for k, at in enumerate(res_order(place_ref)):
+            bias_ref[pl.ds(2 * at, 2)] += ds[32 * k:32 * k + 32].reshape(2, 16, 256)
         shi, slo = split(ds)
         ds_ref[u, :, 0:256] = shi
         ds_ref[u, :, 256:512] = slo
 
 
 def row_inputs_kernel(
-    p_ref, ds_ref, do_ref, dg_ref, q_ref, kt_ref, win_ref, dxo_ref, f_ref, wback, wown
+    place_ref, p_ref, ds_ref, do_ref, dg_ref, q_ref, kt_ref, win_ref, dxo_ref, f_ref, wback, wown
 ):
     @pl.when(pl.program_id(0) == 0)
     def _():
@@ -445,7 +456,9 @@
         phi, plo = split(p_ref[u])
         dv = mm(phi, do, NT) + mm(plo, cat([do[:64], zero], 0), NT)
         dx = mm2(cat([dk, dv], 1), wback[...]).reshape(8, 32, 64)
-        f_ref[:, u] = cat([dx[:, :16], dx[:, 16:]], 2)
+        dense = cat([dx[:, :16], dx[:, 16:]], 2)
+        for k, at in enumerate(res_order(place_ref)):
+            f_ref[at, u] = dense[k]
         qhi, qlo = split(dq)
         dxo = mm(cat([qhi, dg[:64], qlo, dg[64:]], 0), wown[...], TN)
         dxo_ref[u] = jnp.sum(dxo.reshape(8, 32, 64), 0)
@@ -500,8 +513,8 @@
         proj_kernel,
         grid=(16 // GROUP,),
         in_specs=[
-            pl.BlockSpec((8, GROUP, 16, 128), lambda s: (0, s, 0, 0)),
-            pl.BlockSpec((8, 1, 16, 128), lambda s: (0, 16, 0, 0)),
+            *[row((17, 16, 128)) for _ in range(8)],
+            *[pl.BlockSpec((1, 16, 128), lambda s: (16, 0, 0)) for _ in range(8)],
             row((16, 32, 128)), full((64, 256)),
         ],
         out_specs=[
@@ -518,15 +531,15 @@
             pltpu.VMEM((128, 128), bf16), pltpu.VMEM((128, 128), bf16),
         ],
         compiler_params=VMEM,
-    )(rows, rows, own, win)
-
-
-def row_forward(k2, vt, q, gate, live, own, bias, wo):
+    )(*rows, *rows, own, win)
+
+
+def row_forward(place, k2, vt, q, gate, live, own, bias, wo):
     return pl.pallas_call(
         row_fwd_kernel,
         grid=(16 // GROUP,),
         in_specs=[
-            row((16, 256, 128)), row((16, 128, 256)), row((16, 128, 256)), row((16, 64, 256)),
+            SMEM, row((16, 256, 128)), row((16, 128, 256)), row((16, 128, 256)), row((16, 64, 256)),
             full((16, 256)), row((16, 32, 128)), full((16, 16, 256)), full((64, 64)),
         ],
         out_specs=[
@@ -538,10 +551,10 @@
             sds((16, 2, 16, 128)),
         ],
         compiler_params=VMEM,
-    )(k2, vt, q, gate, live, own, bias, wo)
-
-
-def outer_product(core, ct, ct2, factors, dblock, w, m2, c2, m1, own, adj, cw, wvo, wtf):
+    )(place, k2, vt, q, gate, live, own, bias, wo)
+
+
+def outer_product(place, ct, ct2, factors, dblock, w, m2, c2, m1, own, adj, cw, wvo, wtf):
     half = OWN_STEP // 2
     one = pl.BlockSpec((8, 1, OWN_STEP, 16, 128), lambda s: (0, 0, s, 0, 0))
     two = pl.BlockSpec((8, 1, half, 32, 128), lambda s: (0, 1, s, 0, 0))
@@ -549,7 +562,7 @@
         outer_kernel,
         grid=(32 // OWN_STEP,),
         in_specs=[
-            pl.BlockSpec(memory_space=pltpu.SMEM),
+            SMEM,
             full((8, 20, 16, 128)),
             pl.BlockSpec((1, 20, 16, 128), lambda s: (0, 0, 0, 0)),
             one, two, one, two,
@@ -570,18 +583,18 @@
         ],
         compiler_params=VMEM,
     )(
-        core, factors, dblock, ct.reshape(8, 2, 32, 16, 128), ct.reshape(8, 2, 16, 32, 128),
+        place, factors, dblock, ct.reshape(8, 2, 32, 16, 128), ct.reshape(8, 2, 16, 32, 128),
         ct2.reshape(8, 2, 32, 16, 128), ct2.reshape(8, 2, 16, 32, 128), w, m2, c2, m1, own, adj,
         cw, wvo, wtf,
     )
 
 
-def row_backward(e1, c2, m1, own, g2, dcg, cw, p, o, v2, gate, any_live, wo):
+def row_backward(place, e1, c2, m1, own, g2, dcg, cw, p, o, v2, gate, any_live, wo):
     return pl.pallas_call(
         row_bwd_kernel,
         grid=(16 // GROUP,),
         in_specs=[
-            full((16, 16, 128)), full((16, 32, 128)), full((16, 32, 64)), full((16, 32, 128)),
+            SMEM, full((16, 16, 128)), full((16, 32, 128)), full((16, 32, 64)), full((16, 32, 128)),
             full((16, 32, 64)), full((16, 32, 64)), full((64, 256)),
             row((16, 256, 256)), row((16, 64, 256)), row((16, 256, 128)), row((16, 64, 256)),
             row((16, 8, 256)), full((64, 64)),
@@ -596,22 +609,22 @@
         ],
         scratch_shapes=[pltpu.VMEM((16, 32, 64), f32)],
         compiler_params=VMEM,
-    )(e1, c2, m1, own, g2, dcg, cw, p, o, v2, gate, any_live, wo)
-
-
-def row_inputs(p, ds, do, dg, q, kt, win):
+    )(place, e1, c2, m1, own, g2, dcg, cw, p, o, v2, gate, any_live, wo)
+
+
+def row_inputs(place, p, ds, do, dg, q, kt, win):
     return pl.pallas_call(
         row_inputs_kernel,
         grid=(16 // GROUP,),
         in_specs=[
-            row((16, 256, 256)), row((16, 256, 512)), row((16, 128, 256)), row((16, 128, 256)),
+            SMEM, row((16, 256, 256)), row((16, 256, 512)), row((16, 128, 256)), row((16, 128, 256)),
             row((16, 128, 256)), row((16, 128, 256)), full((64, 256)),
         ],
         out_specs=[row((16, 32, 64)), pl.BlockSpec((8, GROUP, 16, 128), lambda s: (0, s, 0, 0))],
         out_shape=[sds((16, 32, 64)), sds((8, 16, 16, 128))],
         scratch_shapes=[pltpu.VMEM((256, 64), bf16), pltpu.VMEM((256, 64), bf16)],
         compiler_params=VMEM,
-    )(p, ds, do, dg, q, kt, win)
+    )(place, p, ds, do, dg, q, kt, win)
 
 
 def body(
@@ -630,15 +643,17 @@
     adjoint_of_result_track,
     pairwise_cotangent,
 ):
-    smem = pl.BlockSpec(memory_space=pltpu.SMEM)
+    place = jnp.stack([lax.axis_index("depth"), lax.axis_index("res")]).astype(jnp.int32)
     vmem = pl.BlockSpec(memory_space=pltpu.VMEM)
     row_block, own = pl.pallas_call(
         pack_kernel,
-        in_specs=[vmem, vmem, vmem, smem],
-        out_shape=[sds((8, 17, 16, 128), bf16), sds((16, 32, 128), bf16)],
+        in_specs=[vmem, vmem, vmem, SMEM],
+        out_shape=[sds((17, 16, 128), bf16), sds((16, 32, 128), bf16)],
         compiler_params=VMEM,
     )(alignment_state, alignment_mask, residue_entry_mask.reshape(1, 32), sequence_live_count)
-    rows = lax.all_to_all(row_block, "res", 0, 0)
+    rows = [row_block] + [
+        lax.ppermute(row_block, "res", [(r, r ^ k) for r in range(8)]) for k in range(1, 8)
+    ]
     bias_block = whole_call(
         bias_kernel, sds((16, 16, 256)), pairwise_state, pairwise_bias_weights,
         scratch=[pltpu.VMEM((32, 16, 128), f32)],
@@ -656,17 +671,15 @@
     turned = pairwise_cotangent.transpose(1, 0, 2)
     perm = [(d * 8 + r, (2 * r + d % 2) * 8 + d // 2) for d in range(16) for r in range(8)]
     turned = lax.ppermute(turned, ("depth", "res"), perm)
-    both = cat([pairwise_cotangent.reshape(512, 128), turned.reshape(512, 128)], 0)
-    both = jnp.broadcast_to(both[None], (8, 1024, 128))
-
-    bias_block, rows = lax.optimization_barrier((bias_block, rows))
+    both = whole_call(turn_kernel, sds((8, 1024, 128), bf16), pairwise_cotangent, turned)
+
     bias = lax.all_to_all(bias_block, "depth", 0, 0)
+    bias, both, *rows = lax.optimization_barrier((bias, both, *rows))
     k2, v2, kt, vt, q, gate, live = project(rows, own, horizontal_intake_coefs)
-    bias, both = lax.optimization_barrier((bias, both))
     same_core = [[c + 2 * k for k in range(8)] for c in range(2)]
     ct = lax.all_to_all(both, "depth", 0, 0, axis_index_groups=same_core)
     p, o, m1, any_live, c1 = row_forward(
-        k2, vt, q, gate, live, own, bias, horizontal_readout_coefs
+        place, k2, vt, q, gate, live, own, bias, horizontal_readout_coefs
     )
     c1, ct = lax.optimization_barrier((c1, ct))
     ct2 = lax.ppermute(ct, "depth", [(d, d ^ 1) for d in range(16)])
@@ -678,17 +691,16 @@
         m1, c2, own, cw, vertical_readout_coefs, tensor_factor_coefs,
     )
     factors = lax.all_to_all(dblock, "res", 0, 0)
-    core = (lax.axis_index("depth") % 2).astype(jnp.int32).reshape(1)
     g2, dcg, e1 = outer_product(
-        core, ct, ct2, factors, dblock, outer_output_weights, m2, c2, m1, own,
+        place, ct, ct2, factors, dblock, outer_output_weights, m2, c2, m1, own,
         adjoint_of_result_track, cw, vertical_readout_coefs, tensor_factor_coefs,
     )
     e1 = lax.all_to_all(e1, "depth", 0, 0)
     g1, ds, do, dg, bblock = row_backward(
-        e1, c2, m1, own, g2, dcg, cw, p, o, v2, gate, any_live, horizontal_readout_coefs
+        place, e1, c2, m1, own, g2, dcg, cw, p, o, v2, gate, any_live, horizontal_readout_coefs
     )
     bsum = lax.all_to_all(bblock, "depth", 0, 0)
-    dxo, fblock = row_inputs(p, ds, do, dg, q, kt, horizontal_intake_coefs)
+    dxo, fblock = row_inputs(place, p, ds, do, dg, q, kt, horizontal_intake_coefs)
     fblock, bsum = lax.optimization_barrier((fblock, bsum))
     fsum = lax.all_to_all(fblock, "res", 0, 0)
     alignment_gradient = whole_call(final_rows_kernel, sds((16, 32, 64)), fsum, dxo, g1, own)

time: 191 us -> 185 us (0.969)
  waiting for transfers between devices: 47.1 us -> 24.3 us
  blocking collectives: 26.2 us -> 38.2 us
  starting transfers between devices: 42.4 us -> 47.2 us
    ppermute x0 -> x7, starting transfers between devices: none -> 14.2 us  [body(): lax.ppermute(row_block, 'res', [(r, r ^ k) for r in range(8)])]
    all_to_all x2 -> x0, starting transfers between devices: 13.9 us -> none  [the longest x1 7.93 us: body(): factors = lax.all_to_all(dblock, 'res', 0, 0)]
    all_to_all x0 -> x1, blocking collectives: none -> 12.8 us  [body(): factors = lax.all_to_all(dblock, 'res', 0, 0)]
    all_to_all x2 -> x0, waiting for transfers between devices: 11.4 us -> none  [the longest x1 8.57 us: body(): factors = lax.all_to_all(dblock, 'res', 0, 0)]
    all_to_all x1, waiting for transfers between devices: 8.63 us -> 0.01 us  [body(): bias = lax.all_to_all(bias_block, 'depth', 0, 0)]
    all_to_all x1, waiting for transfers between devices: 5.35 us -> 0.94 us  [body(): ct = lax.all_to_all(both, 'depth', 0, 0, axis_index_groups=same_core)]
    ppermute x1, starting transfers between devices: 1.94 us -> 5.51 us  [body(): ct2 = lax.ppermute(ct, 'depth', [(d, d ^ 1) for d in range(16)])]
    unnamed x36 -> x38, local copies, waits for them, and re-layouts: 7.92 us -> 9.79 us
  transfers between devices with their start and end apart: 9 -> 14, of which waited for: 6 -> 5; matrix products, arithmetic and copies ran while one was open for 1% -> 1% of each run, Pallas kernels for 19% -> 19%
where the time goes in v4:
time: 185 us; the launch traced here: 184 us
  Pallas kernels  61.9 us (33%)
  starting transfers between devices  47.2 us (26%)
  blocking collectives  38.2 us (21%)
  waiting for transfers between devices  24.3 us (13%)
  local copies, waits for them, and re-layouts  10.3 us (6%)
    pallas_call x1, Pallas kernels, outer_product(): pl.pallas_call(outer_kernel, grid=(32 // OWN_STEP,), in_specs=[SMEM, full...  15.4 us
    ppermute x7, starting transfers between devices, body(): lax.ppermute(row_block, 'res', [(r, r ^ k) for r in range(8)])  14.2 us
    all_to_all x1, blocking collectives, body(): e1 = lax.all_to_all(e1, 'depth', 0, 0)  13.3 us
    all_to_all x1, waiting for transfers between devices, body(): fsum = lax.all_to_all(fblock, 'res', 0, 0)  13.3 us
    pallas_call x1, Pallas kernels, row_forward(): pl.pallas_call(row_fwd_kernel, grid=(16 // GROUP,), in_specs=[SMEM, row((...  13.1 us
    all_to_all x1, blocking collectives, body(): factors = lax.all_to_all(dblock, 'res', 0, 0)  12.8 us
    all_to_all x1, blocking collectives, body(): c2 = lax.all_to_all(c2, 'depth', 0, 0)  12.1 us
    unnamed x38, local copies, waits for them, and re-layouts  9.79 us
  transfers between devices with their start and end apart: 14, of which 5 were waited for; matrix products, arithmetic and copies ran while one was open for 1% of the time, Pallas kernels for 19%

profile of v4, /device:TPU:1, one launch (start us, length us, event | category | flops | bytes accessed | tf_op | source)
XLA Modules:
  0.0 183.6 jit_solution(8494254335806617666)
XLA Ops:
  0.6 0.8 copy.19.wb_ref
  1.4 0.9 copy-done.6
  2.3 1.8 shard_map.149
  4.2 9.3 %all-to-all-start = ((f32[16,16,256]{2,1,0:T(8,128)}), f32[16,16,256]{2,1,0:T(8,128)S(1)}, u32[]{:S(2)}, u32[]{:S(2)}) async-start(f32[16,16,256]{2,1,0:T(8,128)} %shard_map.149), calls=%async_computation | async-start | bytes 524288 | tf_op jit(solution)/shard_map/all_to_all | solution.py:676
  13.4 0.9 copy.27
  14.4 0.7 collective-permute-start
  15.7 0.0 copy-start.11
  15.7 0.9 copy-done.11
  16.6 0.7 copy-done.15
  17.3 0.7 copy-done.16
  18.0 0.2 shard_map.151
  18.2 8.1 %collective-permute-start.7 = (bf16[17,16,128]{2,1,0:T(8,128)(2,1)S(1)}, bf16[17,16,128]{2,1,0:T(8,128)(2,1)S(1)}, u32[]{:S(2)}, u32[]{:S(2)}) collective-permute-start(bf16[17,16,128]{2,1,0:T(8,128)(2,1)S(1)} %get-tuple-element.43.refs_0_.refs_8_), channel_id=1, source_target_pairs={{0,7},{1,6},{2,5},{3,4},{4,3},{5,2},{6,1},{7,0},{8,15},{9,14},{10,... | collective-permute-start | bytes 208904 | tf_op jit(solution)/shard_map/ppermute | solution.py:655
  26.3 0.0 collective-permute-start.6
  26.3 1.1 collective-permute-start.5
  27.5 0.9 collective-permute-start.4
  28.4 0.0 collective-permute-done.7.refs_7_.refs_15_
  28.4 2.8 %collective-permute-start.3 = (bf16[17,16,128]{2,1,0:T(8,128)(2,1)S(1)}, bf16[17,16,128]{2,1,0:T(8,128)(2,1)S(1)}, u32[]{:S(2)}, u32[]{:S(2)}) collective-permute-start(bf16[17,16,128]{2,1,0:T(8,128)(2,1)S(1)} %get-tuple-element.43.refs_0_.refs_8_), channel_id=1, source_target_pairs={{0,3},{1,2},{2,1},{3,0},{4,7},{5,6},{6,5},{7,4},{8,11},{9,10},{10,... | collective-permute-start | bytes 208904 | tf_op jit(solution)/shard_map/ppermute | solution.py:655
  31.1 0.7 collective-permute-done.6.refs_6_.refs_14_
  31.9 1.3 collective-permute-start.2
  33.1 0.0 collective-permute-done.turned_ref
  33.1 0.0 collective-permute-start.1
  33.2 0.9 copy-done
  34.1 1.7 shard_map.150
  35.7 0.0 collective-permute-done.5.refs_5_.refs_13_
  35.7 0.0 collective-permute-done.4.refs_4_.refs_12_
  35.7 0.0 collective-permute-done.3.refs_3_.refs_11_
  35.7 0.8 collective-permute-done.2.refs_2_.refs_10_
  36.5 0.0 collective-permute-done.1.refs_1_.refs_9_
  36.5 0.0 all-to-all-done.bias_ref
  36.6 4.7 %all-to-all-start.1 = ((bf16[8,1024,128]{2,1,0:T(8,128)(2,1)}), bf16[8,1024,128]{2,1,0:T(8,128)(2,1)}, u32[]{:S(2)}, u32[]{:S(2)}) async-start(bf16[8,1024,128]{2,1,0:T(8,128)(2,1)} %shard_map.150), calls=%async_computation.1 | async-start | bytes 4194304 | tf_op jit(solution)/shard_map/all_to_all | solution.py:680
  41.3 0.1 pad_add_fusion.place_ref
  41.3 6.8 %shard_map.152 = (bf16[16,256,128]{2,1,0:T(8,128)(2,1)S(1)}, bf16[16,256,128]{2,1,0:T(8,128)(2,1)S(1)}, bf16[16,128,256]{2,1,0:T(8,128)(2,1)S(1)}, bf16[16,128,2...) custom-call(bf16[17,16,128]{2,1,0:T(8,128)(2,1)S(1)} %get-tuple-element., ...), custom_call_target="tpu_custom_call" | custom-call | tf_op jit(solution)/shard_map/pallas_call | solution.py:512
  48.2 1.0 copy-done.2
  49.2 1.0 copy-done.3
  50.2 13.1 %shard_map.153 = (f32[16,256,256]{2,1,0:T(8,128)}, f32[16,64,256]{2,1,0:T(8,128)S(1)}, f32[16,32,64]{2,1,0:T(8,128)S(1)}, f32[16,8,256]{2,1,0:T(8,128)S(1)}, f32[16,2,16,128]{3,2,1,0:T(8,128)}) custom-call(s32[2]{0:T(128)S(1)} %pad_add_fusion.place_ref, bf16[16,256,128]{2,1,0:T(8,128)(2,1)S(1)} %get-tuple-element.52.k2_ref, ...), custom_call_target="tpu_custom_call" | custom-call | tf_op jit(solution)/shard_map/pallas_call | solution.py:538
  63.3 1.0 copy-done.4
  64.3 0.9 all-to-all-done.1
  65.3 5.5 %collective-permute-start.8 = (bf16[8,1024,128]{2,1,0:T(8,128)(2,1)}, bf16[8,1024,128]{2,1,0:T(8,128)(2,1)}, u32[]{:S(2)}, u32[]{:S(2)}) collective-permute-start(bf16[8,1024,128]{2,1,0:T(8,128)(2,1)} %all-to-all-done.1), channel_id=1, source_target_pairs={{0,8},{8,0},{16,24},{24,16},{32,40},{40,32},{48,56},{56,48},{64,72... | collective-permute-start | bytes 6291464 | tf_op jit(solution)/shard_map/ppermute | solution.py:685
  70.8 0.0 copy-done.17
  70.8 0.1 fusion.1
  70.8 0.1 copy.21
  70.9 0.1 copy.22
  71.0 0.1 copy.24
  71.1 0.1 copy.23
  71.2 5.2 %all-to-all-start.2 = ((f32[16,2,16,128]{3,2,1,0:T(8,128)}), f32[16,2,16,128]{3,2,1,0:T(8,128)S(1)}, u32[]{:S(2)}, u32[]{:S(2)}) async-start(f32[16,2,16,128]{3,2,1,0:T(8,128)} %get-tuple-element.62), calls=%async_computation.2 | async-start | bytes 524288 | tf_op jit(solution)/shard_map/all_to_all | solution.py:686
  76.4 0.1 fusion
  76.5 0.1 pad_maximum_fusion.cw_ref
  76.6 8.5 %all-to-all-done.2.c1_ref = f32[16,2,16,128]{3,2,1,0:T(8,128)S(1)} async-done(((f32[16,2,16,128]{3,2,1,0:T(8,128)}), f32[16,2,16,128]{3,2,1,0:T(8,128)S(1)}, u32[]{:S(2)}, u32[]{:S(2)}) %all-to-all-start.2) | async-done | bytes 262176 | tf_op jit(solution)/shard_map/all_to_all | solution.py:686
  85.1 1.2 shard_map.154
  86.3 12.1 %all_to_all.40.c2_ref = f32[16,32,128]{2,1,0:T(8,128)S(1)} all-to-all(f32[16,32,128]{2,1,0:T(8,128)S(1)} %shard_map.154), channel_id=1, replica_groups=mesh['depth'=16,'res'=8] {'depth'}, dimensions={0} | all-to-all | bytes 524288 | tf_op jit(solution)/shard_map/all_to_all | solution.py:688
  98.4 1.2 shard_map.155
  99.6 12.8 %all_to_all.41.da_ref = bf16[8,20,16,128]{3,2,1,0:T(8,128)(2,1)S(1)} all-to-all(bf16[8,20,16,128]{3,2,1,0:T(8,128)(2,1)S(1)} %get-tuple-element.63.own_ref), channel_id=1, replica_groups=mesh['depth'=16,'res'=8] {'res'}, dimensions={0} | all-to-all | bytes 1310720 | tf_op jit(solution)/shard_map/all_to_all | solution.py:693
  112.3 0.0 collective-permute-done.8
  112.4 15.4 %shard_map.156 = (f32[16,32,64]{2,1,0:T(8,128)S(1)}, f32[16,32,64]{2,1,0:T(8,128)S(1)}, f32[16,16,128]{2,1,0:T(8,128)S(1)}) custom-call(s32[2]{0:T(128)S(1)} %pad_add_fusion.place_ref, bf16[8,20,16,128]{3,2,1,0:T(8,128)(2,1)S(1)} %all_to_all.41.da_ref, bf16[8,20,16,128]{3,2,1,0:T(8,128)(2,1)S(1)} %get-tuple-element.63.own_ref, ...), custom_call_target="tpu_custom_call" | custom-call | tf_op jit(solution)/shard_map/pallas_call | solution.py:561
  127.8 13.3 %all_to_all.42.e1_ref = f32[16,16,128]{2,1,0:T(8,128)S(1)} all-to-all(f32[16,16,128]{2,1,0:T(8,128)S(1)} %get-tuple-element.66), channel_id=1, replica_groups=mesh['depth'=16,'res'=8] {'depth'}, dimensions={0} | all-to-all | bytes 262144 | tf_op jit(solution)/shard_map/all_to_all | solution.py:698
  141.1 9.1 %shard_map.157 = (f32[16,32,64]{2,1,0:T(8,128)S(1)}, bf16[16,256,512]{2,1,0:T(8,128)(2,1)}, bf16[16,128,256]{2,1,0:T(8,128)(2,1)S(1)}, bf16[16,128,256]{2,1,0:T(8,128)(2,1)S(1)}, f32[16,16,256]{2,1,0:T(8,128)}) custom-call(s32[2]{0:T(128)S(1)} %pad_add_fusion.place_ref, f32[16,16,128]{2,1,0:T(8,128)S(1)} %all_to_all.42.e1_ref, ...), custom_call_target="tpu_custom_call" | custom-call | tf_op jit(solution)/shard_map/pallas_call | solution.py:593
  150.2 4.0 %all-to-all-start.6 = ((f32[16,16,256]{2,1,0:T(8,128)}), f32[16,16,256]{2,1,0:T(8,128)S(1)}, u32[]{:S(2)}, u32[]{:S(2)}) async-start(f32[16,16,256]{2,1,0:T(8,128)} %get-tuple-element.77), calls=%async_computation.6 | async-start | bytes 524288 | tf_op jit(solution)/shard_map/all_to_all | solution.py:702
  154.2 8.6 %shard_map.158 = (f32[16,32,64]{2,1,0:T(8,128)S(1)}, f32[8,16,16,128]{3,2,1,0:T(8,128)S(1)}) custom-call(s32[2]{0:T(128)S(1)} %pad_add_fusion.place_ref, f32[16,256,256]{2,1,0:T(8,128)} %get-tuple-element.58.p_ref, bf16[16,256,512]{2,1,0:T(8,128)(2,1)} %get-tuple-element.72.ds_ref, bf16[16,128,256]{2,1,0:T(8,128)(2,1)S(1)} %get-tuple-element.73.do_ref, ...), custom_call_target="tpu_custom_call" | custom-call | tf_op jit(solution)/shard_map/pallas_call | solution.py:616
  162.8 1.0 copy-done.5
  163.8 0.0 all-to-all-done.6.b_ref
  163.8 3.7 %all-to-all-start.7 = ((f32[8,16,16,128]{3,2,1,0:T(8,128)}), f32[8,16,16,128]{3,2,1,0:T(8,128)S(1)}, u32[]{:S(2)}, u32[]{:S(2)}) async-start(f32[8,16,16,128]{3,2,1,0:T(8,128)} %copy-done.5), calls=%async_computation.7 | async-start | bytes 2097152 | tf_op jit(solution)/shard_map/all_to_all | solution.py:705
  167.5 1.6 shard_map.160
  169.1 13.3 %all-to-all-done.7.f_ref = f32[8,16,16,128]{3,2,1,0:T(8,128)S(1)} async-done(((f32[8,16,16,128]{3,2,1,0:T(8,128)}), f32[8,16,16,128]{3,2,1,0:T(8,128)S(1)}, u32[]{:S(2)}, u32[]{:S(2)}) %all-to-all-start.7) | async-done | bytes 1048608 | tf_op jit(solution)/shard_map/all_to_all | solution.py:705
  182.4 1.1 shard_map.159
  (27 shorter events, 0.1 us)
Async XLA Ops:
  1.4 0.9 copy-start.6
  4.2 32.4 %all-to-all-start = ((f32[16,16,256]{2,1,0:T(8,128)}), f32[16,16,256]{2,1,0:T(8,128)S(1)}, u32[]{:S(2)}, u32[]{:S(2)}) async-start(f32[16,16,256]{2,1,0:T(8,128)} %shard_map.149), calls=%async_computation | async-start | bytes 524288 | tf_op jit(solution)/shard_map/all_to_all | solution.py:676
  14.4 18.8 %collective-permute-start = (bf16[16,32,128]{2,1,0:T(8,128)(2,1)S(1)}, bf16[16,32,128]{2,1,0:T(8,128)(2,1)S(1)}, u32[]{:S(2)}, u32[]{:S(2)}) collective-permute-start(bf16[16,32,128]{2,1,0:T(8,128)(2,1)S(1)} %bitcast.15), channel_id=1, source_target_pairs={{0,0},{1,16},{2,32},{3,48},{4,64},{5,80},{6,96},{7,112},{8,8},{9,2... | collective-permute-start | bytes 393224 | tf_op jit(solution)/shard_map/ppermute | solution.py:673
  15.7 0.9 copy-start.11
  16.6 0.7 copy-start.15
  17.3 0.7 copy-start.16
  18.2 10.2 %collective-permute-start.7 = (bf16[17,16,128]{2,1,0:T(8,128)(2,1)S(1)}, bf16[17,16,128]{2,1,0:T(8,128)(2,1)S(1)}, u32[]{:S(2)}, u32[]{:S(2)}) collective-permute-start(bf16[17,16,128]{2,1,0:T(8,128)(2,1)S(1)} %get-tuple-element.43.refs_0_.refs_8_), channel_id=1, source_target_pairs={{0,7},{1,6},{2,5},{3,4},{4,3},{5,2},{6,1},{7,0},{8,15},{9,14},{10,... | collective-permute-start | bytes 208904 | tf_op jit(solution)/shard_map/ppermute | solution.py:655
  26.3 5.6 %collective-permute-start.6 = (bf16[17,16,128]{2,1,0:T(8,128)(2,1)S(1)}, bf16[17,16,128]{2,1,0:T(8,128)(2,1)S(1)}, u32[]{:S(2)}, u32[]{:S(2)}) collective-permute-start(bf16[17,16,128]{2,1,0:T(8,128)(2,1)S(1)} %get-tuple-element.43.refs_0_.refs_8_), channel_id=1, source_target_pairs={{0,6},{1,7},{2,4},{3,5},{4,2},{5,3},{6,0},{7,1},{8,14},{9,15},{10,... | collective-permute-start | bytes 208904 | tf_op jit(solution)/shard_map/ppermute | solution.py:655
  26.3 9.4 %collective-permute-start.5 = (bf16[17,16,128]{2,1,0:T(8,128)(2,1)S(1)}, bf16[17,16,128]{2,1,0:T(8,128)(2,1)S(1)}, u32[]{:S(2)}, u32[]{:S(2)}) collective-permute-start(bf16[17,16,128]{2,1,0:T(8,128)(2,1)S(1)} %get-tuple-element.43.refs_0_.refs_8_), channel_id=1, source_target_pairs={{0,5},{1,4},{2,7},{3,6},{4,1},{5,0},{6,3},{7,2},{8,13},{9,12},{10,... | collective-permute-start | bytes 208904 | tf_op jit(solution)/shard_map/ppermute | solution.py:655
  27.5 8.3 %collective-permute-start.4 = (bf16[17,16,128]{2,1,0:T(8,128)(2,1)S(1)}, bf16[17,16,128]{2,1,0:T(8,128)(2,1)S(1)}, u32[]{:S(2)}, u32[]{:S(2)}) collective-permute-start(bf16[17,16,128]{2,1,0:T(8,128)(2,1)S(1)} %get-tuple-element.43.refs_0_.refs_8_), channel_id=1, source_target_pairs={{0,4},{1,5},{2,6},{3,7},{4,0},{5,1},{6,2},{7,3},{8,12},{9,13},{10,... | collective-permute-start | bytes 208904 | tf_op jit(solution)/shard_map/ppermute | solution.py:655
  28.4 7.4 %collective-permute-start.3 = (bf16[17,16,128]{2,1,0:T(8,128)(2,1)S(1)}, bf16[17,16,128]{2,1,0:T(8,128)(2,1)S(1)}, u32[]{:S(2)}, u32[]{:S(2)}) collective-permute-start(bf16[17,16,128]{2,1,0:T(8,128)(2,1)S(1)} %get-tuple-element.43.refs_0_.refs_8_), channel_id=1, source_target_pairs={{0,3},{1,2},{2,1},{3,0},{4,7},{5,6},{6,5},{7,4},{8,11},{9,10},{10,... | collective-permute-start | bytes 208904 | tf_op jit(solution)/shard_map/ppermute | solution.py:655
  31.9 4.7 %collective-permute-start.2 = (bf16[17,16,128]{2,1,0:T(8,128)(2,1)S(1)}, bf16[17,16,128]{2,1,0:T(8,128)(2,1)S(1)}, u32[]{:S(2)}, u32[]{:S(2)}) collective-permute-start(bf16[17,16,128]{2,1,0:T(8,128)(2,1)S(1)} %get-tuple-element.43.refs_0_.refs_8_), channel_id=1, source_target_pairs={{0,2},{1,3},{2,0},{3,1},{4,6},{5,7},{6,4},{7,5},{8,10},{9,11},{10,... | collective-permute-start | bytes 208904 | tf_op jit(solution)/shard_map/ppermute | solution.py:655
  33.1 3.4 %collective-permute-start.1 = (bf16[17,16,128]{2,1,0:T(8,128)(2,1)S(1)}, bf16[17,16,128]{2,1,0:T(8,128)(2,1)S(1)}, u32[]{:S(2)}, u32[]{:S(2)}) collective-permute-start(bf16[17,16,128]{2,1,0:T(8,128)(2,1)S(1)} %get-tuple-element.43.refs_0_.refs_8_), channel_id=1, source_target_pairs={{0,1},{1,0},{2,3},{3,2},{4,5},{5,4},{6,7},{7,6},{8,9},{9,8},{10,11... | collective-permute-start | bytes 208904 | tf_op jit(solution)/shard_map/ppermute | solution.py:655
  33.1 0.9 copy-start
  35.7 5.6 %copy-start.10 = (bf16[64,256]{1,0:T(8,128)(2,1)S(1)}, bf16[64,256]{1,0:T(8,128)(2,1)}, u32[]{:S(2)}) copy-start(bf16[64,256]{1,0:T(8,128)(2,1)} %win_ref.1) | copy-start | bytes 98308
  35.7 14.5 %copy-start.12 = (bf16[64,64]{1,0:T(8,128)(2,1)S(1)}, bf16[64,64]{1,0:T(8,128)(2,1)}, u32[]{:S(2)}) copy-start(bf16[64,64]{1,0:T(8,128)(2,1)} %wo_ref.3) | copy-start | bytes 24580
  36.6 28.7 %all-to-all-start.1 = ((bf16[8,1024,128]{2,1,0:T(8,128)(2,1)}), bf16[8,1024,128]{2,1,0:T(8,128)(2,1)}, u32[]{:S(2)}, u32[]{:S(2)}) async-start(bf16[8,1024,128]{2,1,0:T(8,128)(2,1)} %shard_map.150), calls=%async_computation.1 | async-start | bytes 4194304 | tf_op jit(solution)/shard_map/all_to_all | solution.py:680
  48.2 1.0 copy-start.2
  49.2 1.0 copy-start.3
  50.2 20.6 %copy-start.17 = (bf16[64,144]{1,0:T(8,128)(2,1)S(1)}, bf16[64,144]{1,0:T(8,128)(2,1)}, u32[]{:S(2)}) copy-start(bf16[64,144]{1,0:T(8,128)(2,1)} %param.22) | copy-start | bytes 55300
  50.2 48.2 %copy-start.13 = (bf16[64,64]{1,0:T(8,128)(2,1)S(1)}, bf16[64,64]{1,0:T(8,128)(2,1)}, u32[]{:S(2)}) copy-start(bf16[64,64]{1,0:T(8,128)(2,1)} %wv_ref.3) | copy-start | bytes 24580
  50.2 48.2 %copy-start.14 = (bf16[64,64]{1,0:T(8,128)(2,1)S(1)}, bf16[64,64]{1,0:T(8,128)(2,1)}, u32[]{:S(2)}) copy-start(bf16[64,64]{1,0:T(8,128)(2,1)} %wt_ref.3) | copy-start | bytes 24580
  63.3 1.0 copy-start.4
  64.3 48.0 %copy-start.8 = (bf16[1024,128]{1,0:T(8,128)(2,1)S(1)}, bf16[1024,128]{1,0:T(8,128)(2,1)}, u32[]{:S(2)}) copy-start(bf16[1024,128]{1,0:T(8,128)(2,1)} %w_ref.1) | copy-start | bytes 786436
  64.3 48.0 %copy-start.9 = (bf16[16,32,64]{2,1,0:T(8,128)(2,1)S(1)}, bf16[16,32,64]{2,1,0:T(8,128)(2,1)}, u32[]{:S(2)}) copy-start(bf16[16,32,64]{2,1,0:T(8,128)(2,1)} %adj_ref.1) | copy-start | bytes 196612
  65.3 47.1 %collective-permute-start.8 = (bf16[8,1024,128]{2,1,0:T(8,128)(2,1)}, bf16[8,1024,128]{2,1,0:T(8,128)(2,1)}, u32[]{:S(2)}, u32[]{:S(2)}) collective-permute-start(bf16[8,1024,128]{2,1,0:T(8,128)(2,1)} %all-to-all-done.1), channel_id=1, source_target_pairs={{0,8},{8,0},{16,24},{24,16},{32,40},{40,32},{48,56},{56,48},{64,72... | collective-permute-start | bytes 6291464 | tf_op jit(solution)/shard_map/ppermute | solution.py:685
  71.2 13.9 %all-to-all-start.2 = ((f32[16,2,16,128]{3,2,1,0:T(8,128)}), f32[16,2,16,128]{3,2,1,0:T(8,128)S(1)}, u32[]{:S(2)}, u32[]{:S(2)}) async-start(f32[16,2,16,128]{3,2,1,0:T(8,128)} %get-tuple-element.62), calls=%async_computation.2 | async-start | bytes 524288 | tf_op jit(solution)/shard_map/all_to_all | solution.py:686
  150.2 13.6 %all-to-all-start.6 = ((f32[16,16,256]{2,1,0:T(8,128)}), f32[16,16,256]{2,1,0:T(8,128)S(1)}, u32[]{:S(2)}, u32[]{:S(2)}) async-start(f32[16,16,256]{2,1,0:T(8,128)} %get-tuple-element.77), calls=%async_computation.6 | async-start | bytes 524288 | tf_op jit(solution)/shard_map/all_to_all | solution.py:702
  162.8 1.0 copy-start.5
  163.8 3.7 %copy-start.1 = (bf16[32,16,128]{2,1,0:T(8,128)(2,1)S(1)}, bf16[32,16,128]{2,1,0:T(8,128)(2,1)}, u32[]{:S(2)}) copy-start(bf16[32,16,128]{2,1,0:T(8,128)(2,1)} %ct_ref.3) | copy-start | bytes 393220
  163.8 3.7 %copy-start.7 = (bf16[32,16,128]{2,1,0:T(8,128)(2,1)S(1)}, bf16[32,16,128]{2,1,0:T(8,128)(2,1)}, u32[]{:S(2)}) copy-start(bf16[32,16,128]{2,1,0:T(8,128)(2,1)} %pair_ref.3) | copy-start | bytes 393220
  163.8 18.6 %all-to-all-start.7 = ((f32[8,16,16,128]{3,2,1,0:T(8,128)}), f32[8,16,16,128]{3,2,1,0:T(8,128)S(1)}, u32[]{:S(2)}, u32[]{:S(2)}) async-start(f32[8,16,16,128]{3,2,1,0:T(8,128)} %copy-done.5), calls=%async_computation.7 | async-start | bytes 2097152 | tf_op jit(solution)/shard_map/all_to_all | solution.py:705

commit v5 on v4

--- a/solution.py
+++ b/solution.py
@@ -13,10 +13,16 @@
 NN = (((1,), (0,)), ((), ()))
 NT = (((1,), (1,)), ((), ()))
 TN = (((0,), (0,)), ((), ()))
-GROUP = 4
+GROUP = 8
 SMEM = pl.BlockSpec(memory_space=pltpu.SMEM)
 OWN_STEP = 8
-VMEM = pltpu.CompilerParams(vmem_limit_bytes=50 * 1024 * 1024)
+def limit(mib):
+    return pltpu.CompilerParams(vmem_limit_bytes=mib * 1024 * 1024)
+
+
+VMEM = limit(50)
+LARGE = limit(60)
+SMALL = limit(50)
 
 
 def mm(a, b, dims=NN):
@@ -76,28 +82,24 @@
     return (a == b).astype(f32)
 
 
-def bias_kernel(pair_ref, wb_ref, out_ref, scr):
-    xn, _ = norm_rows(pair_ref[...].astype(f32).reshape(512, 128))
-    scr[...] = xn.reshape(32, 16, 128)
-    wbt = wb_ref[...].astype(f32).T
-    w2 = cat([wbt, wbt], 1).astype(bf16)
-    own = head_mask(8, 256, 1, 32)
-    rows = []
-    for j in range(16):
-        x2 = pair2(scr[:, j, :])
-        tiled = cat([x2] * 8, 0)
-        full = mm(w2, tiled, NT)
-        rows.append(jnp.sum(full * own, 0, keepdims=True))
-    block = cat(rows, 0)
-    for k in range(16):
-        out_ref[k] = block
-
-
-def res_order(place_ref):
-    return [jnp.bitwise_xor(place_ref[1], k) for k in range(8)]
-
-
-def pack_kernel(x_ref, mask_ref, res_ref, count_ref, rows_ref, own_ref):
+def prepare_kernel(
+    pair_hbm, wb_hbm, ct_hbm, x_hbm, mask_hbm, res_hbm, count_ref,
+    bias_ref, rows_ref, own_ref, turned_ref,
+    scr, pair_ref, wb_ref, ct_ref, x_ref, mask_ref, res_ref, sems,
+):
+    moves = [
+        pltpu.make_async_copy(src, dst, sems.at[k])
+        for k, (src, dst) in enumerate(
+            (
+                (x_hbm, x_ref), (mask_hbm, mask_ref), (res_hbm, res_ref), (ct_hbm, ct_ref),
+                (pair_hbm, pair_ref), (wb_hbm, wb_ref),
+            )
+        )
+    ]
+    for move in moves:
+        move.start()
+    for move in moves:
+        move.wait()
     seq = lax.broadcasted_iota(jnp.int32, (16, 32), 0)
     alive = (seq < count_ref[0]).astype(f32)
     live = mask_ref[...].astype(f32) * res_ref[...].astype(f32) * alive
@@ -108,10 +110,30 @@
         for k in range(16)
     ]
     own_ref[...] = cat([x.astype(f32), cat(cols, 0)], 2).astype(bf16)
-    dense = cat([x[:, :16], x[:, 16:]], 2)
-    plane = cat([live, jnp.zeros((16, 96), f32)], 1).astype(bf16)
-    rows_ref[0:16] = dense
-    rows_ref[16] = plane
+    rows_ref[0:16] = cat([x[:, :16], x[:, 16:]], 2)
+    rows_ref[16] = cat([live, jnp.zeros((16, 96), f32)], 1).astype(bf16)
+
+    scr[0] = ct_ref[...].astype(f32)
+    for j in range(16):
+        turned_ref[j] = scr[0, :, j, :].astype(bf16)
+
+    xn, _ = norm_rows(pair_ref[...].astype(f32).reshape(512, 128))
+    scr[1] = xn.reshape(32, 16, 128)
+    w2 = cat([wb_ref[...], wb_ref[...]], 1)
+    heads = head_mask(8, 256, 1, 32)
+    rows = []
+    for j in range(16):
+        x2 = pair2(scr[1, :, j, :])
+        tiled = cat([x2] * 8, 0)
+        full = mm(w2, tiled, NT)
+        rows.append(jnp.sum(full * heads, 0, keepdims=True))
+    block = cat(rows, 0)
+    for k in range(16):
+        bias_ref[k] = block
+
+
+def res_order(place_ref):
+    return [jnp.bitwise_xor(place_ref[1], k) for k in range(8)]
 
 
 def unpack(p):
@@ -151,19 +173,25 @@
         hi = x.astype(bf16).astype(f32)
         return jnp.where(lane < 64, hi, x - hi).astype(bf16)
 
-    for u in range(GROUP):
-        xn, _ = norm_rows(unpack(cat([ref[u][None] for ref in g_refs], 0).astype(f32)))
-        x2 = pair2(xn)
-        k2_ref[u] = two(mm(x2, wkk[...]))
-        v2_ref[u] = two(mm(x2, wvv[...]))
-        hi, lo = split(mm(wkvt[...], x2, NT))
+    every = range(GROUP)
+    x2s = [
+        pair2(norm_rows(unpack(cat([ref[u][None] for ref in g_refs], 0).astype(f32)))[0])
+        for u in every
+    ]
+    xos = [pair2(norm_rows(own_ref[u].astype(f32)[:, :64])[0]) for u in every]
+    ks = [mm(x2, wkk[...]) for x2 in x2s]
+    vs = [mm(x2, wvv[...]) for x2 in x2s]
+    kvts = [mm(wkvt[...], x2, NT) for x2 in x2s]
+    qgs = [mm(wqg[...], cat([xo] * 8, 0), NT) for xo in xos]
+    for u in every:
+        k2_ref[u] = two(ks[u])
+        v2_ref[u] = two(vs[u])
+        hi, lo = split(kvts[u])
         kt_ref[u] = cat([hi[:64], lo[:64]], 0)
         vt_ref[u] = cat([hi[64:], lo[64:]], 0)
-        xon, _ = norm_rows(own_ref[u].astype(f32)[:, :64])
-        qg = mm(wqg[...], cat([pair2(xon)] * 8, 0), NT)
-        qhi, qlo = split(qg[:64] * heads)
+        qhi, qlo = split(qgs[u][:64] * heads)
         q_ref[u] = cat([qhi, qlo], 0)
-        gate_ref[u] = jax.nn.sigmoid(qg[64:])
+        gate_ref[u] = jax.nn.sigmoid(qgs[u][64:])
 
 
 def row_fwd_kernel(
@@ -176,14 +204,19 @@
     wo2 = cat([wo, wo], 0)
     seq = lax.broadcasted_iota(jnp.int32, (16, 128), 0)
     bias = cat([bias_ref[pl.ds(2 * at, 2)].reshape(32, 256) for at in res_order(place_ref)], 0)
-    for u in range(GROUP):
+    every = range(GROUP)
+    alive, logit = [], []
+    for u in every:
         pick = (seq == s * GROUP + u).astype(bf16)
         live = mm(live_ref[...], pick, TN)
+        alive.append(live)
         k2 = k2_ref[u]
         qhi, qlo = q_ref[u, 0:64], q_ref[u, 64:128]
-        logits = mm(k2, cat([qhi, qhi], 0)) + mm(k2[:, :64], qlo)
-        logits = logits + bias
-        logits = jnp.where(cat([live, live], 1) > 0, logits, NEG)
+        logit.append(mm(k2, cat([qhi, qhi], 0)) + mm(k2[:, :64], qlo))
+    outs = []
+    for u in every:
+        live = alive[u]
+        logits = jnp.where(cat([live, live], 1) > 0, logit[u] + bias, NEG)
         e = jnp.exp(logits - jnp.max(logits, 0, keepdims=True))
         p = e * (1.0 / jnp.sum(e, 0, keepdims=True))
         p_ref[u] = p
@@ -192,9 +225,10 @@
         phi, plo = split(p)
         vt = vt_ref[u]
         first = mm(vt, phi)
-        o = (first[:64] + first[64:] + mm(vt[:64], plo)) * heads
-        o_ref[u] = o
-        ahi, alo = split(o * gate_ref[u])
+        outs.append((first[:64] + first[64:] + mm(vt[:64], plo)) * heads)
+    for u in every:
+        o_ref[u] = outs[u]
+        ahi, alo = split(outs[u] * gate_ref[u])
         y = mm(cat([ahi, alo], 0), wo2, TN)
         own = own_ref[u].astype(f32)
         m1 = own[:, :64] + jnp.sum(y.reshape(8, 32, 64), 0)
@@ -408,28 +442,37 @@
     heads = head_mask(64, 256, 8, 32)
     wo = wo_ref[...]
     wo2 = cat([wo, wo], 1)
-    for u in range(GROUP):
+    every = range(GROUP)
+    douts = []
+    for u in every:
         dm = g1s[s * GROUP + u]
         g1_ref[u] = dm
+        douts.append(mm(wo2, cat([pair2(dm)] * 8, 0), NT))
+    dos, deltas, dps = [], [], []
+    for u in every:
         o = o_ref[u]
-        v2 = v2_ref[u]
         gate = gate_ref[u]
-        dout = mm(wo2, cat([pair2(dm)] * 8, 0), NT)
-        hi, lo = split(dout * o * gate * (1.0 - gate))
+        hi, lo = split(douts[u] * o * gate * (1.0 - gate))
         dg_ref[u] = cat([hi, lo], 0)
-        do = dout * gate * heads
+        do = douts[u] * gate * heads
         hi, lo = split(do)
         do_ref[u] = cat([hi, lo], 0)
         do_live = do * any_ref[u, 0:1, :]
-        delta = jnp.sum(do_live * o, 0, keepdims=True)
-        lhi, llo = split(do_live)
-        dp = mm(v2, cat([lhi, lhi], 0)) + mm(v2[:, :64], llo)
-        ds = p_ref[u] * (dp - delta)
-        for k, at in enumerate(res_order(place_ref)):
-            bias_ref[pl.ds(2 * at, 2)] += ds[32 * k:32 * k + 32].reshape(2, 16, 256)
+        dos.append(do_live)
+        deltas.append(jnp.sum(do_live * o, 0, keepdims=True))
+    for u in every:
+        v2 = v2_ref[u]
+        lhi, llo = split(dos[u])
+        dps.append(mm(v2, cat([lhi, lhi], 0)) + mm(v2[:, :64], llo))
+    total = jnp.zeros((256, 256), f32)
+    for u in every:
+        ds = p_ref[u] * (dps[u] - deltas[u])
+        total = total + ds
         shi, slo = split(ds)
         ds_ref[u, :, 0:256] = shi
         ds_ref[u, :, 256:512] = slo
+    for k, at in enumerate(res_order(place_ref)):
+        bias_ref[pl.ds(2 * at, 2)] += total[32 * k:32 * k + 32].reshape(2, 16, 256)
 
 
 def row_inputs_kernel(
@@ -444,24 +487,31 @@
 
     heads = head_mask(64, 256, 8, 32) * SCALE
     zero = jnp.zeros((64, 256), bf16)
-    for u in range(GROUP):
+    every = range(GROUP)
+    dqs, dks, dvs = [], [], []
+    for u in every:
         shi, slo = ds_ref[u, :, 0:256], ds_ref[u, :, 256:512]
         kt = kt_ref[u]
         q = q_ref[u]
+        first = mm(kt, shi)
+        dqs.append((first[:64] + first[64:] + mm(kt[:64], slo)) * heads)
+        dks.append(mm(shi, q, NT) + mm(slo, cat([q[:64], zero], 0), NT))
+    for u in every:
         do = do_ref[u]
+        phi, plo = split(p_ref[u])
+        dvs.append(mm(phi, do, NT) + mm(plo, cat([do[:64], zero], 0), NT))
+    dxs = [mm2(cat([dks[u], dvs[u]], 1), wback[...]).reshape(8, 32, 64) for u in every]
+    dxos = []
+    for u in every:
         dg = dg_ref[u]
-        first = mm(kt, shi)
-        dq = (first[:64] + first[64:] + mm(kt[:64], slo)) * heads
-        dk = mm(shi, q, NT) + mm(slo, cat([q[:64], zero], 0), NT)
-        phi, plo = split(p_ref[u])
-        dv = mm(phi, do, NT) + mm(plo, cat([do[:64], zero], 0), NT)
-        dx = mm2(cat([dk, dv], 1), wback[...]).reshape(8, 32, 64)
-        dense = cat([dx[:, :16], dx[:, 16:]], 2)
-        for k, at in enumerate(res_order(place_ref)):
+        qhi, qlo = split(dqs[u])
+        dxos.append(mm(cat([qhi, dg[:64], qlo, dg[64:]], 0), wown[...], TN))
+    order = res_order(place_ref)
+    for u in every:
+        dense = cat([dxs[u][:, :16], dxs[u][:, 16:]], 2)
+        for k, at in enumerate(order):
             f_ref[at, u] = dense[k]
-        qhi, qlo = split(dq)
-        dxo = mm(cat([qhi, dg[:64], qlo, dg[64:]], 0), wown[...], TN)
-        dxo_ref[u] = jnp.sum(dxo.reshape(8, 32, 64), 0)
+        dxo_ref[u] = jnp.sum(dxos[u].reshape(8, 32, 64), 0)
 
 
 def final_rows_kernel(f_ref, dxo_ref, g1_ref, own_ref, out_ref):
@@ -475,8 +525,7 @@
 
 def final_pair_kernel(b_ref, pair_ref, wb_ref, ct_ref, out_ref, scr):
     total = jnp.sum(b_ref[...], 0)
-    wbt = wb_ref[...].astype(f32).T
-    w2 = cat([wbt, wbt], 0).astype(bf16)
+    w2 = cat([wb_ref[...], wb_ref[...]], 0)
     own = head_mask(8, 256, 1, 32)
     for j in range(16):
         wide = jnp.broadcast_to(total[j:j + 1, :], (8, 256)) * own
@@ -492,6 +541,10 @@
     return jax.ShapeDtypeStruct(shape, dtype)
 
 
+def far(shape, dtype=f32):
+    return pltpu.HBM(shape, dtype)
+
+
 def full(shape):
     zeros = (0,) * len(shape)
     return pl.BlockSpec(shape, lambda s: zeros)
@@ -522,7 +575,7 @@
             row((16, 128, 256)), row((16, 64, 256)), full((16, 256)),
         ],
         out_shape=[
-            sds((16, 256, 128), bf16), sds((16, 256, 128), bf16), sds((16, 128, 256), bf16),
+            sds((16, 256, 128), bf16), far((16, 256, 128), bf16), far((16, 128, 256), bf16),
             sds((16, 128, 256), bf16), sds((16, 128, 256), bf16), sds((16, 64, 256)),
             sds((16, 256), bf16),
         ],
@@ -547,7 +600,7 @@
             full((16, 2, 16, 128)),
         ],
         out_shape=[
-            sds((16, 256, 256)), sds((16, 64, 256)), sds((16, 32, 64)), sds((16, 8, 256)),
+            far((16, 256, 256)), far((16, 64, 256)), sds((16, 32, 64)), sds((16, 8, 256)),
             sds((16, 2, 16, 128)),
         ],
         compiler_params=VMEM,
@@ -604,11 +657,11 @@
             full((16, 16, 256)),
         ],
         out_shape=[
-            sds((16, 32, 64)), sds((16, 256, 512), bf16), sds((16, 128, 256), bf16),
+            sds((16, 32, 64)), far((16, 256, 512), bf16), sds((16, 128, 256), bf16),
             sds((16, 128, 256), bf16), sds((16, 16, 256)),
         ],
         scratch_shapes=[pltpu.VMEM((16, 32, 64), f32)],
-        compiler_params=VMEM,
+        compiler_params=SMALL,
     )(place, e1, c2, m1, own, g2, dcg, cw, p, o, v2, gate, any_live, wo)
 
 
@@ -623,7 +676,7 @@
         out_specs=[row((16, 32, 64)), pl.BlockSpec((8, GROUP, 16, 128), lambda s: (0, s, 0, 0))],
         out_shape=[sds((16, 32, 64)), sds((8, 16, 16, 128))],
         scratch_shapes=[pltpu.VMEM((256, 64), bf16), pltpu.VMEM((256, 64), bf16)],
-        compiler_params=VMEM,
+        compiler_params=SMALL,
     )(place, p, ds, do, dg, q, kt, win)
 
 
@@ -644,20 +697,29 @@
     pairwise_cotangent,
 ):
     place = jnp.stack([lax.axis_index("depth"), lax.axis_index("res")]).astype(jnp.int32)
-    vmem = pl.BlockSpec(memory_space=pltpu.VMEM)
-    row_block, own = pl.pallas_call(
-        pack_kernel,
-        in_specs=[vmem, vmem, vmem, SMEM],
-        out_shape=[sds((17, 16, 128), bf16), sds((16, 32, 128), bf16)],
-        compiler_params=VMEM,
-    )(alignment_state, alignment_mask, residue_entry_mask.reshape(1, 32), sequence_live_count)
+    hbm = pl.BlockSpec(memory_space=pltpu.HBM)
+    heads_first = pairwise_bias_weights.T
+    bias_block, row_block, own, turned = pl.pallas_call(
+        prepare_kernel,
+        in_specs=[hbm] * 6 + [SMEM],
+        out_shape=[
+            sds((16, 16, 256)), sds((17, 16, 128), bf16), sds((16, 32, 128), bf16),
+            sds((16, 32, 128), bf16),
+        ],
+        scratch_shapes=[
+            pltpu.VMEM((2, 32, 16, 128), f32), pltpu.VMEM((32, 16, 128), bf16),
+            pltpu.VMEM((8, 128), bf16), pltpu.VMEM((32, 16, 128), bf16),
+            pltpu.VMEM((16, 32, 64), bf16), pltpu.VMEM((16, 32), jnp.int32),
+            pltpu.VMEM((1, 32), jnp.int32), pltpu.SemaphoreType.DMA((6,)),
+        ],
+        compiler_params=LARGE,
+    )(
+        pairwise_state, heads_first, pairwise_cotangent, alignment_state,
+        alignment_mask, residue_entry_mask.reshape(1, 32), sequence_live_count,
+    )
     rows = [row_block] + [
         lax.ppermute(row_block, "res", [(r, r ^ k) for r in range(8)]) for k in range(1, 8)
     ]
-    bias_block = whole_call(
-        bias_kernel, sds((16, 16, 256)), pairwise_state, pairwise_bias_weights,
-        scratch=[pltpu.VMEM((32, 16, 128), f32)],
-    )
     cw = cat(
         [
             column_input_weights[:, :64],
@@ -668,7 +730,6 @@
         1,
     )
 
-    turned = pairwise_cotangent.transpose(1, 0, 2)
     perm = [(d * 8 + r, (2 * r + d % 2) * 8 + d // 2) for d in range(16) for r in range(8)]
     turned = lax.ppermute(turned, ("depth", "res"), perm)
     both = whole_call(turn_kernel, sds((8, 1024, 128), bf16), pairwise_cotangent, turned)
@@ -705,7 +766,7 @@
     fsum = lax.all_to_all(fblock, "res", 0, 0)
     alignment_gradient = whole_call(final_rows_kernel, sds((16, 32, 64)), fsum, dxo, g1, own)
     pair_grad = whole_call(
-        final_pair_kernel, sds((32, 16, 128)), bsum, pairwise_state, pairwise_bias_weights,
+        final_pair_kernel, sds((32, 16, 128)), bsum, pairwise_state, heads_first,
         pairwise_cotangent, scratch=[pltpu.VMEM((32, 16, 128), f32)],
     )
     return alignment_gradient, pair_grad

time: 185 us -> 181 us (0.978)
  waiting for transfers between devices: 24.3 us -> 34.3 us
  local copies, waits for them, and re-layouts: 10.3 us -> 2.46 us
  Pallas kernels: 61.9 us -> 54.5 us
  blocking collectives: 38.2 us -> 41 us
    all_to_all x1, waiting for transfers between devices: 0.94 us -> 10.2 us  [body(): ct = lax.all_to_all(both, 'depth', 0, 0, axis_index_groups=same_core)]
    unnamed x38 -> x28, local copies, waits for them, and re-layouts: 9.79 us -> 1.94 us
    pallas_call x1, Pallas kernels: 13.1 us -> 6.53 us  [row_forward(): pl.pallas_call(row_fwd_kernel, grid=(16 // GROUP,), in_specs=[SMEM, row((...]
    pallas_call x1, Pallas kernels: 0.23 us -> 3.13 us  [body(): pl.pallas_call(prepare_kernel, in_specs=[hbm] * 6 + [SMEM], out_shape=[sd...]
    all_to_all x1, blocking collectives: 12.8 us -> 15.2 us  [body(): factors = lax.all_to_all(dblock, 'res', 0, 0)]
    pallas_call x6 -> x5, Pallas kernels: 8.58 us -> 6.8 us  [whole_call(): pl.pallas_call(kernel, out_shape=out_shape, scratch_shapes=list(scratch),...]
  transfers between devices with their start and end apart: 14 -> 14, of which waited for: 5 -> 7; matrix products, arithmetic and copies ran while one was open for 1% -> 0% of each run, Pallas kernels for 19% -> 15%
where the time goes in v5:
time: 181 us; the launch traced here: 180 us
  Pallas kernels  54.5 us (30%)
  starting transfers between devices  46.5 us (26%)
  blocking collectives  41 us (23%)
  waiting for transfers between devices  34.3 us (19%)
  local copies, waits for them, and re-layouts  2.46 us (1%)
    pallas_call x1, Pallas kernels, outer_product(): pl.pallas_call(outer_kernel, grid=(32 // OWN_STEP,), in_specs=[SMEM, full...  15.5 us
    all_to_all x1, blocking collectives, body(): factors = lax.all_to_all(dblock, 'res', 0, 0)  15.2 us
    ppermute x7, starting transfers between devices, body(): lax.ppermute(row_block, 'res', [(r, r ^ k) for r in range(8)])  14.9 us
    all_to_all x1, blocking collectives, body(): e1 = lax.all_to_all(e1, 'depth', 0, 0)  13.6 us
    all_to_all x1, waiting for transfers between devices, body(): fsum = lax.all_to_all(fblock, 'res', 0, 0)  13.1 us
    all_to_all x1, blocking collectives, body(): c2 = lax.all_to_all(c2, 'depth', 0, 0)  12.1 us
    all_to_all x1, waiting for transfers between devices, body(): ct = lax.all_to_all(both, 'depth', 0, 0, axis_index_groups=same_core)  10.2 us
    all_to_all x1, starting transfers between devices, body(): bias = lax.all_to_all(bias_block, 'depth', 0, 0)  9.3 us
  transfers between devices with their start and end apart: 14, of which 7 were waited for; matrix products, arithmetic and copies ran while one was open for 0% of the time, Pallas kernels for 15%

profile of v5, /device:TPU:1, one launch (start us, length us, event | category | flops | bytes accessed | tf_op | source)
XLA Modules:
  0.0 180.3 jit_solution(5413155382887200358)
XLA Ops:
  1.3 3.1 %shard_map.149 = (f32[16,16,256]{2,1,0:T(8,128)}, bf16[17,16,128]{2,1,0:T(8,128)(2,1)}, bf16[16,32,128]{2,1,0:T(8,128)(2,1)}, bf16[16,32,128]{2,1,0:T(8,128)(2,1)}) custom-call(bf16[32,16,128]{2,1,0:T(8,128)(2,1)} %pair_ref.1, bf16[8,128]{1,0:T(8,128)(2,1)} %bitcast.12, bf16[32,16,128]{2,1,0:T(8,128)(2,1)} %ct_ref.3, bf16[16,32,64]{2,1,0:T(8,128)(2,1)} %x_hbm.1, ...), custom_call_target="tpu_custom_call" | custom-call | tf_op jit(solution)/shard_map/pallas_call | solution.py:702
  4.4 9.3 %all-to-all-start = ((f32[16,16,256]{2,1,0:T(8,128)}), f32[16,16,256]{2,1,0:T(8,128)S(1)}, u32[]{:S(2)}, u32[]{:S(2)}) async-start(f32[16,16,256]{2,1,0:T(8,128)} %get-tuple-element.44), calls=%async_computation | async-start | bytes 524288 | tf_op jit(solution)/shard_map/all_to_all | solution.py:737
  13.7 1.6 collective-permute-start
  15.3 7.2 %collective-permute-start.7 = (bf16[17,16,128]{2,1,0:T(8,128)(2,1)}, bf16[17,16,128]{2,1,0:T(8,128)(2,1)S(1)}, u32[]{:S(2)}, u32[]{:S(2)}) collective-permute-start(bf16[17,16,128]{2,1,0:T(8,128)(2,1)} %get-tuple-element.47.refs_0_.refs_8_), channel_id=1, source_target_pairs={{0,7},{1,6},{2,5},{3,4},{4,3},{5,2},{6,1},{7,0},{8,15},{9,14},{10,... | collective-permute-start | bytes 208904 | tf_op jit(solution)/shard_map/ppermute | solution.py:721
  22.5 0.0 collective-permute-start.6
  22.5 1.1 collective-permute-start.5
  23.6 0.9 collective-permute-start.4
  24.5 0.6 collective-permute-done.7.refs_7_.refs_15_
  25.2 3.8 %collective-permute-start.3 = (bf16[17,16,128]{2,1,0:T(8,128)(2,1)}, bf16[17,16,128]{2,1,0:T(8,128)(2,1)S(1)}, u32[]{:S(2)}, u32[]{:S(2)}) collective-permute-start(bf16[17,16,128]{2,1,0:T(8,128)(2,1)} %get-tuple-element.47.refs_0_.refs_8_), channel_id=1, source_target_pairs={{0,3},{1,2},{2,1},{3,0},{4,7},{5,6},{6,5},{7,4},{8,11},{9,10},{10,... | collective-permute-start | bytes 208904 | tf_op jit(solution)/shard_map/ppermute | solution.py:721
  29.0 0.0 collective-permute-done.6.refs_6_.refs_14_
  29.0 1.8 %collective-permute-start.2 = (bf16[17,16,128]{2,1,0:T(8,128)(2,1)}, bf16[17,16,128]{2,1,0:T(8,128)(2,1)S(1)}, u32[]{:S(2)}, u32[]{:S(2)}) collective-permute-start(bf16[17,16,128]{2,1,0:T(8,128)(2,1)} %get-tuple-element.47.refs_0_.refs_8_), channel_id=1, source_target_pairs={{0,2},{1,3},{2,0},{3,1},{4,6},{5,7},{6,4},{7,5},{8,10},{9,11},{10,... | collective-permute-start | bytes 208904 | tf_op jit(solution)/shard_map/ppermute | solution.py:721
  30.8 0.0 collective-permute-done.turned_ref
  30.8 0.0 collective-permute-start.1
  30.8 0.9 copy-done.2
  31.7 1.7 shard_map.150
  33.4 0.0 collective-permute-done.5.refs_5_.refs_13_
  33.4 0.0 collective-permute-done.4.refs_4_.refs_12_
  33.4 0.0 collective-permute-done.3.refs_3_.refs_11_
  33.4 0.4 collective-permute-done.2.refs_2_.refs_10_
  33.8 0.8 collective-permute-done.1.refs_1_.refs_9_
  34.7 0.0 all-to-all-done.bias_ref
  34.7 4.9 %all-to-all-start.1 = ((bf16[8,1024,128]{2,1,0:T(8,128)(2,1)}), bf16[8,1024,128]{2,1,0:T(8,128)(2,1)}, u32[]{:S(2)}, u32[]{:S(2)}) async-start(bf16[8,1024,128]{2,1,0:T(8,128)(2,1)} %shard_map.150), calls=%async_computation.1 | async-start | bytes 4194304 | tf_op jit(solution)/shard_map/all_to_all | solution.py:741
  39.6 0.1 pad_add_fusion.place_ref
  39.7 0.0 copy-done
  39.7 0.0 copy-done.5
  39.7 0.0 copy-done.8
  39.7 6.8 %shard_map.151 = (bf16[16,256,128]{2,1,0:T(8,128)(2,1)S(1)}, bf16[16,256,128]{2,1,0:T(8,128)(2,1)}, bf16[16,128,256]{2,1,0:T(8,128)(2,1)}, bf16[16,128,256]{2,1,...) custom-call(bf16[17,16,128]{2,1,0:T(8,128)(2,1)S(1)} %copy-done.5, ...), custom_call_target="tpu_custom_call" | custom-call | tf_op jit(solution)/shard_map/pallas_call | solution.py:565
  46.5 1.0 copy-done.1
  47.5 0.0 copy-done.9
  47.5 6.5 %shard_map.152 = (f32[16,256,256]{2,1,0:T(8,128)}, f32[16,64,256]{2,1,0:T(8,128)}, f32[16,32,64]{2,1,0:T(8,128)S(1)}, f32[16,8,256]{2,1,0:T(8,128)S(1)}, f32[16,2,16,128]{3,2,1,0:T(8,128)}) custom-call(s32[2]{0:T(128)S(1)} %pad_add_fusion.place_ref, bf16[16,256,128]{2,1,0:T(8,128)(2,1)S(1)} %get-tuple-element.56.k2_ref, ...), custom_call_target="tpu_custom_call" | custom-call | tf_op jit(solution)/shard_map/pallas_call | solution.py:591
  54.0 0.0 copy-start.6
  54.1 0.0 copy-start.7
  54.1 10.2 %all-to-all-done.1 = bf16[8,1024,128]{2,1,0:T(8,128)(2,1)} async-done(((bf16[8,1024,128]{2,1,0:T(8,128)(2,1)}), bf16[8,1024,128]{2,1,0:T(8,128)(2,1)}, u32[]{:S(2)}, u32[]{:S(2)}) %all-to-all-start.1) | async-done | bytes 2097184 | tf_op jit(solution)/shard_map/all_to_all | solution.py:741
  64.3 4.8 %collective-permute-start.8 = (bf16[8,1024,128]{2,1,0:T(8,128)(2,1)}, bf16[8,1024,128]{2,1,0:T(8,128)(2,1)}, u32[]{:S(2)}, u32[]{:S(2)}) collective-permute-start(bf16[8,1024,128]{2,1,0:T(8,128)(2,1)} %all-to-all-done.1), channel_id=1, source_target_pairs={{0,8},{8,0},{16,24},{24,16},{32,40},{40,32},{48,56},{56,48},{64,72... | collective-permute-start | bytes 6291464 | tf_op jit(solution)/shard_map/ppermute | solution.py:746
  69.1 0.1 fusion.1
  69.2 0.1 copy.16
  69.2 0.1 copy.17
  69.3 0.1 copy.19
  69.5 0.1 copy.18
  69.6 3.4 %all-to-all-start.2 = ((f32[16,2,16,128]{3,2,1,0:T(8,128)}), f32[16,2,16,128]{3,2,1,0:T(8,128)S(1)}, u32[]{:S(2)}, u32[]{:S(2)}) async-start(f32[16,2,16,128]{3,2,1,0:T(8,128)} %get-tuple-element.66), calls=%async_computation.2 | async-start | bytes 524288 | tf_op jit(solution)/shard_map/all_to_all | solution.py:747
  73.0 0.1 fusion
  73.1 0.1 pad_maximum_fusion.cw_ref
  73.2 8.4 %all-to-all-done.2.c1_ref = f32[16,2,16,128]{3,2,1,0:T(8,128)S(1)} async-done(((f32[16,2,16,128]{3,2,1,0:T(8,128)}), f32[16,2,16,128]{3,2,1,0:T(8,128)S(1)}, u32[]{:S(2)}, u32[]{:S(2)}) %all-to-all-start.2) | async-done | bytes 262176 | tf_op jit(solution)/shard_map/all_to_all | solution.py:747
  81.6 1.2 shard_map.153
  82.8 12.1 %all_to_all.40.c2_ref = f32[16,32,128]{2,1,0:T(8,128)S(1)} all-to-all(f32[16,32,128]{2,1,0:T(8,128)S(1)} %shard_map.153), channel_id=1, replica_groups=mesh['depth'=16,'res'=8] {'depth'}, dimensions={0} | all-to-all | bytes 524288 | tf_op jit(solution)/shard_map/all_to_all | solution.py:749
  95.0 0.0 copy-done.10
  95.0 1.2 shard_map.154
  96.2 15.2 %all_to_all.41.da_ref = bf16[8,20,16,128]{3,2,1,0:T(8,128)(2,1)S(1)} all-to-all(bf16[8,20,16,128]{3,2,1,0:T(8,128)(2,1)S(1)} %get-tuple-element.67.own_ref), channel_id=1, replica_groups=mesh['depth'=16,'res'=8] {'res'}, dimensions={0} | all-to-all | bytes 1310720 | tf_op jit(solution)/shard_map/all_to_all | solution.py:754
  111.4 0.0 collective-permute-done.8
  111.4 0.0 copy-done.6
  111.4 15.5 %shard_map.155 = (f32[16,32,64]{2,1,0:T(8,128)S(1)}, f32[16,32,64]{2,1,0:T(8,128)S(1)}, f32[16,16,128]{2,1,0:T(8,128)S(1)}) custom-call(s32[2]{0:T(128)S(1)} %pad_add_fusion.place_ref, bf16[8,20,16,128]{3,2,1,0:T(8,128)(2,1)S(1)} %all_to_all.41.da_ref, bf16[8,20,16,128]{3,2,1,0:T(8,128)(2,1)S(1)} %get-tuple-element.67.own_ref, ...), custom_call_target="tpu_custom_call" | custom-call | tf_op jit(solution)/shard_map/pallas_call | solution.py:614
  126.9 13.6 %all_to_all.42.e1_ref = f32[16,16,128]{2,1,0:T(8,128)S(1)} all-to-all(f32[16,16,128]{2,1,0:T(8,128)S(1)} %get-tuple-element.70), channel_id=1, replica_groups=mesh['depth'=16,'res'=8] {'depth'}, dimensions={0} | all-to-all | bytes 262144 | tf_op jit(solution)/shard_map/all_to_all | solution.py:759
  140.5 7.7 %shard_map.156 = (f32[16,32,64]{2,1,0:T(8,128)S(1)}, bf16[16,256,512]{2,1,0:T(8,128)(2,1)}, bf16[16,128,256]{2,1,0:T(8,128)(2,1)S(1)}, bf16[16,128,256]{2,1,0:T(8,128)(2,1)S(1)}, f32[16,16,256]{2,1,0:T(8,128)}) custom-call(s32[2]{0:T(128)S(1)} %pad_add_fusion.place_ref, f32[16,16,128]{2,1,0:T(8,128)S(1)} %all_to_all.42.e1_ref, ...), custom_call_target="tpu_custom_call" | custom-call | tf_op jit(solution)/shard_map/pallas_call | solution.py:646
  148.2 4.0 %all-to-all-start.6 = ((f32[16,16,256]{2,1,0:T(8,128)}), f32[16,16,256]{2,1,0:T(8,128)S(1)}, u32[]{:S(2)}, u32[]{:S(2)}) async-start(f32[16,16,256]{2,1,0:T(8,128)} %get-tuple-element.81), calls=%async_computation.6 | async-start | bytes 524288 | tf_op jit(solution)/shard_map/all_to_all | solution.py:763
  152.1 8.0 %shard_map.157 = (f32[16,32,64]{2,1,0:T(8,128)S(1)}, f32[8,16,16,128]{3,2,1,0:T(8,128)}) custom-call(s32[2]{0:T(128)S(1)} %pad_add_fusion.place_ref, f32[16,256,256]{2,1,0:T(8,128)} %get-tuple-element.62.p_ref, bf16[16,256,512]{2,1,0:T(8,128)(2,1)} %get-tuple-element.76.ds_ref, bf16[16,128,256]{2,1,0:T(8,128)(2,1)S(1)} %get-tuple-element.77.do_ref, ...), custom_call_target="tpu_custom_call" | custom-call | tf_op jit(solution)/shard_map/pallas_call | solution.py:669
  160.2 0.0 copy-start.12
  160.2 0.7 all-to-all-done.6.b_ref
  160.9 3.6 %all-to-all-start.7 = ((f32[8,16,16,128]{3,2,1,0:T(8,128)}), f32[8,16,16,128]{3,2,1,0:T(8,128)S(1)}, u32[]{:S(2)}, u32[]{:S(2)}) async-start(f32[8,16,16,128]{3,2,1,0:T(8,128)} %get-tuple-element.82), calls=%async_computation.7 | async-start | bytes 2097152 | tf_op jit(solution)/shard_map/all_to_all | solution.py:766
  164.4 0.0 copy-done.3
  164.5 0.0 copy-done.4
  164.5 0.0 copy-done.12
  164.5 1.6 shard_map.159
  166.1 13.1 %all-to-all-done.7.f_ref = f32[8,16,16,128]{3,2,1,0:T(8,128)S(1)} async-done(((f32[8,16,16,128]{3,2,1,0:T(8,128)}), f32[8,16,16,128]{3,2,1,0:T(8,128)S(1)}, u32[]{:S(2)}, u32[]{:S(2)}) %all-to-all-start.7) | async-done | bytes 1048608 | tf_op jit(solution)/shard_map/all_to_all | solution.py:766
  179.2 1.1 shard_map.158
  (16 shorter events, 0.0 us)
Async XLA Ops:
  4.4 30.3 %all-to-all-start = ((f32[16,16,256]{2,1,0:T(8,128)}), f32[16,16,256]{2,1,0:T(8,128)S(1)}, u32[]{:S(2)}, u32[]{:S(2)}) async-start(f32[16,16,256]{2,1,0:T(8,128)} %get-tuple-element.44), calls=%async_computation | async-start | bytes 524288 | tf_op jit(solution)/shard_map/all_to_all | solution.py:737
  13.7 17.1 %collective-permute-start = (bf16[16,32,128]{2,1,0:T(8,128)(2,1)}, bf16[16,32,128]{2,1,0:T(8,128)(2,1)S(1)}, u32[]{:S(2)}, u32[]{:S(2)}) collective-permute-start(bf16[16,32,128]{2,1,0:T(8,128)(2,1)} %get-tuple-element.45), channel_id=1, source_target_pairs={{0,0},{1,16},{2,32},{3,48},{4,64},{5,80},{6,96},{7,112},{8,8},{9,2... | collective-permute-start | bytes 393224 | tf_op jit(solution)/shard_map/ppermute | solution.py:734
  15.3 9.9 %collective-permute-start.7 = (bf16[17,16,128]{2,1,0:T(8,128)(2,1)}, bf16[17,16,128]{2,1,0:T(8,128)(2,1)S(1)}, u32[]{:S(2)}, u32[]{:S(2)}) collective-permute-start(bf16[17,16,128]{2,1,0:T(8,128)(2,1)} %get-tuple-element.47.refs_0_.refs_8_), channel_id=1, source_target_pairs={{0,7},{1,6},{2,5},{3,4},{4,3},{5,2},{6,1},{7,0},{8,15},{9,14},{10,... | collective-permute-start | bytes 208904 | tf_op jit(solution)/shard_map/ppermute | solution.py:721
  22.5 6.5 %collective-permute-start.6 = (bf16[17,16,128]{2,1,0:T(8,128)(2,1)}, bf16[17,16,128]{2,1,0:T(8,128)(2,1)S(1)}, u32[]{:S(2)}, u32[]{:S(2)}) collective-permute-start(bf16[17,16,128]{2,1,0:T(8,128)(2,1)} %get-tuple-element.47.refs_0_.refs_8_), channel_id=1, source_target_pairs={{0,6},{1,7},{2,4},{3,5},{4,2},{5,3},{6,0},{7,1},{8,14},{9,15},{10,... | collective-permute-start | bytes 208904 | tf_op jit(solution)/shard_map/ppermute | solution.py:721
  22.5 10.9 %collective-permute-start.5 = (bf16[17,16,128]{2,1,0:T(8,128)(2,1)}, bf16[17,16,128]{2,1,0:T(8,128)(2,1)S(1)}, u32[]{:S(2)}, u32[]{:S(2)}) collective-permute-start(bf16[17,16,128]{2,1,0:T(8,128)(2,1)} %get-tuple-element.47.refs_0_.refs_8_), channel_id=1, source_target_pairs={{0,5},{1,4},{2,7},{3,6},{4,1},{5,0},{6,3},{7,2},{8,13},{9,12},{10,... | collective-permute-start | bytes 208904 | tf_op jit(solution)/shard_map/ppermute | solution.py:721
  23.6 9.8 %collective-permute-start.4 = (bf16[17,16,128]{2,1,0:T(8,128)(2,1)}, bf16[17,16,128]{2,1,0:T(8,128)(2,1)S(1)}, u32[]{:S(2)}, u32[]{:S(2)}) collective-permute-start(bf16[17,16,128]{2,1,0:T(8,128)(2,1)} %get-tuple-element.47.refs_0_.refs_8_), channel_id=1, source_target_pairs={{0,4},{1,5},{2,6},{3,7},{4,0},{5,1},{6,2},{7,3},{8,12},{9,13},{10,... | collective-permute-start | bytes 208904 | tf_op jit(solution)/shard_map/ppermute | solution.py:721
  25.2 8.3 %collective-permute-start.3 = (bf16[17,16,128]{2,1,0:T(8,128)(2,1)}, bf16[17,16,128]{2,1,0:T(8,128)(2,1)S(1)}, u32[]{:S(2)}, u32[]{:S(2)}) collective-permute-start(bf16[17,16,128]{2,1,0:T(8,128)(2,1)} %get-tuple-element.47.refs_0_.refs_8_), channel_id=1, source_target_pairs={{0,3},{1,2},{2,1},{3,0},{4,7},{5,6},{6,5},{7,4},{8,11},{9,10},{10,... | collective-permute-start | bytes 208904 | tf_op jit(solution)/shard_map/ppermute | solution.py:721
  29.0 4.9 %collective-permute-start.2 = (bf16[17,16,128]{2,1,0:T(8,128)(2,1)}, bf16[17,16,128]{2,1,0:T(8,128)(2,1)S(1)}, u32[]{:S(2)}, u32[]{:S(2)}) collective-permute-start(bf16[17,16,128]{2,1,0:T(8,128)(2,1)} %get-tuple-element.47.refs_0_.refs_8_), channel_id=1, source_target_pairs={{0,2},{1,3},{2,0},{3,1},{4,6},{5,7},{6,4},{7,5},{8,10},{9,11},{10,... | collective-permute-start | bytes 208904 | tf_op jit(solution)/shard_map/ppermute | solution.py:721
  30.8 3.9 %collective-permute-start.1 = (bf16[17,16,128]{2,1,0:T(8,128)(2,1)}, bf16[17,16,128]{2,1,0:T(8,128)(2,1)S(1)}, u32[]{:S(2)}, u32[]{:S(2)}) collective-permute-start(bf16[17,16,128]{2,1,0:T(8,128)(2,1)} %get-tuple-element.47.refs_0_.refs_8_), channel_id=1, source_target_pairs={{0,1},{1,0},{2,3},{3,2},{4,5},{5,4},{6,7},{7,6},{8,9},{9,8},{10,11... | collective-permute-start | bytes 208904 | tf_op jit(solution)/shard_map/ppermute | solution.py:721
  30.8 0.9 copy-start.2
  33.4 6.3 %copy-start = (bf16[16,32,128]{2,1,0:T(8,128)(2,1)S(1)}, bf16[16,32,128]{2,1,0:T(8,128)(2,1)}, u32[]{:S(2)}) copy-start(bf16[16,32,128]{2,1,0:T(8,128)(2,1)} %get-tuple-element.55.refs_16_.own_ref.ownx_ref) | copy-start | bytes 393220
  33.4 6.3 %copy-start.5 = (bf16[17,16,128]{2,1,0:T(8,128)(2,1)S(1)}, bf16[17,16,128]{2,1,0:T(8,128)(2,1)}, u32[]{:S(2)}) copy-start(bf16[17,16,128]{2,1,0:T(8,128)(2,1)} %get-tuple-element.47.refs_0_.refs_8_) | copy-start | bytes 208900
  33.4 6.3 %copy-start.8 = (bf16[64,256]{1,0:T(8,128)(2,1)S(1)}, bf16[64,256]{1,0:T(8,128)(2,1)}, u32[]{:S(2)}) copy-start(bf16[64,256]{1,0:T(8,128)(2,1)} %win_ref.1) | copy-start | bytes 98308
  33.4 14.1 %copy-start.9 = (bf16[64,64]{1,0:T(8,128)(2,1)S(1)}, bf16[64,64]{1,0:T(8,128)(2,1)}, u32[]{:S(2)}) copy-start(bf16[64,64]{1,0:T(8,128)(2,1)} %wo_ref.3) | copy-start | bytes 24580
  34.7 29.6 %all-to-all-start.1 = ((bf16[8,1024,128]{2,1,0:T(8,128)(2,1)}), bf16[8,1024,128]{2,1,0:T(8,128)(2,1)}, u32[]{:S(2)}, u32[]{:S(2)}) async-start(bf16[8,1024,128]{2,1,0:T(8,128)(2,1)} %shard_map.150), calls=%async_computation.1 | async-start | bytes 4194304 | tf_op jit(solution)/shard_map/all_to_all | solution.py:741
  46.5 1.0 copy-start.1
  47.5 21.6 %copy-start.13 = (bf16[64,144]{1,0:T(8,128)(2,1)S(1)}, bf16[64,144]{1,0:T(8,128)(2,1)}, u32[]{:S(2)}) copy-start(bf16[64,144]{1,0:T(8,128)(2,1)} %param.22) | copy-start | bytes 55300
  47.5 47.5 %copy-start.10 = (bf16[64,64]{1,0:T(8,128)(2,1)S(1)}, bf16[64,64]{1,0:T(8,128)(2,1)}, u32[]{:S(2)}) copy-start(bf16[64,64]{1,0:T(8,128)(2,1)} %wv_ref.3) | copy-start | bytes 24580
  47.5 47.5 %copy-start.11 = (bf16[64,64]{1,0:T(8,128)(2,1)S(1)}, bf16[64,64]{1,0:T(8,128)(2,1)}, u32[]{:S(2)}) copy-start(bf16[64,64]{1,0:T(8,128)(2,1)} %wt_ref.3) | copy-start | bytes 24580
  54.0 57.3 %copy-start.6 = (bf16[1024,128]{1,0:T(8,128)(2,1)S(1)}, bf16[1024,128]{1,0:T(8,128)(2,1)}, u32[]{:S(2)}) copy-start(bf16[1024,128]{1,0:T(8,128)(2,1)} %w_ref.1) | copy-start | bytes 786436
  54.1 57.3 %copy-start.7 = (bf16[16,32,64]{2,1,0:T(8,128)(2,1)S(1)}, bf16[16,32,64]{2,1,0:T(8,128)(2,1)}, u32[]{:S(2)}) copy-start(bf16[16,32,64]{2,1,0:T(8,128)(2,1)} %adj_ref.1) | copy-start | bytes 196612
  64.3 47.1 %collective-permute-start.8 = (bf16[8,1024,128]{2,1,0:T(8,128)(2,1)}, bf16[8,1024,128]{2,1,0:T(8,128)(2,1)}, u32[]{:S(2)}, u32[]{:S(2)}) collective-permute-start(bf16[8,1024,128]{2,1,0:T(8,128)(2,1)} %all-to-all-done.1), channel_id=1, source_target_pairs={{0,8},{8,0},{16,24},{24,16},{32,40},{40,32},{48,56},{56,48},{64,72... | collective-permute-start | bytes 6291464 | tf_op jit(solution)/shard_map/ppermute | solution.py:746
  69.6 12.1 %all-to-all-start.2 = ((f32[16,2,16,128]{3,2,1,0:T(8,128)}), f32[16,2,16,128]{3,2,1,0:T(8,128)S(1)}, u32[]{:S(2)}, u32[]{:S(2)}) async-start(f32[16,2,16,128]{3,2,1,0:T(8,128)} %get-tuple-element.66), calls=%async_computation.2 | async-start | bytes 524288 | tf_op jit(solution)/shard_map/all_to_all | solution.py:747
  148.2 12.7 %all-to-all-start.6 = ((f32[16,16,256]{2,1,0:T(8,128)}), f32[16,16,256]{2,1,0:T(8,128)S(1)}, u32[]{:S(2)}, u32[]{:S(2)}) async-start(f32[16,16,256]{2,1,0:T(8,128)} %get-tuple-element.81), calls=%async_computation.6 | async-start | bytes 524288 | tf_op jit(solution)/shard_map/all_to_all | solution.py:763
  160.2 4.3 %copy-start.3 = (bf16[32,16,128]{2,1,0:T(8,128)(2,1)S(1)}, bf16[32,16,128]{2,1,0:T(8,128)(2,1)}, u32[]{:S(2)}) copy-start(bf16[32,16,128]{2,1,0:T(8,128)(2,1)} %ct_ref.3) | copy-start | bytes 393220
  160.2 4.3 %copy-start.4 = (bf16[32,16,128]{2,1,0:T(8,128)(2,1)S(1)}, bf16[32,16,128]{2,1,0:T(8,128)(2,1)}, u32[]{:S(2)}) copy-start(bf16[32,16,128]{2,1,0:T(8,128)(2,1)} %pair_ref.1) | copy-start | bytes 393220
  160.2 4.3 %copy-start.12 = (bf16[128,8]{0,1:T(8,128)(2,1)S(1)}, bf16[128,8]{0,1:T(8,128)(2,1)}, u32[]{:S(2)}) copy-start(bf16[128,8]{0,1:T(8,128)(2,1)} %param.20) | copy-start | bytes 6148
  160.9 18.3 %all-to-all-start.7 = ((f32[8,16,16,128]{3,2,1,0:T(8,128)}), f32[8,16,16,128]{3,2,1,0:T(8,128)S(1)}, u32[]{:S(2)}, u32[]{:S(2)}) async-start(f32[8,16,16,128]{3,2,1,0:T(8,128)} %get-tuple-element.82), calls=%async_computation.7 | async-start | bytes 2097152 | tf_op jit(solution)/shard_map/all_to_all | solution.py:766

commit v6 on v5

--- a/solution.py
+++ b/solution.py
@@ -468,9 +468,7 @@
     for u in every:
         ds = p_ref[u] * (dps[u] - deltas[u])
         total = total + ds
-        shi, slo = split(ds)
-        ds_ref[u, :, 0:256] = shi
-        ds_ref[u, :, 256:512] = slo
+        ds_ref[u] = ds
     for k, at in enumerate(res_order(place_ref)):
         bias_ref[pl.ds(2 * at, 2)] += total[32 * k:32 * k + 32].reshape(2, 16, 256)
 
@@ -490,7 +488,7 @@
     every = range(GROUP)
     dqs, dks, dvs = [], [], []
     for u in every:
-        shi, slo = ds_ref[u, :, 0:256], ds_ref[u, :, 256:512]
+        shi, slo = split(ds_ref[u])
         kt = kt_ref[u]
         q = q_ref[u]
         first = mm(kt, shi)
@@ -653,11 +651,11 @@
             row((16, 8, 256)), full((64, 64)),
         ],
         out_specs=[
-            row((16, 32, 64)), row((16, 256, 512)), row((16, 128, 256)), row((16, 128, 256)),
+            row((16, 32, 64)), row((16, 256, 256)), row((16, 128, 256)), row((16, 128, 256)),
             full((16, 16, 256)),
         ],
         out_shape=[
-            sds((16, 32, 64)), far((16, 256, 512), bf16), sds((16, 128, 256), bf16),
+            sds((16, 32, 64)), far((16, 256, 256)), sds((16, 128, 256), bf16),
             sds((16, 128, 256), bf16), sds((16, 16, 256)),
         ],
         scratch_shapes=[pltpu.VMEM((16, 32, 64), f32)],
@@ -670,7 +668,7 @@
         row_inputs_kernel,
         grid=(16 // GROUP,),
         in_specs=[
-            SMEM, row((16, 256, 256)), row((16, 256, 512)), row((16, 128, 256)), row((16, 128, 256)),
+            SMEM, row((16, 256, 256)), row((16, 256, 256)), row((16, 128, 256)), row((16, 128, 256)),
             row((16, 128, 256)), row((16, 128, 256)), full((64, 256)),
         ],
         out_specs=[row((16, 32, 64)), pl.BlockSpec((8, GROUP, 16, 128), lambda s: (0, s, 0, 0))],

time: 181 us -> 181 us (level)
  no operation moved by 1% of the time
where the time goes in v6:
time: 181 us; the launch traced here: 180 us
  Pallas kernels  54.3 us (30%)
  starting transfers between devices  46.5 us (26%)
  blocking collectives  41 us (23%)
  waiting for transfers between devices  34.3 us (19%)
  local copies, waits for them, and re-layouts  2.46 us (1%)
    pallas_call x1, Pallas kernels, outer_product(): pl.pallas_call(outer_kernel, grid=(32 // OWN_STEP,), in_specs=[SMEM, full...  15.5 us
    all_to_all x1, blocking collectives, body(): factors = lax.all_to_all(dblock, 'res', 0, 0)  15.2 us
    ppermute x7, starting transfers between devices, body(): lax.ppermute(row_block, 'res', [(r, r ^ k) for r in range(8)])  14.9 us
    all_to_all x1, blocking collectives, body(): e1 = lax.all_to_all(e1, 'depth', 0, 0)  13.6 us
    all_to_all x1, waiting for transfers between devices, body(): fsum = lax.all_to_all(fblock, 'res', 0, 0)  13.1 us
    all_to_all x1, blocking collectives, body(): c2 = lax.all_to_all(c2, 'depth', 0, 0)  12.1 us
    all_to_all x1, waiting for transfers between devices, body(): ct = lax.all_to_all(both, 'depth', 0, 0, axis_index_groups=same_core)  10.2 us
    all_to_all x1, starting transfers between devices, body(): bias = lax.all_to_all(bias_block, 'depth', 0, 0)  9.3 us
  transfers between devices with their start and end apart: 14, of which 7 were waited for; matrix products, arithmetic and copies ran while one was open for 0% of the time, Pallas kernels for 15%

profile of v6, /device:TPU:1, one launch (start us, length us, event | category | flops | bytes accessed | tf_op | source)
XLA Modules:
  0.0 180.1 jit_solution(1418671414906542296)
XLA Ops:
  1.3 3.1 %shard_map.149 = (f32[16,16,256]{2,1,0:T(8,128)}, bf16[17,16,128]{2,1,0:T(8,128)(2,1)}, bf16[16,32,128]{2,1,0:T(8,128)(2,1)}, bf16[16,32,128]{2,1,0:T(8,128)(2,1)}) custom-call(bf16[32,16,128]{2,1,0:T(8,128)(2,1)} %pair_ref.1, bf16[8,128]{1,0:T(8,128)(2,1)} %bitcast.12, bf16[32,16,128]{2,1,0:T(8,128)(2,1)} %ct_ref.3, bf16[16,32,64]{2,1,0:T(8,128)(2,1)} %x_hbm.1, ...), custom_call_target="tpu_custom_call" | custom-call | tf_op jit(solution)/shard_map/pallas_call | solution.py:700
  4.4 9.3 %all-to-all-start = ((f32[16,16,256]{2,1,0:T(8,128)}), f32[16,16,256]{2,1,0:T(8,128)S(1)}, u32[]{:S(2)}, u32[]{:S(2)}) async-start(f32[16,16,256]{2,1,0:T(8,128)} %get-tuple-element.44), calls=%async_computation | async-start | bytes 524288 | tf_op jit(solution)/shard_map/all_to_all | solution.py:735
  13.7 1.6 collective-permute-start
  15.3 7.2 %collective-permute-start.7 = (bf16[17,16,128]{2,1,0:T(8,128)(2,1)}, bf16[17,16,128]{2,1,0:T(8,128)(2,1)S(1)}, u32[]{:S(2)}, u32[]{:S(2)}) collective-permute-start(bf16[17,16,128]{2,1,0:T(8,128)(2,1)} %get-tuple-element.47.refs_0_.refs_8_), channel_id=1, source_target_pairs={{0,7},{1,6},{2,5},{3,4},{4,3},{5,2},{6,1},{7,0},{8,15},{9,14},{10,... | collective-permute-start | bytes 208904 | tf_op jit(solution)/shard_map/ppermute | solution.py:719
  22.5 0.0 collective-permute-start.6
  22.5 1.1 collective-permute-start.5
  23.6 0.9 collective-permute-start.4
  24.5 0.6 collective-permute-done.7.refs_7_.refs_15_
  25.2 3.8 %collective-permute-start.3 = (bf16[17,16,128]{2,1,0:T(8,128)(2,1)}, bf16[17,16,128]{2,1,0:T(8,128)(2,1)S(1)}, u32[]{:S(2)}, u32[]{:S(2)}) collective-permute-start(bf16[17,16,128]{2,1,0:T(8,128)(2,1)} %get-tuple-element.47.refs_0_.refs_8_), channel_id=1, source_target_pairs={{0,3},{1,2},{2,1},{3,0},{4,7},{5,6},{6,5},{7,4},{8,11},{9,10},{10,... | collective-permute-start | bytes 208904 | tf_op jit(solution)/shard_map/ppermute | solution.py:719
  29.0 0.0 collective-permute-done.6.refs_6_.refs_14_
  29.0 1.8 %collective-permute-start.2 = (bf16[17,16,128]{2,1,0:T(8,128)(2,1)}, bf16[17,16,128]{2,1,0:T(8,128)(2,1)S(1)}, u32[]{:S(2)}, u32[]{:S(2)}) collective-permute-start(bf16[17,16,128]{2,1,0:T(8,128)(2,1)} %get-tuple-element.47.refs_0_.refs_8_), channel_id=1, source_target_pairs={{0,2},{1,3},{2,0},{3,1},{4,6},{5,7},{6,4},{7,5},{8,10},{9,11},{10,... | collective-permute-start | bytes 208904 | tf_op jit(solution)/shard_map/ppermute | solution.py:719
  30.8 0.0 collective-permute-done.turned_ref
  30.8 0.0 collective-permute-start.1
  30.8 0.9 copy-done.2
  31.7 1.7 shard_map.150
  33.4 0.0 collective-permute-done.5.refs_5_.refs_13_
  33.4 0.0 collective-permute-done.4.refs_4_.refs_12_
  33.4 0.0 collective-permute-done.3.refs_3_.refs_11_
  33.4 0.4 collective-permute-done.2.refs_2_.refs_10_
  33.8 0.8 collective-permute-done.1.refs_1_.refs_9_
  34.7 0.0 all-to-all-done.bias_ref
  34.7 4.9 %all-to-all-start.1 = ((bf16[8,1024,128]{2,1,0:T(8,128)(2,1)}), bf16[8,1024,128]{2,1,0:T(8,128)(2,1)}, u32[]{:S(2)}, u32[]{:S(2)}) async-start(bf16[8,1024,128]{2,1,0:T(8,128)(2,1)} %shard_map.150), calls=%async_computation.1 | async-start | bytes 4194304 | tf_op jit(solution)/shard_map/all_to_all | solution.py:739
  39.6 0.1 pad_add_fusion.place_ref
  39.7 0.0 copy-done
  39.7 0.0 copy-done.5
  39.7 0.0 copy-done.8
  39.7 6.8 %shard_map.151 = (bf16[16,256,128]{2,1,0:T(8,128)(2,1)S(1)}, bf16[16,256,128]{2,1,0:T(8,128)(2,1)}, bf16[16,128,256]{2,1,0:T(8,128)(2,1)}, bf16[16,128,256]{2,1,...) custom-call(bf16[17,16,128]{2,1,0:T(8,128)(2,1)S(1)} %copy-done.5, ...), custom_call_target="tpu_custom_call" | custom-call | tf_op jit(solution)/shard_map/pallas_call | solution.py:563
  46.5 1.0 copy-done.1
  47.5 0.0 copy-done.9
  47.5 6.5 %shard_map.152 = (f32[16,256,256]{2,1,0:T(8,128)}, f32[16,64,256]{2,1,0:T(8,128)}, f32[16,32,64]{2,1,0:T(8,128)S(1)}, f32[16,8,256]{2,1,0:T(8,128)S(1)}, f32[16,2,16,128]{3,2,1,0:T(8,128)}) custom-call(s32[2]{0:T(128)S(1)} %pad_add_fusion.place_ref, bf16[16,256,128]{2,1,0:T(8,128)(2,1)S(1)} %get-tuple-element.56.k2_ref, ...), custom_call_target="tpu_custom_call" | custom-call | tf_op jit(solution)/shard_map/pallas_call | solution.py:589
  54.0 0.0 copy-start.6
  54.1 0.0 copy-start.7
  54.1 10.2 %all-to-all-done.1 = bf16[8,1024,128]{2,1,0:T(8,128)(2,1)} async-done(((bf16[8,1024,128]{2,1,0:T(8,128)(2,1)}), bf16[8,1024,128]{2,1,0:T(8,128)(2,1)}, u32[]{:S(2)}, u32[]{:S(2)}) %all-to-all-start.1) | async-done | bytes 2097184 | tf_op jit(solution)/shard_map/all_to_all | solution.py:739
  64.3 4.8 %collective-permute-start.8 = (bf16[8,1024,128]{2,1,0:T(8,128)(2,1)}, bf16[8,1024,128]{2,1,0:T(8,128)(2,1)}, u32[]{:S(2)}, u32[]{:S(2)}) collective-permute-start(bf16[8,1024,128]{2,1,0:T(8,128)(2,1)} %all-to-all-done.1), channel_id=1, source_target_pairs={{0,8},{8,0},{16,24},{24,16},{32,40},{40,32},{48,56},{56,48},{64,72... | collective-permute-start | bytes 6291464 | tf_op jit(solution)/shard_map/ppermute | solution.py:744
  69.1 0.1 fusion.1
  69.2 0.1 copy.16
  69.2 0.1 copy.17
  69.3 0.1 copy.19
  69.5 0.1 copy.18
  69.6 3.4 %all-to-all-start.2 = ((f32[16,2,16,128]{3,2,1,0:T(8,128)}), f32[16,2,16,128]{3,2,1,0:T(8,128)S(1)}, u32[]{:S(2)}, u32[]{:S(2)}) async-start(f32[16,2,16,128]{3,2,1,0:T(8,128)} %get-tuple-element.66), calls=%async_computation.2 | async-start | bytes 524288 | tf_op jit(solution)/shard_map/all_to_all | solution.py:745
  73.0 0.1 fusion
  73.1 0.1 pad_maximum_fusion.cw_ref
  73.2 8.4 %all-to-all-done.2.c1_ref = f32[16,2,16,128]{3,2,1,0:T(8,128)S(1)} async-done(((f32[16,2,16,128]{3,2,1,0:T(8,128)}), f32[16,2,16,128]{3,2,1,0:T(8,128)S(1)}, u32[]{:S(2)}, u32[]{:S(2)}) %all-to-all-start.2) | async-done | bytes 262176 | tf_op jit(solution)/shard_map/all_to_all | solution.py:745
  81.6 1.2 shard_map.153
  82.8 12.1 %all_to_all.40.c2_ref = f32[16,32,128]{2,1,0:T(8,128)S(1)} all-to-all(f32[16,32,128]{2,1,0:T(8,128)S(1)} %shard_map.153), channel_id=1, replica_groups=mesh['depth'=16,'res'=8] {'depth'}, dimensions={0} | all-to-all | bytes 524288 | tf_op jit(solution)/shard_map/all_to_all | solution.py:747
  95.0 0.0 copy-done.11
  95.0 1.2 shard_map.154
  96.2 15.2 %all_to_all.41.da_ref = bf16[8,20,16,128]{3,2,1,0:T(8,128)(2,1)S(1)} all-to-all(bf16[8,20,16,128]{3,2,1,0:T(8,128)(2,1)S(1)} %get-tuple-element.67.own_ref), channel_id=1, replica_groups=mesh['depth'=16,'res'=8] {'res'}, dimensions={0} | all-to-all | bytes 1310720 | tf_op jit(solution)/shard_map/all_to_all | solution.py:752
  111.4 0.0 collective-permute-done.8
  111.4 0.0 copy-done.7
  111.4 15.5 %shard_map.155 = (f32[16,32,64]{2,1,0:T(8,128)S(1)}, f32[16,32,64]{2,1,0:T(8,128)S(1)}, f32[16,16,128]{2,1,0:T(8,128)S(1)}) custom-call(s32[2]{0:T(128)S(1)} %pad_add_fusion.place_ref, bf16[8,20,16,128]{3,2,1,0:T(8,128)(2,1)S(1)} %all_to_all.41.da_ref, bf16[8,20,16,128]{3,2,1,0:T(8,128)(2,1)S(1)} %get-tuple-element.67.own_ref, ...), custom_call_target="tpu_custom_call" | custom-call | tf_op jit(solution)/shard_map/pallas_call | solution.py:612
  126.9 13.6 %all_to_all.42.e1_ref = f32[16,16,128]{2,1,0:T(8,128)S(1)} all-to-all(f32[16,16,128]{2,1,0:T(8,128)S(1)} %get-tuple-element.70), channel_id=1, replica_groups=mesh['depth'=16,'res'=8] {'depth'}, dimensions={0} | all-to-all | bytes 262144 | tf_op jit(solution)/shard_map/all_to_all | solution.py:757
  140.5 7.5 %shard_map.156 = (f32[16,32,64]{2,1,0:T(8,128)S(1)}, f32[16,256,256]{2,1,0:T(8,128)}, bf16[16,128,256]{2,1,0:T(8,128)(2,1)S(1)}, bf16[16,128,256]{2,1,0:T(8,128)(2,1)S(1)}, f32[16,16,256]{2,1,0:T(8,128)}) custom-call(s32[2]{0:T(128)S(1)} %pad_add_fusion.place_ref, f32[16,16,128]{2,1,0:T(8,128)S(1)} %all_to_all.42.e1_ref, ...), custom_call_target="tpu_custom_call" | custom-call | tf_op jit(solution)/shard_map/pallas_call | solution.py:644
  148.0 4.0 %all-to-all-start.6 = ((f32[16,16,256]{2,1,0:T(8,128)}), f32[16,16,256]{2,1,0:T(8,128)S(1)}, u32[]{:S(2)}, u32[]{:S(2)}) async-start(f32[16,16,256]{2,1,0:T(8,128)} %get-tuple-element.81), calls=%async_computation.6 | async-start | bytes 524288 | tf_op jit(solution)/shard_map/all_to_all | solution.py:761
  151.9 8.1 %shard_map.157 = (f32[16,32,64]{2,1,0:T(8,128)S(1)}, f32[8,16,16,128]{3,2,1,0:T(8,128)}) custom-call(s32[2]{0:T(128)S(1)} %pad_add_fusion.place_ref, f32[16,256,256]{2,1,0:T(8,128)} %get-tuple-element.62.p_ref, f32[16,256,256]{2,1,0:T(8,128)} %get-tuple-element.76.ds_ref, bf16[16,128,256]{2,1,0:T(8,128)(2,1)S(1)} %get-tuple-element.77.do_ref, ...), custom_call_target="tpu_custom_call" | custom-call | tf_op jit(solution)/shard_map/pallas_call | solution.py:667
  160.0 0.0 copy-start.12
  160.0 0.6 all-to-all-done.6.b_ref
  160.7 3.6 %all-to-all-start.7 = ((f32[8,16,16,128]{3,2,1,0:T(8,128)}), f32[8,16,16,128]{3,2,1,0:T(8,128)S(1)}, u32[]{:S(2)}, u32[]{:S(2)}) async-start(f32[8,16,16,128]{3,2,1,0:T(8,128)} %get-tuple-element.82), calls=%async_computation.7 | async-start | bytes 2097152 | tf_op jit(solution)/shard_map/all_to_all | solution.py:764
  164.2 0.0 copy-done.3
  164.3 0.0 copy-done.4
  164.3 0.0 copy-done.12
  164.3 1.6 shard_map.159
  165.9 13.1 %all-to-all-done.7.f_ref = f32[8,16,16,128]{3,2,1,0:T(8,128)S(1)} async-done(((f32[8,16,16,128]{3,2,1,0:T(8,128)}), f32[8,16,16,128]{3,2,1,0:T(8,128)S(1)}, u32[]{:S(2)}, u32[]{:S(2)}) %all-to-all-start.7) | async-done | bytes 1048608 | tf_op jit(solution)/shard_map/all_to_all | solution.py:764
  179.0 1.1 shard_map.158
  (16 shorter events, 0.0 us)
Async XLA Ops:
  4.4 30.3 %all-to-all-start = ((f32[16,16,256]{2,1,0:T(8,128)}), f32[16,16,256]{2,1,0:T(8,128)S(1)}, u32[]{:S(2)}, u32[]{:S(2)}) async-start(f32[16,16,256]{2,1,0:T(8,128)} %get-tuple-element.44), calls=%async_computation | async-start | bytes 524288 | tf_op jit(solution)/shard_map/all_to_all | solution.py:735
  13.7 17.1 %collective-permute-start = (bf16[16,32,128]{2,1,0:T(8,128)(2,1)}, bf16[16,32,128]{2,1,0:T(8,128)(2,1)S(1)}, u32[]{:S(2)}, u32[]{:S(2)}) collective-permute-start(bf16[16,32,128]{2,1,0:T(8,128)(2,1)} %get-tuple-element.45), channel_id=1, source_target_pairs={{0,0},{1,16},{2,32},{3,48},{4,64},{5,80},{6,96},{7,112},{8,8},{9,2... | collective-permute-start | bytes 393224 | tf_op jit(solution)/shard_map/ppermute | solution.py:732
  15.3 9.9 %collective-permute-start.7 = (bf16[17,16,128]{2,1,0:T(8,128)(2,1)}, bf16[17,16,128]{2,1,0:T(8,128)(2,1)S(1)}, u32[]{:S(2)}, u32[]{:S(2)}) collective-permute-start(bf16[17,16,128]{2,1,0:T(8,128)(2,1)} %get-tuple-element.47.refs_0_.refs_8_), channel_id=1, source_target_pairs={{0,7},{1,6},{2,5},{3,4},{4,3},{5,2},{6,1},{7,0},{8,15},{9,14},{10,... | collective-permute-start | bytes 208904 | tf_op jit(solution)/shard_map/ppermute | solution.py:719
  22.5 6.5 %collective-permute-start.6 = (bf16[17,16,128]{2,1,0:T(8,128)(2,1)}, bf16[17,16,128]{2,1,0:T(8,128)(2,1)S(1)}, u32[]{:S(2)}, u32[]{:S(2)}) collective-permute-start(bf16[17,16,128]{2,1,0:T(8,128)(2,1)} %get-tuple-element.47.refs_0_.refs_8_), channel_id=1, source_target_pairs={{0,6},{1,7},{2,4},{3,5},{4,2},{5,3},{6,0},{7,1},{8,14},{9,15},{10,... | collective-permute-start | bytes 208904 | tf_op jit(solution)/shard_map/ppermute | solution.py:719
  22.5 10.9 %collective-permute-start.5 = (bf16[17,16,128]{2,1,0:T(8,128)(2,1)}, bf16[17,16,128]{2,1,0:T(8,128)(2,1)S(1)}, u32[]{:S(2)}, u32[]{:S(2)}) collective-permute-start(bf16[17,16,128]{2,1,0:T(8,128)(2,1)} %get-tuple-element.47.refs_0_.refs_8_), channel_id=1, source_target_pairs={{0,5},{1,4},{2,7},{3,6},{4,1},{5,0},{6,3},{7,2},{8,13},{9,12},{10,... | collective-permute-start | bytes 208904 | tf_op jit(solution)/shard_map/ppermute | solution.py:719
  23.6 9.8 %collective-permute-start.4 = (bf16[17,16,128]{2,1,0:T(8,128)(2,1)}, bf16[17,16,128]{2,1,0:T(8,128)(2,1)S(1)}, u32[]{:S(2)}, u32[]{:S(2)}) collective-permute-start(bf16[17,16,128]{2,1,0:T(8,128)(2,1)} %get-tuple-element.47.refs_0_.refs_8_), channel_id=1, source_target_pairs={{0,4},{1,5},{2,6},{3,7},{4,0},{5,1},{6,2},{7,3},{8,12},{9,13},{10,... | collective-permute-start | bytes 208904 | tf_op jit(solution)/shard_map/ppermute | solution.py:719
  25.2 8.3 %collective-permute-start.3 = (bf16[17,16,128]{2,1,0:T(8,128)(2,1)}, bf16[17,16,128]{2,1,0:T(8,128)(2,1)S(1)}, u32[]{:S(2)}, u32[]{:S(2)}) collective-permute-start(bf16[17,16,128]{2,1,0:T(8,128)(2,1)} %get-tuple-element.47.refs_0_.refs_8_), channel_id=1, source_target_pairs={{0,3},{1,2},{2,1},{3,0},{4,7},{5,6},{6,5},{7,4},{8,11},{9,10},{10,... | collective-permute-start | bytes 208904 | tf_op jit(solution)/shard_map/ppermute | solution.py:719
  29.0 4.9 %collective-permute-start.2 = (bf16[17,16,128]{2,1,0:T(8,128)(2,1)}, bf16[17,16,128]{2,1,0:T(8,128)(2,1)S(1)}, u32[]{:S(2)}, u32[]{:S(2)}) collective-permute-start(bf16[17,16,128]{2,1,0:T(8,128)(2,1)} %get-tuple-element.47.refs_0_.refs_8_), channel_id=1, source_target_pairs={{0,2},{1,3},{2,0},{3,1},{4,6},{5,7},{6,4},{7,5},{8,10},{9,11},{10,... | collective-permute-start | bytes 208904 | tf_op jit(solution)/shard_map/ppermute | solution.py:719
  30.8 3.9 %collective-permute-start.1 = (bf16[17,16,128]{2,1,0:T(8,128)(2,1)}, bf16[17,16,128]{2,1,0:T(8,128)(2,1)S(1)}, u32[]{:S(2)}, u32[]{:S(2)}) collective-permute-start(bf16[17,16,128]{2,1,0:T(8,128)(2,1)} %get-tuple-element.47.refs_0_.refs_8_), channel_id=1, source_target_pairs={{0,1},{1,0},{2,3},{3,2},{4,5},{5,4},{6,7},{7,6},{8,9},{9,8},{10,11... | collective-permute-start | bytes 208904 | tf_op jit(solution)/shard_map/ppermute | solution.py:719
  30.8 0.9 copy-start.2
  33.4 6.3 %copy-start = (bf16[16,32,128]{2,1,0:T(8,128)(2,1)S(1)}, bf16[16,32,128]{2,1,0:T(8,128)(2,1)}, u32[]{:S(2)}) copy-start(bf16[16,32,128]{2,1,0:T(8,128)(2,1)} %get-tuple-element.55.refs_16_.own_ref.ownx_ref) | copy-start | bytes 393220
  33.4 6.3 %copy-start.5 = (bf16[17,16,128]{2,1,0:T(8,128)(2,1)S(1)}, bf16[17,16,128]{2,1,0:T(8,128)(2,1)}, u32[]{:S(2)}) copy-start(bf16[17,16,128]{2,1,0:T(8,128)(2,1)} %get-tuple-element.47.refs_0_.refs_8_) | copy-start | bytes 208900
  33.4 6.3 %copy-start.8 = (bf16[64,256]{1,0:T(8,128)(2,1)S(1)}, bf16[64,256]{1,0:T(8,128)(2,1)}, u32[]{:S(2)}) copy-start(bf16[64,256]{1,0:T(8,128)(2,1)} %win_ref.1) | copy-start | bytes 98308
  33.4 14.1 %copy-start.9 = (bf16[64,64]{1,0:T(8,128)(2,1)S(1)}, bf16[64,64]{1,0:T(8,128)(2,1)}, u32[]{:S(2)}) copy-start(bf16[64,64]{1,0:T(8,128)(2,1)} %wo_ref.3) | copy-start | bytes 24580
  34.7 29.6 %all-to-all-start.1 = ((bf16[8,1024,128]{2,1,0:T(8,128)(2,1)}), bf16[8,1024,128]{2,1,0:T(8,128)(2,1)}, u32[]{:S(2)}, u32[]{:S(2)}) async-start(bf16[8,1024,128]{2,1,0:T(8,128)(2,1)} %shard_map.150), calls=%async_computation.1 | async-start | bytes 4194304 | tf_op jit(solution)/shard_map/all_to_all | solution.py:739
  46.5 1.0 copy-start.1
  47.5 21.6 %copy-start.13 = (bf16[64,144]{1,0:T(8,128)(2,1)S(1)}, bf16[64,144]{1,0:T(8,128)(2,1)}, u32[]{:S(2)}) copy-start(bf16[64,144]{1,0:T(8,128)(2,1)} %param.22) | copy-start | bytes 55300
  47.5 47.5 %copy-start.10 = (bf16[64,64]{1,0:T(8,128)(2,1)S(1)}, bf16[64,64]{1,0:T(8,128)(2,1)}, u32[]{:S(2)}) copy-start(bf16[64,64]{1,0:T(8,128)(2,1)} %wv_ref.3) | copy-start | bytes 24580
  47.5 47.5 %copy-start.11 = (bf16[64,64]{1,0:T(8,128)(2,1)S(1)}, bf16[64,64]{1,0:T(8,128)(2,1)}, u32[]{:S(2)}) copy-start(bf16[64,64]{1,0:T(8,128)(2,1)} %wt_ref.3) | copy-start | bytes 24580
  54.0 57.3 %copy-start.6 = (bf16[1024,128]{1,0:T(8,128)(2,1)S(1)}, bf16[1024,128]{1,0:T(8,128)(2,1)}, u32[]{:S(2)}) copy-start(bf16[1024,128]{1,0:T(8,128)(2,1)} %w_ref.1) | copy-start | bytes 786436
  54.1 57.3 %copy-start.7 = (bf16[16,32,64]{2,1,0:T(8,128)(2,1)S(1)}, bf16[16,32,64]{2,1,0:T(8,128)(2,1)}, u32[]{:S(2)}) copy-start(bf16[16,32,64]{2,1,0:T(8,128)(2,1)} %adj_ref.1) | copy-start | bytes 196612
  64.3 47.1 %collective-permute-start.8 = (bf16[8,1024,128]{2,1,0:T(8,128)(2,1)}, bf16[8,1024,128]{2,1,0:T(8,128)(2,1)}, u32[]{:S(2)}, u32[]{:S(2)}) collective-permute-start(bf16[8,1024,128]{2,1,0:T(8,128)(2,1)} %all-to-all-done.1), channel_id=1, source_target_pairs={{0,8},{8,0},{16,24},{24,16},{32,40},{40,32},{48,56},{56,48},{64,72... | collective-permute-start | bytes 6291464 | tf_op jit(solution)/shard_map/ppermute | solution.py:744
  69.6 12.1 %all-to-all-start.2 = ((f32[16,2,16,128]{3,2,1,0:T(8,128)}), f32[16,2,16,128]{3,2,1,0:T(8,128)S(1)}, u32[]{:S(2)}, u32[]{:S(2)}) async-start(f32[16,2,16,128]{3,2,1,0:T(8,128)} %get-tuple-element.66), calls=%async_computation.2 | async-start | bytes 524288 | tf_op jit(solution)/shard_map/all_to_all | solution.py:745
  148.0 12.7 %all-to-all-start.6 = ((f32[16,16,256]{2,1,0:T(8,128)}), f32[16,16,256]{2,1,0:T(8,128)S(1)}, u32[]{:S(2)}, u32[]{:S(2)}) async-start(f32[16,16,256]{2,1,0:T(8,128)} %get-tuple-element.81), calls=%async_computation.6 | async-start | bytes 524288 | tf_op jit(solution)/shard_map/all_to_all | solution.py:761
  160.0 4.2 %copy-start.3 = (bf16[32,16,128]{2,1,0:T(8,128)(2,1)S(1)}, bf16[32,16,128]{2,1,0:T(8,128)(2,1)}, u32[]{:S(2)}) copy-start(bf16[32,16,128]{2,1,0:T(8,128)(2,1)} %ct_ref.3) | copy-start | bytes 393220
  160.0 4.2 %copy-start.4 = (bf16[32,16,128]{2,1,0:T(8,128)(2,1)S(1)}, bf16[32,16,128]{2,1,0:T(8,128)(2,1)}, u32[]{:S(2)}) copy-start(bf16[32,16,128]{2,1,0:T(8,128)(2,1)} %pair_ref.1) | copy-start | bytes 393220
  160.0 4.2 %copy-start.12 = (bf16[128,8]{0,1:T(8,128)(2,1)S(1)}, bf16[128,8]{0,1:T(8,128)(2,1)}, u32[]{:S(2)}) copy-start(bf16[128,8]{0,1:T(8,128)(2,1)} %param.20) | copy-start | bytes 6148
  160.7 18.3 %all-to-all-start.7 = ((f32[8,16,16,128]{3,2,1,0:T(8,128)}), f32[8,16,16,128]{3,2,1,0:T(8,128)S(1)}, u32[]{:S(2)}, u32[]{:S(2)}) async-start(f32[8,16,16,128]{3,2,1,0:T(8,128)} %get-tuple-element.82), calls=%async_computation.7 | async-start | bytes 2097152 | tf_op jit(solution)/shard_map/all_to_all | solution.py:764
